TPU v7x, 32 devices: a whole 2x2x4 slice. The times are simulated.
32 devices in a mesh: tm: 8 (over z, core), expert: 4 (over y, x).
Axes of the slice: x: 2, y: 2, z: 4, core: 2. Of those that a mesh axis runs over, the one named last changes fastest.
Arguments:
- frames: bfloat16 [2, 2048, 1536], P(None, ('tm', 'expert')), may hold values from -6 to 6
- expert_out: bfloat16 [2, 8, 4, 32, 8, 1536], P(None, 'tm', None, 'expert'), may hold values from -6 to 6
- routes: int32 [2, 2048, 2], P(None, ('tm', 'expert')), may hold values from 0 to 31, all different within a row; in each aligned block of 64 rows (0 to 63, 64 to 127, ..., all dimensions but the last counted through in order) at most 8 rows name the same one
- order: int32 [2, 32, 64], P(None, ('tm', 'expert')), may hold values from 0 to 63, each once within a row
- probs: float32 [2, 2048, 2], P(None, ('tm', 'expert')), may hold values from 0.05 to 1
- lengths: int32 [2, 8], replicated, may hold values from 1 to 1024, 2048 in all within a row
- gain: float32 [1536], replicated, may hold values from 0.1 to 1.9
- kernel: float32 [31, 1536], replicated, may hold values from -1 to 1
- grad_out: bfloat16 [2, 2048, 1536], P(None, ('tm', 'expert')), may hold values from -6 to 6
Outputs:
- grad_x: bfloat16 [2, 2048, 1536], P(None, ('tm', 'expert'))
- grad_expert: bfloat16 [2, 8, 4, 32, 8, 1536], P(None, 'tm', None, 'expert')
- grad_probs: float32 [2, 2048, 2], P(None, ('tm', 'expert'))
- grad_kernel: float32 [31, 1536], P(None, 'expert')
- grad_gain: float32 [1536], P('expert')
Inputs may be any that keep to these rules, and one draw needn't show every extreme that they name: `routes`: the two experts of a frame differ; among the 64 frames of one time block of one micro-batch no expert is named more than 8 times, a bound that some block reaches. `order`: each time block's row holds every number of 0 .. 63 once. Each micro-batch's lengths sum to 2048; the largest is exactly 1024.
All inputs are finite; a program needn't handle non-finite values.
Results may differ from a plain program's by a relative error of at most 0.0056.
Values may be sent and summed in bfloat16 or wider, within the bound.
No kernel may reach another device: no remote copies, remote signals or barrier semaphores. Data moves between devices by JAX's collectives and lax.ppermute only.
A program may use at most 64 MiB of HBM per device.

v0:
```python
import math

import jax
import jax.numpy as jnp
from jax import lax
from jax.sharding import PartitionSpec as P

EXPERTS = 32
KW = 31
HALF = 15
CAP = 8


def padded_2(cells, sides, width):
    for axis, dim in sides:
        count = lax.axis_size(axis)
        ends = count - 1
        head = lax.slice_in_dim(cells, 0, width, axis=dim)
        tail = lax.slice_in_dim(cells, cells.shape[dim] - width, cells.shape[dim], axis=dim)
        cells = jnp.concatenate(
            [
                lax.ppermute(tail, axis, [(i, (i + 1) % count) for i in range(ends)]),
                cells,
                lax.ppermute(head, axis, [((i + 1) % count, i) for i in range(ends)]),
            ],
            axis=dim,
        )
    return cells


def slot_table(route_rows, order_row):
    row_count = route_rows.shape[0]
    sort_keys = (order_row[:, None] * 2 + jnp.arange(2, dtype=jnp.int32)[None, :]).reshape(-1)
    owners = route_rows.reshape(-1)
    before = (owners[:, None] == owners[None, :]) & (sort_keys[None, :] < sort_keys[:, None])
    return jnp.sum(before.astype(jnp.int32), axis=1).reshape(row_count, 2)


def padded_segments(first_frame, row_count, frame_total, lengths_row):
    positions = first_frame - HALF + jnp.arange(row_count + 2 * HALF, dtype=jnp.int32)
    utt_ends = jnp.cumsum(lengths_row)
    segments = jnp.sum((positions[:, None] >= utt_ends[None, :]).astype(jnp.int32), axis=1)
    inside = (positions >= 0) & (positions < frame_total)
    return jnp.where(inside, segments, -1)


def neighbour_masks(seg_padded, row_count):
    centre = seg_padded[HALF : HALF + row_count]
    return [
        (seg_padded[offset : offset + row_count] == centre).astype(jnp.float32)[:, None]
        for offset in range(KW)
    ]


def conv_forward(padded, kernel_part, masks, row_count):
    running = jnp.zeros((row_count, padded.shape[1]), jnp.float32)
    for offset in range(KW):
        running = running + kernel_part[offset][None, :] * (
            padded[offset : offset + row_count].astype(jnp.float32) * masks[offset]
        )
    return running


def swish_slope(values):
    sigmoid_v = jax.nn.sigmoid(values)
    return sigmoid_v * (1.0 + values * (1.0 - sigmoid_v))


def conv_backward(padded, grad_padded, grad_mid, kernel_part, masks, row_count):
    running = jnp.zeros((row_count, padded.shape[1]), jnp.float32)
    grad_float = grad_mid.astype(jnp.float32)
    kernel_rows = []
    for offset in range(KW):
        running = running + kernel_part[KW - 1 - offset][None, :] * (
            grad_padded[offset : offset + row_count].astype(jnp.float32) * masks[offset]
        )
        kernel_rows.append(
            jnp.sum(
                padded[offset : offset + row_count].astype(jnp.float32)
                * masks[offset]
                * grad_float,
                axis=0,
            )
        )
    return (running.astype(jnp.bfloat16), jnp.stack(kernel_rows))


def local(frames, expert_out, routes, order, probs, lengths, gain, kernel, grad_out):
    micro_count = frames.shape[0]
    row_count = frames.shape[1]
    width = frames.shape[2]
    expert_count = lax.axis_size("expert")
    frame_total = row_count * lax.axis_size("tm") * expert_count
    scale_norm = 1.0 / math.sqrt(micro_count * frame_total)
    kernel_sum = jnp.zeros((KW, width), jnp.float32)
    gain_sum = jnp.zeros((width,), jnp.float32)
    grad_x_list = []
    grad_expert_list = []
    grad_probs_list = []
    for micro in range(micro_count):
        received = lax.all_to_all(
            expert_out[micro], "expert", split_axis=1, concat_axis=2, tiled=True
        )
        table_rows = received.reshape(EXPERTS * CAP, width)
        route_rows = routes[micro]
        slots = slot_table(route_rows, order[micro, 0])
        flat_index = (route_rows * CAP + slots).reshape(-1)
        picked = table_rows[flat_index].reshape(row_count, 2, width)
        weights = probs[micro]
        mixed = (
            frames[micro].astype(jnp.float32)
            + weights[:, 0:1] * picked[:, 0].astype(jnp.float32)
            + weights[:, 1:2] * picked[:, 1].astype(jnp.float32)
        )
        centre_mean = jnp.mean(mixed, axis=1, keepdims=True)
        centred = mixed - centre_mean
        rstd = lax.rsqrt(jnp.mean(centred * centred, axis=1, keepdims=True) + 1e-05)
        nhat = centred * rstd
        conv_in = (nhat * gain[None, :]).astype(jnp.bfloat16)
        seg_padded = padded_segments(
            lax.axis_index(("tm", "expert")) * row_count, row_count, frame_total, lengths[micro]
        )
        masks = neighbour_masks(seg_padded, row_count)
        padded = padded_2(conv_in, ((("tm", "expert"), 0),), HALF)
        conv_out = conv_forward(padded, kernel, masks, row_count)
        grad_conv = (grad_out[micro].astype(jnp.float32) * swish_slope(conv_out)).astype(
            jnp.bfloat16
        )
        grad_padded = padded_2(grad_conv, ((("tm", "expert"), 0),), HALF)
        grad_in, kernel_terms = conv_backward(
            padded, grad_padded, grad_conv, kernel, masks, row_count
        )
        kernel_sum = kernel_sum + kernel_terms
        grad_in_f = grad_in.astype(jnp.float32)
        gain_sum = gain_sum + jnp.sum(grad_in_f * nhat, axis=0)
        d_norm = grad_in_f * gain[None, :]
        dmixed = grad_out[micro].astype(jnp.float32) + rstd * (
            d_norm
            - jnp.mean(d_norm, axis=1, keepdims=True)
            - nhat * jnp.mean(d_norm * nhat, axis=1, keepdims=True)
        )
        grad_x_list.append(dmixed.astype(jnp.bfloat16))
        grad_probs_list.append(jnp.sum(dmixed[:, None, :] * picked.astype(jnp.float32), axis=2))
        values = (
            (weights[:, :, None] * dmixed[:, None, :])
            .astype(jnp.bfloat16)
            .reshape(2 * row_count, width)
        )
        outgoing = jnp.zeros((EXPERTS * CAP, width), jnp.bfloat16).at[flat_index].set(values)
        sent_back = lax.all_to_all(
            outgoing.reshape(1, 1, EXPERTS, CAP, width),
            "expert",
            split_axis=2,
            concat_axis=1,
            tiled=True,
        )
        grad_expert_list.append(sent_back)
    gain_row = gain_sum[None, :]
    kernel_share, gain_share = (
        lax.psum_scatter(kernel_sum, "expert", scatter_dimension=1, tiled=True),
        lax.psum_scatter(gain_row, "expert", scatter_dimension=1, tiled=True),
    )
    kernel_total, gain_total = lax.psum((kernel_share, gain_share), "tm")
    return (
        jnp.stack(grad_x_list),
        jnp.stack(grad_expert_list),
        jnp.stack(grad_probs_list),
        kernel_total * scale_norm,
        gain_total.reshape(-1) * scale_norm,
    )


def solution(mesh):
    placed = (
        P(None, ("tm", "expert"), None),
        P(None, "tm", None, "expert", None, None),
        P(None, ("tm", "expert"), None),
        P(None, ("tm", "expert"), None),
        P(None, ("tm", "expert"), None),
        P(),
        P(),
        P(),
        P(None, ("tm", "expert"), None),
    )
    return jax.shard_map(
        local,
        mesh=mesh,
        in_specs=placed,
        out_specs=(
            P(None, ("tm", "expert"), None),
            P(None, "tm", None, "expert", None, None),
            P(None, ("tm", "expert"), None),
            P(None, "expert"),
            P("expert"),
        ),
        check_vma=False,
    )
```

profile of v0, /device:TPU:0, one launch (start us, length us, event | category | flops | bytes accessed | tf_op | source)
XLA Modules:
  0.0 199.8 jit_solution(35444437039401121)
XLA Ops:
  7.2 2.6 %slice_bitcast_fusion.1 = (bf16[1,4,8,8,1536]{4,3,2,0,1:T(8,128)(2,1)}, bf16[1,4,8,8,1536]{4,3,2,0,1:T(8,128)(2,1)}) fusion(bf16[2,1,4,8,8,1536]{5,4,3,2,1,0:T(8,128)(2,1)} %param.10), kind=kLoop, calls=%fused_computation.187 | loop fusion | bytes 3145728 | tf_op jit(solution)/shard_map/squeeze | solution.py:102
  9.8 5.3 %all-to-all-start = ((bf16[1,4,8,8,1536]{4,3,2,0,1:T(8,128)(2,1)}), bf16[1,4,8,8,1536]{4,3,2,0,1:T(8,128)(2,1)S(1)}, u32[]{:S(2)}, u32[]{:S(2)}) async-start(bf16[1,4,8,8,1536]{4,3,2,0,1:T(8,128)(2,1)} %get-tuple-element.120), calls=%async_computation | async-start | bytes 1572864 | tf_op jit(solution)/shard_map/all_to_all | solution.py:101
  19.9 6.0 %all-to-all-done = bf16[1,4,8,8,1536]{4,3,2,0,1:T(8,128)(2,1)S(1)} async-done(((bf16[1,4,8,8,1536]{4,3,2,0,1:T(8,128)(2,1)}), bf16[1,4,8,8,1536]{4,3,2,0,1:T(8,128)(2,1)S(1)}, u32[]{:S(2)}, u32[]{:S(2)}) %all-to-all-start) | async-done | bytes 786464 | tf_op jit(solution)/shard_map/all_to_all | solution.py:101
  25.9 3.5 %all-to-all-start.1 = ((bf16[1,4,8,8,1536]{4,3,2,0,1:T(8,128)(2,1)}), bf16[1,4,8,8,1536]{4,3,2,0,1:T(8,128)(2,1)S(1)}, u32[]{:S(2)}, u32[]{:S(2)}) async-start(bf16[1,4,8,8,1536]{4,3,2,0,1:T(8,128)(2,1)} %get-tuple-element.121), calls=%async_computation.1 | async-start | bytes 1572864 | tf_op jit(solution)/shard_map/all_to_all | solution.py:101
  31.2 8.5 %all-to-all-done.1 = bf16[1,4,8,8,1536]{4,3,2,0,1:T(8,128)(2,1)S(1)} async-done(((bf16[1,4,8,8,1536]{4,3,2,0,1:T(8,128)(2,1)}), bf16[1,4,8,8,1536]{4,3,2,0,1:T(8,128)(2,1)S(1)}, u32[]{:S(2)}, u32[]{:S(2)}) %all-to-all-start.1) | async-done | bytes 786464 | tf_op jit(solution)/shard_map/all_to_all | solution.py:101
  43.0 3.3 %collective-permute-start.4 = (bf16[15,1536]{1,0:T(8,128)(2,1)S(1)}, bf16[15,1536]{1,0:T(8,128)(2,1)S(1)}, u32[]{:S(2)}, u32[]{:S(2)}) collective-permute-start(bf16[15,1536]{1,0:T(8,128)(2,1)S(1)} %get-tuple-element.136), channel_id=1, source_target_pairs={{0,1},{1,2},{2,3},{3,4},{4,5},{5,6},{6,7},{7,8},{8,9},{9,10},{10,1... | collective-permute-start | bytes 138248 | tf_op jit(solution)/shard_map/ppermute | solution.py:22
  46.3 1.3 collective-permute-start.5
  47.6 4.5 %collective-permute-start = (bf16[15,1536]{1,0:T(8,128)(2,1)S(1)}, bf16[15,1536]{1,0:T(8,128)(2,1)S(1)}, u32[]{:S(2)}, u32[]{:S(2)}) collective-permute-start(bf16[15,1536]{1,0:T(8,128)(2,1)S(1)} %get-tuple-element.132), channel_id=1, source_target_pairs={{0,1},{1,2},{2,3},{3,4},{4,5},{5,6},{6,7},{7,8},{8,9},{9,10},{10,1... | collective-permute-start | bytes 138248 | tf_op jit(solution)/shard_map/ppermute | solution.py:22
  52.2 1.3 collective-permute-start.1
  53.6 5.7 %fusion.142 = (f32[1536]{0:T(1024)}, f32[1536]{0:T(1024)}, f32[1536]{0:T(1024)}, f32[1536]{0:T(1024)}, f32[1536]{0:T(1024)}, /*index=5*/f32[1536]{0:T(1024)}, bf16[64,1536]{1,0:T(8,128)(2,1)S(1)}) fusion(f32[64]{0:T(128)S(1)} %get-tuple-element.187, bf16[15,1536]{1,0:T(8,128)(2,1)S(1)} %collective-permute-done.5, ...), kind=kLoop, calls=%fused_computation.340 | loop fusion | flops 26041344 | bytes 916992 | tf_op jit(solution)/shard_map/reduce_sum | solution.py:78
  59.3 4.9 %collective-permute-start.6 = (bf16[15,1536]{1,0:T(8,128)(2,1)S(1)}, bf16[15,1536]{1,0:T(8,128)(2,1)S(1)}, u32[]{:S(2)}, u32[]{:S(2)}) collective-permute-start(bf16[15,1536]{1,0:T(8,128)(2,1)S(1)} %get-tuple-element.134), channel_id=1, source_target_pairs={{0,1},{1,2},{2,3},{3,4},{4,5},{5,6},{6,7},{7,8},{8,9},{9,10},{10,1... | collective-permute-start | bytes 138248 | tf_op jit(solution)/shard_map/ppermute | solution.py:22
  64.2 1.3 collective-permute-start.7
  65.6 5.7 %fusion.95 = (f32[1536]{0:T(1024)}, f32[1536]{0:T(1024)}, f32[1536]{0:T(1024)}, f32[1536]{0:T(1024)}, f32[1536]{0:T(1024)}, /*index=5*/f32[1536]{0:T(1024)S(1)}, bf16[64,1536]{1,0:T(8,128)(2,1)S(1)}) fusion(f32[64]{0:T(128)S(1)} %get-tuple-element.157, bf16[15,1536]{1,0:T(8,128)(2,1)S(1)} %collective-permute-done.1, ...), kind=kLoop, calls=%fused_computation.293 | loop fusion | flops 26041344 | bytes 916992 | tf_op jit(solution)/shard_map/reduce_sum | solution.py:78
  71.3 5.4 %collective-permute-start.2 = (bf16[15,1536]{1,0:T(8,128)(2,1)S(1)}, bf16[15,1536]{1,0:T(8,128)(2,1)S(1)}, u32[]{:S(2)}, u32[]{:S(2)}) collective-permute-start(bf16[15,1536]{1,0:T(8,128)(2,1)S(1)} %get-tuple-element.130), channel_id=1, source_target_pairs={{0,1},{1,2},{2,3},{3,4},{4,5},{5,6},{6,7},{7,8},{8,9},{9,10},{10,1... | collective-permute-start | bytes 138248 | tf_op jit(solution)/shard_map/ppermute | solution.py:22
  76.8 1.5 collective-permute-start.3
  79.2 1.3 fusion.143
  80.5 1.3 fusion.126
  81.9 1.3 fusion.127
  84.2 1.3 fusion.96
  85.6 1.3 fusion.79
  87.0 1.3 fusion.80
  89.3 2.7 %fusion.45 = (f32[1536]{0:T(1024)S(1)}, f32[64]{0:T(128)S(1)}, f32[64]{0:T(128)S(1)}, bf16[64,1536]{1,0:T(8,128)(2,1)S(1)}) fusion(f32[64,1536]{1,0:T(8,128)S(1)} %get-tuple-element.125, f32[64]{0:T(128)S(1)} %add_rsqrt_fusion, f32[64]{0:T(128)S(1)} %broadcast_multiply_fusion.5, f32[1536]{0:T(1024)S(1)} %copy-done.7, f32[64]{0:T(128)S(1)} %get-tuple-element.215, ...), kind=kLoop, calls=%fused_computation.243 | loop fusion | flops 21821824 | bytes 1090048 | tf_op jit(solution)/shard_map/reduce_sum | solution.py:135
  93.5 2.7 %fusion.25 = (f32[1536]{0:T(1024)S(1)}, f32[64]{0:T(128)S(1)}, f32[64]{0:T(128)S(1)}, bf16[64,1536]{1,0:T(8,128)(2,1)S(1)}) fusion(f32[64,1536]{1,0:T(8,128)S(1)} %get-tuple-element.114, f32[64]{0:T(128)S(1)} %add_rsqrt_fusion.1, f32[64]{0:T(128)S(1)} %broadcast_multiply_fusion.8, f32[1536]{0:T(1024)S(1)} %copy-done.7, f32[64]{0:T(128)S(1)} %copy-done.52, ...), kind=kLoop, calls=%fused_computation.223 | loop fusion | flops 21821824 | bytes 1090048 | tf_op jit(solution)/shard_map/reduce_sum | solution.py:135
  97.2 1.1 reshape_bitcast_fusion
  98.4 1.8 convert_bitcast_fusion.1
  101.4 2.4 %scatter_custom_fusion = bf16[256,1536]{1,0:T(8,128)(2,1)} fusion(s32[128]{0:T(128)} %copy-done.124, f32[128,1536]{1,0:T(8,128)S(1)} %mul.2849, f32[128]{0:T(128)S(1)} %copy-done.118, bf16[]{:T(256)} %constant.57.clone.1), kind=kCustom, calls=%fused_computation.246 | custom fusion | flops 393216 | bytes 1573888 | tf_op jit(solution)/shard_map/scatter | solution.py:149
  104.0 6.4 %all-to-all-start.2 = ((bf16[1,1,32,8,1536]{4,3,1,0,2:T(8,128)(2,1)}), bf16[1,1,32,8,1536]{4,3,1,0,2:T(8,128)(2,1)S(1)}, u32[]{:S(2)}, u32[]{:S(2)}) async-start(bf16[1,1,32,8,1536]{4,3,1,0,2:T(8,128)(2,1)} %bitcast.34), calls=%async_computation.2 | async-start | bytes 1572864 | tf_op jit(solution)/shard_map/all_to_all | solution.py:150
  129.0 2.5 %scatter_custom_fusion.1 = bf16[256,1536]{1,0:T(8,128)(2,1)} fusion(s32[128]{0:T(128)} %copy-done.123, f32[128,1536]{1,0:T(8,128)S(1)} %mul.2854, f32[128]{0:T(128)S(1)} %copy-done.117, bf16[]{:T(256)} %constant.57.clone.1), kind=kCustom, calls=%fused_computation.247 | custom fusion | flops 393216 | bytes 1573888 | tf_op jit(solution)/shard_map/scatter | solution.py:149
  132.1 4.2 %all-to-all-start.3 = ((bf16[1,1,32,8,1536]{4,3,1,0,2:T(8,128)(2,1)}), bf16[1,1,32,8,1536]{4,3,1,0,2:T(8,128)(2,1)S(1)}, u32[]{:S(2)}, u32[]{:S(2)}) async-start(bf16[1,1,32,8,1536]{4,3,1,0,2:T(8,128)(2,1)} %bitcast.36), calls=%async_computation.3 | async-start | bytes 1572864 | tf_op jit(solution)/shard_map/all_to_all | solution.py:150
  138.1 23.3 %reduce-scatter.5.cloned.1.call-done = f32[31,384]{1,0:T(8,128)} async-done(((f32[31,1536]{1,0:T(8,128)}), f32[31,384]{1,0:T(8,128)}) %reduce-scatter.5.cloned.1.call-update) | async-done | bytes 47632 | tf_op jit(solution)/shard_map/reduce_scatter | solution.py:160
  161.4 29.1 %all-reduce = (f32[31,384]{1,0:T(8,128)S(1)}, f32[1,384]{1,0:T(1,128)S(1)}) all-reduce(f32[31,384]{1,0:T(8,128)} %reduce-scatter.5.cloned.1.call-done, f32[1,384]{1,0:T(1,128)S(1)} %copy.59), channel_id=1, replica_groups=mesh['tm'=8,'expert'=4] {'tm'}, use_global_device_ids=true, to_apply=%region_81.82 | all-reduce | flops 12288 | bytes 98304 | tf_op jit(solution)/shard_map/psum | solution.py:163
  191.7 1.3 pad_maximum_fusion
  (411 shorter events, 37.2 us)
Async XLA Ops:
  9.8 16.1 %all-to-all-start = ((bf16[1,4,8,8,1536]{4,3,2,0,1:T(8,128)(2,1)}), bf16[1,4,8,8,1536]{4,3,2,0,1:T(8,128)(2,1)S(1)}, u32[]{:S(2)}, u32[]{:S(2)}) async-start(bf16[1,4,8,8,1536]{4,3,2,0,1:T(8,128)(2,1)} %get-tuple-element.120), calls=%async_computation | async-start | bytes 1572864 | tf_op jit(solution)/shard_map/all_to_all | solution.py:101
  15.9 68.2 %copy-start.51 = (f32[64]{0:T(128)}, f32[64]{0:T(128)S(1)}, u32[]{:S(2)}) copy-start(f32[64]{0:T(128)S(1)} %get-tuple-element.185) | copy-start | bytes 772
  15.9 71.0 %copy-start.49 = (f32[64]{0:T(128)}, f32[64]{0:T(128)S(1)}, u32[]{:S(2)}) copy-start(f32[64]{0:T(128)S(1)} %get-tuple-element.184) | copy-start | bytes 772
  15.9 77.2 %copy-start.47 = (f32[64]{0:T(128)}, f32[64]{0:T(128)S(1)}, u32[]{:S(2)}) copy-start(f32[64]{0:T(128)S(1)} %get-tuple-element.183) | copy-start | bytes 772
  19.7 60.8 %copy-start.87 = (f32[64]{0:T(128)}, f32[64]{0:T(128)S(1)}, u32[]{:S(2)}) copy-start(f32[64]{0:T(128)S(1)} %get-tuple-element.186) | copy-start | bytes 772
  19.8 65.7 %copy-start.55 = (f32[64]{0:T(128)}, f32[64]{0:T(128)S(1)}, u32[]{:S(2)}) copy-start(f32[64]{0:T(128)S(1)} %get-tuple-element.175) | copy-start | bytes 772
  19.8 65.7 %copy-start.57 = (f32[64]{0:T(128)}, f32[64]{0:T(128)S(1)}, u32[]{:S(2)}) copy-start(f32[64]{0:T(128)S(1)} %get-tuple-element.176) | copy-start | bytes 772
  19.8 65.7 %copy-start.59 = (f32[64]{0:T(128)}, f32[64]{0:T(128)S(1)}, u32[]{:S(2)}) copy-start(f32[64]{0:T(128)S(1)} %get-tuple-element.177) | copy-start | bytes 772
  19.8 65.7 %copy-start.61 = (f32[64]{0:T(128)}, f32[64]{0:T(128)S(1)}, u32[]{:S(2)}) copy-start(f32[64]{0:T(128)S(1)} %get-tuple-element.178) | copy-start | bytes 772
  19.9 67.1 %copy-start.63 = (f32[64]{0:T(128)}, f32[64]{0:T(128)S(1)}, u32[]{:S(2)}) copy-start(f32[64]{0:T(128)S(1)} %get-tuple-element.179) | copy-start | bytes 772
  19.9 67.1 %copy-start.65 = (f32[64]{0:T(128)}, f32[64]{0:T(128)S(1)}, u32[]{:S(2)}) copy-start(f32[64]{0:T(128)S(1)} %get-tuple-element.180) | copy-start | bytes 772
  19.9 67.1 %copy-start.67 = (f32[64]{0:T(128)}, f32[64]{0:T(128)S(1)}, u32[]{:S(2)}) copy-start(f32[64]{0:T(128)S(1)} %get-tuple-element.181) | copy-start | bytes 772
  19.9 67.1 %copy-start.69 = (f32[64]{0:T(128)}, f32[64]{0:T(128)S(1)}, u32[]{:S(2)}) copy-start(f32[64]{0:T(128)S(1)} %get-tuple-element.182) | copy-start | bytes 772
  19.9 73.3 %copy-start.48 = (f32[64]{0:T(128)}, f32[64]{0:T(128)S(1)}, u32[]{:S(2)}) copy-start(f32[64]{0:T(128)S(1)} %get-tuple-element.174) | copy-start | bytes 772
  25.9 13.8 %all-to-all-start.1 = ((bf16[1,4,8,8,1536]{4,3,2,0,1:T(8,128)(2,1)}), bf16[1,4,8,8,1536]{4,3,2,0,1:T(8,128)(2,1)S(1)}, u32[]{:S(2)}, u32[]{:S(2)}) async-start(bf16[1,4,8,8,1536]{4,3,2,0,1:T(8,128)(2,1)} %get-tuple-element.121), calls=%async_computation.1 | async-start | bytes 1572864 | tf_op jit(solution)/shard_map/all_to_all | solution.py:101
  29.4 107.6 %reduce-scatter.7.cloned.1.call-start = ((), (), s32[]{:S(2)}) async-start(), calls=%async_computation.7 | async-start | bytes 983040
  29.9 54.2 %copy-start.71 = (f32[64]{0:T(128)}, f32[64]{0:T(128)S(1)}, u32[]{:S(2)}) copy-start(f32[64]{0:T(128)S(1)} %get-tuple-element.167) | copy-start | bytes 772
  29.9 54.2 %copy-start.73 = (f32[64]{0:T(128)}, f32[64]{0:T(128)S(1)}, u32[]{:S(2)}) copy-start(f32[64]{0:T(128)S(1)} %get-tuple-element.168) | copy-start | bytes 772
  30.0 55.6 %copy-start.83 = (f32[64]{0:T(128)}, f32[64]{0:T(128)S(1)}, u32[]{:S(2)}) copy-start(f32[64]{0:T(128)S(1)} %get-tuple-element.173) | copy-start | bytes 772
  30.0 57.0 %copy-start.81 = (f32[64]{0:T(128)}, f32[64]{0:T(128)S(1)}, u32[]{:S(2)}) copy-start(f32[64]{0:T(128)S(1)} %get-tuple-element.172) | copy-start | bytes 772
  30.1 55.4 %copy-start.85 = (f32[64]{0:T(128)}, f32[64]{0:T(128)S(1)}, u32[]{:S(2)}) copy-start(f32[64]{0:T(128)S(1)} %get-tuple-element.156) | copy-start | bytes 772
  43.0 10.5 %collective-permute-start.4 = (bf16[15,1536]{1,0:T(8,128)(2,1)S(1)}, bf16[15,1536]{1,0:T(8,128)(2,1)S(1)}, u32[]{:S(2)}, u32[]{:S(2)}) collective-permute-start(bf16[15,1536]{1,0:T(8,128)(2,1)S(1)} %get-tuple-element.136), channel_id=1, source_target_pairs={{0,1},{1,2},{2,3},{3,4},{4,5},{5,6},{6,7},{7,8},{8,9},{9,10},{10,1... | collective-permute-start | bytes 138248 | tf_op jit(solution)/shard_map/ppermute | solution.py:22
  46.3 7.2 %collective-permute-start.5 = (bf16[15,1536]{1,0:T(8,128)(2,1)S(1)}, bf16[15,1536]{1,0:T(8,128)(2,1)S(1)}, u32[]{:S(2)}, u32[]{:S(2)}) collective-permute-start(bf16[15,1536]{1,0:T(8,128)(2,1)S(1)} %get-tuple-element.137), channel_id=1, source_target_pairs={{1,0},{2,1},{3,2},{4,3},{5,4},{6,5},{7,6},{8,7},{9,8},{10,9},{11,1... | collective-permute-start | bytes 138248 | tf_op jit(solution)/shard_map/ppermute | solution.py:24
  47.6 17.9 %collective-permute-start = (bf16[15,1536]{1,0:T(8,128)(2,1)S(1)}, bf16[15,1536]{1,0:T(8,128)(2,1)S(1)}, u32[]{:S(2)}, u32[]{:S(2)}) collective-permute-start(bf16[15,1536]{1,0:T(8,128)(2,1)S(1)} %get-tuple-element.132), channel_id=1, source_target_pairs={{0,1},{1,2},{2,3},{3,4},{4,5},{5,6},{6,7},{7,8},{8,9},{9,10},{10,1... | collective-permute-start | bytes 138248 | tf_op jit(solution)/shard_map/ppermute | solution.py:22
  52.2 13.4 %collective-permute-start.1 = (bf16[15,1536]{1,0:T(8,128)(2,1)S(1)}, bf16[15,1536]{1,0:T(8,128)(2,1)S(1)}, u32[]{:S(2)}, u32[]{:S(2)}) collective-permute-start(bf16[15,1536]{1,0:T(8,128)(2,1)S(1)} %get-tuple-element.133), channel_id=1, source_target_pairs={{1,0},{2,1},{3,2},{4,3},{5,4},{6,5},{7,6},{8,7},{9,8},{10,9},{11,1... | collective-permute-start | bytes 138248 | tf_op jit(solution)/shard_map/ppermute | solution.py:24
  59.3 30.0 %collective-permute-start.6 = (bf16[15,1536]{1,0:T(8,128)(2,1)S(1)}, bf16[15,1536]{1,0:T(8,128)(2,1)S(1)}, u32[]{:S(2)}, u32[]{:S(2)}) collective-permute-start(bf16[15,1536]{1,0:T(8,128)(2,1)S(1)} %get-tuple-element.134), channel_id=1, source_target_pairs={{0,1},{1,2},{2,3},{3,4},{4,5},{5,6},{6,7},{7,8},{8,9},{9,10},{10,1... | collective-permute-start | bytes 138248 | tf_op jit(solution)/shard_map/ppermute | solution.py:22
  64.2 25.0 %collective-permute-start.7 = (bf16[15,1536]{1,0:T(8,128)(2,1)S(1)}, bf16[15,1536]{1,0:T(8,128)(2,1)S(1)}, u32[]{:S(2)}, u32[]{:S(2)}) collective-permute-start(bf16[15,1536]{1,0:T(8,128)(2,1)S(1)} %get-tuple-element.135), channel_id=1, source_target_pairs={{1,0},{2,1},{3,2},{4,3},{5,4},{6,5},{7,6},{8,7},{9,8},{10,9},{11,1... | collective-permute-start | bytes 138248 | tf_op jit(solution)/shard_map/ppermute | solution.py:24
  71.3 21.9 %collective-permute-start.2 = (bf16[15,1536]{1,0:T(8,128)(2,1)S(1)}, bf16[15,1536]{1,0:T(8,128)(2,1)S(1)}, u32[]{:S(2)}, u32[]{:S(2)}) collective-permute-start(bf16[15,1536]{1,0:T(8,128)(2,1)S(1)} %get-tuple-element.130), channel_id=1, source_target_pairs={{0,1},{1,2},{2,3},{3,4},{4,5},{5,6},{6,7},{7,8},{8,9},{9,10},{10,1... | collective-permute-start | bytes 138248 | tf_op jit(solution)/shard_map/ppermute | solution.py:22
  76.8 16.4 %collective-permute-start.3 = (bf16[15,1536]{1,0:T(8,128)(2,1)S(1)}, bf16[15,1536]{1,0:T(8,128)(2,1)S(1)}, u32[]{:S(2)}, u32[]{:S(2)}) collective-permute-start(bf16[15,1536]{1,0:T(8,128)(2,1)S(1)} %get-tuple-element.131), channel_id=1, source_target_pairs={{1,0},{2,1},{3,2},{4,3},{5,4},{6,5},{7,6},{8,7},{9,8},{10,9},{11,1... | collective-permute-start | bytes 138248 | tf_op jit(solution)/shard_map/ppermute | solution.py:24
  104.0 28.1 %all-to-all-start.2 = ((bf16[1,1,32,8,1536]{4,3,1,0,2:T(8,128)(2,1)}), bf16[1,1,32,8,1536]{4,3,1,0,2:T(8,128)(2,1)S(1)}, u32[]{:S(2)}, u32[]{:S(2)}) async-start(bf16[1,1,32,8,1536]{4,3,1,0,2:T(8,128)(2,1)} %bitcast.34), calls=%async_computation.2 | async-start | bytes 1572864 | tf_op jit(solution)/shard_map/all_to_all | solution.py:150
  110.4 50.9 %reduce-scatter.5.cloned.1.call-start = ((), (), s32[]{:S(2)}) async-start(), calls=%async_computation.6 | async-start | bytes 245760 | tf_op jit(solution)/shard_map/reduce_scatter | solution.py:160
  132.1 59.6 %all-to-all-start.3 = ((bf16[1,1,32,8,1536]{4,3,1,0,2:T(8,128)(2,1)}), bf16[1,1,32,8,1536]{4,3,1,0,2:T(8,128)(2,1)S(1)}, u32[]{:S(2)}, u32[]{:S(2)}) async-start(bf16[1,1,32,8,1536]{4,3,1,0,2:T(8,128)(2,1)} %bitcast.36), calls=%async_computation.3 | async-start | bytes 1572864 | tf_op jit(solution)/shard_map/all_to_all | solution.py:150
  (107 other events, 1905.2 us)
Sparse Core Ops, SparseCore 0:
  98.5 35.7 reduce-scatter.6
  137.0 24.3 reduce-scatter.4
where the time goes:
time: 202 us; the launch traced here: 200 us
  other arithmetic  45.2 us (22%)
  starting transfers between devices  43.1 us (21%)
  waiting for transfers between devices  37.9 us (19%)
  blocking collectives  29.1 us (14%)
  local copies, waits for them, and re-layouts  28.2 us (14%)
  between operations  16.4 us (8%)
    psum x1, blocking collectives, local(): kernel_total, gain_total = lax.psum((kernel_share, gain_share), 'tm')  29.1 us
    reduce_scatter x1, waiting for transfers between devices, local(): lax.psum_scatter(kernel_sum, 'expert', scatter_dimension=1, tiled=True)  23.3 us
    reduce_sum x12, other arithmetic, conv_backward(): jnp.sum(padded[offset:offset + row_count].astype(jnp.float32) * masks[off...  22.9 us
    ppermute x4, starting transfers between devices, padded_2(): lax.ppermute(tail, axis, [(i, (i + 1) % count) for i in range(ends)])  18.3 us
    all_to_all x2, waiting for transfers between devices, local(): lax.all_to_all(expert_out[micro], 'expert', split_axis=1, concat_axis=2,...  14.5 us
    another operation x64, local copies, waits for them, and re-layouts, conv_backward(): return (running.astype(jnp.bfloat16), jnp.stack(kernel_rows))  14.3 us
    all_to_all x2, starting transfers between devices, local(): lax.all_to_all(outgoing.reshape(1, 1, EXPERTS, CAP, width), 'expert', spl...  10.6 us
    all_to_all x2, starting transfers between devices, local(): lax.all_to_all(expert_out[micro], 'expert', split_axis=1, concat_axis=2,...  8.8 us
  transfers between devices with their start and end apart: 14, of which 3 were waited for; matrix products, arithmetic and copies ran while one was open for 30% of the time, Pallas kernels for 0%

commit v1 on v0

v1 whole, which is shorter than its diff:
```python
import functools
import math

import jax
import jax.numpy as jnp
from jax import lax
from jax.experimental import pallas as pl
from jax.experimental.pallas import tpu as pltpu
from jax.sharding import PartitionSpec as P

EXPERTS = 32
KW = 31
HALF = 15
CAP = 8
SIDE = 32
GSIDE = 16
CHUNK = 256
F32 = jnp.float32
BF16 = jnp.bfloat16
VMEM_LIMIT = 48 * 1024 * 1024


def slot_table(route_rows, order_row):
    row_count = route_rows.shape[0]
    sort_keys = (order_row[:, None] * 2 + jnp.arange(2, dtype=jnp.int32)[None, :]).reshape(-1)
    owners = route_rows.reshape(-1)
    before = (owners[:, None] == owners[None, :]) & (sort_keys[None, :] < sort_keys[:, None])
    return jnp.sum(before.astype(jnp.int32), axis=1).reshape(row_count, 2)


def combine_kernel(
    group_count,
    place_ref,
    own_ref,
    *rest,
):
    table_refs = rest[: group_count - 1]
    frames_ref, flat_ref, probs_ref, gain_ref = rest[group_count - 1 : group_count + 3]
    conv_in_ref, send_ref, nhat_ref, rstd_ref, picked_ref = rest[group_count + 3 :]
    rows = frames_ref.shape[1]
    block = own_ref.shape[1] * own_ref.shape[2]
    width = frames_ref.shape[2]
    flat = flat_ref[0]
    probs = probs_ref[0]
    tables = [own_ref[...].reshape(block, width)] + [r[0] for r in table_refs]
    table = jnp.concatenate(tables, axis=0) if group_count > 1 else tables[0]
    lane = lax.broadcasted_iota(jnp.int32, (rows, group_count * block), 1)
    mixed = frames_ref[0].astype(F32)
    for k in range(2):
        hot = jnp.where(lane == flat[:, k : k + 1], 1.0, 0.0).astype(BF16)
        row = jnp.dot(hot, table, preferred_element_type=F32)
        picked_ref[k] = row.astype(BF16)
        mixed = mixed + probs[:, k : k + 1] * row
    mean = jnp.mean(mixed, axis=1, keepdims=True)
    centred = mixed - mean
    rstd = lax.rsqrt(jnp.mean(centred * centred, axis=1, keepdims=True) + 1e-05)
    nhat = centred * rstd
    nhat_ref[...] = nhat
    rstd_ref[...] = jnp.broadcast_to(rstd, rstd_ref.shape)
    conv_in = (nhat * gain_ref[...]).astype(BF16)
    conv_in_ref[...] = conv_in
    odd = place_ref[1]

    @pl.when(odd == 0)
    def _():
        send_ref[0] = conv_in[rows - SIDE :]
        send_ref[1] = conv_in[:SIDE]

    @pl.when(odd == 1)
    def _():
        send_ref[0] = conv_in[:SIDE]
        send_ref[1] = conv_in[rows - SIDE :]


def swish_slope(values):
    sigmoid_v = jax.nn.sigmoid(values)
    return sigmoid_v * (1.0 + values * (1.0 - sigmoid_v))


def conv_kernel(
    group_count,
    first,
    micro,
    frame_total,
    place_ref,
    lengths_ref,
    conv_in_ref,
    near_ref,
    far_ref,
    grad_out_ref,
    gnear_ref,
    gfar_ref,
    nhat_ref,
    rstd_ref,
    picked_ref,
    flat_row_ref,
    probs_ref,
    gain_ref,
    kernel_ref,
    *rest,
):
    if first:
        grad_x_ref, grad_probs_ref, terms_ref = rest[:3]
        rest = rest[3:]
        last_terms = None
    else:
        last_terms, _, _, grad_x_ref, grad_probs_ref, terms_ref = rest[:6]
        rest = rest[6:]
    out_refs = rest[:group_count]
    window, gout, shifts, gwin, gin, kacc = rest[group_count:]
    rows, width = conv_in_ref.shape
    mid = rows + 2 * GSIDE
    full = rows + 2 * SIDE
    odd = place_ref[1]
    chunks = width // CHUNK

    window[SIDE : SIDE + rows, :] = conv_in_ref[...]
    gout[GSIDE : GSIDE + rows, :] = grad_out_ref[0]

    @pl.when(odd == 0)
    def _():
        window[:SIDE, :] = far_ref[...]
        window[SIDE + rows :, :] = near_ref[...]
        gout[:GSIDE, :] = gfar_ref[0]
        gout[GSIDE + rows :, :] = gnear_ref[0]

    @pl.when(odd == 1)
    def _():
        window[:SIDE, :] = near_ref[...]
        window[SIDE + rows :, :] = far_ref[...]
        gout[:GSIDE, :] = gnear_ref[0]
        gout[GSIDE + rows :, :] = gfar_ref[0]

    gwin[: SIDE - GSIDE, :] = jnp.zeros((SIDE - GSIDE, CHUNK), BF16)
    gwin[SIDE - GSIDE + mid :, :] = jnp.zeros((SIDE - GSIDE, CHUNK), BF16)

    first_frame = place_ref[0]
    t_local = lax.broadcasted_iota(jnp.int32, (mid, full), 0)
    r_local = lax.broadcasted_iota(jnp.int32, (mid, full), 1)
    t_pos = first_frame - GSIDE + t_local
    r_pos = first_frame - SIDE + r_local

    def count(u, carry):
        end, t_seg, r_seg = carry
        end = end + lengths_ref[micro, u]
        return (
            end,
            t_seg + jnp.where(t_pos >= end, 1, 0),
            r_seg + jnp.where(r_pos >= end, 1, 0),
        )

    zero = jnp.zeros((mid, full), jnp.int32)
    _, t_seg, r_seg = lax.fori_loop(0, lengths_ref.shape[1], count, (0, zero, zero))
    same = (t_seg == r_seg) & (t_pos >= 0) & (t_pos < frame_total) & (r_pos >= 0) & (r_pos < frame_total)
    gap = jnp.where(same, r_local - t_local - (SIDE - GSIDE - HALF), -1)
    for i in range(KW):
        shifts[i * mid : (i + 1) * mid, :] = jnp.where(gap == i, 1.0, 0.0).astype(BF16)

    def chunk_step(q, carry):
        s1, s2 = carry
        cols = pl.ds(pl.multiple_of(q * CHUNK, CHUNK), CHUNK)
        taps = kernel_ref[:, cols]
        xw = window[:, cols]
        acc = jnp.zeros((mid, CHUNK), F32)
        for i in range(KW):
            v = jnp.dot(shifts[i * mid : (i + 1) * mid, :], xw, preferred_element_type=F32)
            acc = acc + taps[i : i + 1, :] * v
        g = (gout[:, cols].astype(F32) * swish_slope(acc)).astype(BF16)
        gwin[SIDE - GSIDE : SIDE - GSIDE + mid, :] = g
        gw = gwin[...]
        x = conv_in_ref[:, cols].astype(F32)
        acc = jnp.zeros((rows, CHUNK), F32)
        for j in range(KW):
            base = j * mid + GSIDE
            v = jnp.dot(shifts[base : base + rows, :], gw, preferred_element_type=F32)
            i = KW - 1 - j
            acc = acc + taps[i : i + 1, :] * v
            kacc[i : i + 1, cols] = jnp.sum(x * v, axis=0, keepdims=True)
        grad_in = acc.astype(BF16).astype(F32)
        nhat = nhat_ref[:, cols]
        kacc[KW : KW + 1, cols] = jnp.sum(grad_in * nhat, axis=0, keepdims=True)
        dn = grad_in * gain_ref[:, cols]
        gin[:, cols] = dn
        return (
            s1 + jnp.sum(dn, axis=1, keepdims=True),
            s2 + jnp.sum(dn * nhat, axis=1, keepdims=True),
        )

    none = jnp.zeros((rows, 1), F32)
    s1, s2 = lax.fori_loop(0, chunks, chunk_step, (none, none))
    m1 = s1 * (1.0 / width)
    m2 = s2 * (1.0 / width)
    rstd = rstd_ref[:, :1]
    probs = probs_ref[0]
    slots = out_refs[0].shape[0]
    total = slots * group_count
    spots = lax.broadcasted_iota(jnp.int32, (total, 2 * rows), 0)
    hot = jnp.where(spots == flat_row_ref[0], 1.0, 0.0).astype(BF16)

    def back_step(q, carry):
        p0, p1 = carry
        cols = pl.ds(pl.multiple_of(q * CHUNK, CHUNK), CHUNK)
        dmixed = grad_out_ref[0, :, cols].astype(F32) + rstd * (
            gin[:, cols] - m1 - nhat_ref[:, cols] * m2
        )
        grad_x_ref[0, :, cols] = dmixed.astype(BF16)
        values = jnp.concatenate(
            [(probs[:, 0:1] * dmixed).astype(BF16), (probs[:, 1:2] * dmixed).astype(BF16)], axis=0
        )
        placed = jnp.dot(hot, values, preferred_element_type=F32).astype(BF16)
        for e in range(group_count):
            out_refs[e][:, cols] = placed[e * slots : (e + 1) * slots]
        return (
            p0 + jnp.sum(dmixed * picked_ref[0, :, cols].astype(F32), axis=1, keepdims=True),
            p1 + jnp.sum(dmixed * picked_ref[1, :, cols].astype(F32), axis=1, keepdims=True),
        )

    p0, p1 = lax.fori_loop(0, chunks, back_step, (none, none))
    two = lax.broadcasted_iota(jnp.int32, (rows, 2), 1)
    grad_probs_ref[0] = jnp.where(two == 0, p0, p1)
    part = width // group_count
    for e in range(group_count):
        share = kacc[:, e * part : (e + 1) * part]
        if last_terms is not None:
            share = share + last_terms[e]
        terms_ref[e] = share


def whole(shape):
    return pl.BlockSpec(shape, lambda *_: (0,) * len(shape))


def of_micro(micro, shape):
    return pl.BlockSpec((1,) + shape[1:], lambda *_: (micro,) + (0,) * (len(shape) - 1))


def combine(micro, place, expert_out, tables, frames, flat, probs, gain):
    group_count = len(tables) + 1
    rows, width = frames.shape[1:]
    own = pl.BlockSpec(
        (None, None, 1) + expert_out.shape[3:],
        lambda _, place_ref: (micro, 0, place_ref[2], 0, 0, 0),
    )
    return pl.pallas_call(
        functools.partial(combine_kernel, group_count),
        grid_spec=pltpu.PrefetchScalarGridSpec(
            num_scalar_prefetch=1,
            grid=(1,),
            in_specs=[own]
            + [whole(t.shape) for t in tables]
            + [
                of_micro(micro, frames.shape),
                of_micro(micro, flat.shape),
                of_micro(micro, probs.shape),
                whole(gain.shape),
            ],
            out_specs=[
                whole((rows, width)),
                whole((2, SIDE, width)),
                whole((rows, width)),
                whole((rows, 128)),
                whole((2, rows, width)),
            ],
        ),
        out_shape=[
            jax.ShapeDtypeStruct((rows, width), BF16),
            jax.ShapeDtypeStruct((2, SIDE, width), BF16),
            jax.ShapeDtypeStruct((rows, width), F32),
            jax.ShapeDtypeStruct((rows, 128), F32),
            jax.ShapeDtypeStruct((2, rows, width), BF16),
        ],
        compiler_params=pltpu.CompilerParams(vmem_limit_bytes=VMEM_LIMIT),
        name="combine",
    )(place, expert_out, *tables, frames, flat, probs, gain)


def conv(micro, place, lengths, group_count, frame_total, conv_in, near, far, grad_out, gnear, gfar, nhat, rstd, picked, flat_row, probs, gain, kernel, earlier):
    rows, width = conv_in.shape
    micro_count = grad_out.shape[0]
    first = earlier is None
    slots = EXPERTS * CAP // group_count
    mid = rows + 2 * GSIDE
    full = rows + 2 * SIDE
    terms_shape = (group_count, KW + 1, width // group_count)
    in_specs = [
        whole(conv_in.shape),
        whole(near.shape),
        whole(far.shape),
        of_micro(micro, grad_out.shape),
        of_micro(micro, gnear.shape),
        of_micro(micro, gfar.shape),
        whole(nhat.shape),
        whole(rstd.shape),
        whole(picked.shape),
        of_micro(micro, flat_row.shape),
        of_micro(micro, probs.shape),
        whole(gain.shape),
        whole(kernel.shape),
    ]
    operands = [place, lengths, conv_in, near, far, grad_out, gnear, gfar, nhat, rstd, picked, flat_row, probs, gain, kernel]
    aliases = {}
    if not first:
        in_specs += [whole(terms_shape), pl.BlockSpec(memory_space=pl.ANY), pl.BlockSpec(memory_space=pl.ANY)]
        aliases = {len(operands) + 1: 0, len(operands) + 2: 1}
        operands += [earlier[2], earlier[0], earlier[1]]
    return pl.pallas_call(
        functools.partial(conv_kernel, group_count, first, micro, frame_total),
        grid_spec=pltpu.PrefetchScalarGridSpec(
            num_scalar_prefetch=2,
            grid=(1,),
            in_specs=in_specs,
            out_specs=[
                of_micro(micro, grad_out.shape),
                of_micro(micro, probs.shape),
                whole(terms_shape),
            ]
            + [whole((slots, width))] * group_count,
            scratch_shapes=[
                pltpu.VMEM((full, width), BF16),
                pltpu.VMEM((mid, width), BF16),
                pltpu.VMEM((KW * mid, full), BF16),
                pltpu.VMEM((full, CHUNK), BF16),
                pltpu.VMEM((rows, width), F32),
                pltpu.VMEM((KW + 1, width), F32),
            ],
        ),
        out_shape=[
            jax.ShapeDtypeStruct((micro_count, rows, width), BF16),
            jax.ShapeDtypeStruct(probs.shape, F32),
            jax.ShapeDtypeStruct(terms_shape, F32),
        ]
        + [jax.ShapeDtypeStruct((slots, width), BF16)] * group_count,
        input_output_aliases=aliases,
        compiler_params=pltpu.CompilerParams(vmem_limit_bytes=VMEM_LIMIT),
        name="conv",
    )(*operands)


def take(cells, index):
    return lax.dynamic_index_in_dim(cells, index, axis=0, keepdims=False)


def local(frames, expert_out, routes, order, probs, lengths, gain, kernel, grad_out):
    micro_count, rows, width = frames.shape
    groups = lax.axis_size("expert")
    tm = lax.axis_size("tm")
    both = ("tm", "expert")
    devices = groups * tm
    frame_total = rows * devices
    scale_norm = 1.0 / math.sqrt(micro_count * frame_total)
    me = lax.axis_index("expert")
    here = lax.axis_index(both)
    odd = lax.rem(here, 2)
    place = jnp.stack([here * rows, odd, me]).astype(jnp.int32)
    per = EXPERTS // groups
    block = per * CAP
    near_pairs = [(i, i ^ 1) for i in range(devices)]
    far_pairs = [(i, (i - 1) % devices if i % 2 == 0 else (i + 1) % devices) for i in range(devices)]

    def swap(cells, step):
        return lax.ppermute(cells, "expert", [(i, i ^ step) for i in range(groups)])

    tables = []
    for micro in range(micro_count):
        source = expert_out[micro, 0].reshape(groups, 1, block, width)
        tables.append([swap(take(source, me ^ step), step) for step in range(1, groups)])

    head, tail = grad_out[:, :GSIDE], grad_out[:, rows - GSIDE :]
    gnear = lax.ppermute(jnp.where(odd == 0, tail, head), both, near_pairs)
    gfar = lax.ppermute(jnp.where(odd == 0, head, tail), both, far_pairs)

    slots = jax.vmap(slot_table)(routes, order[:, 0])
    flat = ((routes // per) ^ me) * block + (routes % per) * CAP + slots
    flat_row = jnp.swapaxes(flat, 1, 2).reshape(micro_count, 1, 2 * rows)
    gain_row = gain[None, :]

    earlier = None
    returned = []
    for micro in range(micro_count):
        conv_in, sends, nhat, rstd, picked = combine(
            micro, place, expert_out, tables[micro], frames, flat, probs, gain_row
        )
        near = lax.ppermute(sends[0], both, near_pairs)
        far = lax.ppermute(sends[1], both, far_pairs)
        grad_x, grad_probs, terms, *outs = conv(
            micro, place, lengths, groups, frame_total, conv_in, near, far, grad_out, gnear, gfar,
            nhat, rstd, picked, flat_row, probs, gain_row, kernel, earlier,
        )
        earlier = (grad_x, grad_probs, terms)
        returned.append([outs[0]] + [swap(outs[step], step) for step in range(1, groups)])

    grad_expert = jnp.zeros((micro_count, groups, block, width), BF16)
    for micro in range(micro_count):
        for step in range(groups):
            grad_expert = lax.dynamic_update_slice(
                grad_expert, returned[micro][step][None, None], (micro, me ^ step, 0, 0)
            )
    grad_expert = grad_expert.reshape(micro_count, 1, groups, per, CAP, width)

    total = take(terms, me)
    for step in range(1, groups):
        total = total + swap(take(terms, me ^ step), step)
    step = 1
    while step < tm:
        total = total + lax.ppermute(total, "tm", [(i, i ^ step) for i in range(tm)])
        step *= 2
    total = total * scale_norm
    return grad_x, grad_expert, grad_probs, total[:KW], total[KW]


def solution(mesh):
    placed = (
        P(None, ("tm", "expert"), None),
        P(None, "tm", None, "expert", None, None),
        P(None, ("tm", "expert"), None),
        P(None, ("tm", "expert"), None),
        P(None, ("tm", "expert"), None),
        P(),
        P(),
        P(),
        P(None, ("tm", "expert"), None),
    )
    return jax.shard_map(
        local,
        mesh=mesh,
        in_specs=placed,
        out_specs=(
            P(None, ("tm", "expert"), None),
            P(None, "tm", None, "expert", None, None),
            P(None, ("tm", "expert"), None),
            P(None, "expert"),
            P("expert"),
        ),
        check_vma=False,
    )
```

time: 202 us -> 89.4 us (0.44)
  other arithmetic: 45.2 us -> 1.12 us
  waiting for transfers between devices: 37.9 us -> 8.58 us
  blocking collectives: 29.1 us -> 0 us
  Pallas kernels: 0 us -> 23.5 us
  between operations: 16.4 us -> 0.99 us
  local copies, waits for them, and re-layouts: 28.2 us -> 19.1 us
  starting transfers between devices: 43.1 us -> 35.8 us
    reduce_sum x20 -> x0, other arithmetic: 30.2 us -> none  [the longest x12 22.9 us: conv_backward(): jnp.sum(padded[offset:offset + row_count].astype(jnp.float32) * masks[off...]
    psum x1 -> x0, blocking collectives: 29.1 us -> none  [local(): kernel_total, gain_total = lax.psum((kernel_share, gain_share), 'tm')]
    pallas_call x0 -> x4, Pallas kernels: none -> 23.5 us  [the longest x2 21.1 us: conv(): pl.pallas_call(functools.partial(conv_kernel, group_count, first, micro,...]
    reduce_scatter x1 -> x0, waiting for transfers between devices: 23.3 us -> none  [local(): lax.psum_scatter(kernel_sum, 'expert', scatter_dimension=1, tiled=True)]
    all_to_all x4 -> x0, starting transfers between devices: 19.4 us -> none  [the longest x2 10.6 us: local(): lax.all_to_all(outgoing.reshape(1, 1, EXPERTS, CAP, width), 'expert', spl...]
    all_to_all x4 -> x0, waiting for transfers between devices: 14.5 us -> none  [the longest x2 14.5 us: local(): lax.all_to_all(expert_out[micro], 'expert', split_axis=1, concat_axis=2,...]
    ppermute x8 -> x24, starting transfers between devices: 23.6 us -> 35.8 us  [the longest x15 19.2 us: swap(): return lax.ppermute(cells, 'expert', [(i, i ^ step) for i in range(groups)])]
    another operation x65 -> x1, local copies, waits for them, and re-layouts: 14.3 us -> 2.44 us  [local(): source = expert_out[micro, 0].reshape(groups, 1, block, width)]
  transfers between devices with their start and end apart: 14 -> 24, of which waited for: 3 -> 10; matrix products, arithmetic and copies ran while one was open for 30% -> 13% of each run, Pallas kernels for 0% -> 15%
where the time goes in v1:
time: 89.4 us; the launch traced here: 89.2 us
  starting transfers between devices  35.8 us (40%)
  Pallas kernels  23.5 us (26%)
  local copies, waits for them, and re-layouts  19.1 us (21%)
  waiting for transfers between devices  8.58 us (10%)
  other arithmetic  1.12 us (1%)
  between operations  0.99 us (1%)
    pallas_call x2, Pallas kernels, conv(): pl.pallas_call(functools.partial(conv_kernel, group_count, first, micro,...  21.1 us
    ppermute x15, starting transfers between devices, swap(): return lax.ppermute(cells, 'expert', [(i, i ^ step) for i in range(groups)])  19.2 us
    ppermute x15, waiting for transfers between devices, swap(): return lax.ppermute(cells, 'expert', [(i, i ^ step) for i in range(groups)])  8.49 us
    unnamed x47, local copies, waits for them, and re-layouts  5.61 us
    dynamic_update_slice x8, local copies, waits for them, and re-layouts, local(): lax.dynamic_update_slice(grad_expert, returned[micro][step][None, None],...  5.52 us
    ppermute x2, starting transfers between devices, local(): far = lax.ppermute(sends[1], both, far_pairs)  4.66 us
    ppermute x3, starting transfers between devices, local(): lax.ppermute(total, 'tm', [(i, i ^ step) for i in range(tm)])  4.5 us
    ppermute x1, starting transfers between devices, local(): gfar = lax.ppermute(jnp.where(odd == 0, head, tail), both, far_pairs)  2.85 us
  transfers between devices with their start and end apart: 24, of which 10 were waited for; matrix products, arithmetic and copies ran while one was open for 13% of the time, Pallas kernels for 15%

profile of v1, /device:TPU:0, one launch (start us, length us, event | category | flops | bytes accessed | tf_op | source)
XLA Modules:
  0.0 89.2 jit_solution(1464139365256275649)
XLA Ops:
  0.7 2.4 %slice_bitcast_fusion = (bf16[4,1,64,1536]{3,2,1,0:T(8,128)(2,1)S(1)}, bf16[4,1,64,1536]{3,2,1,0:T(8,128)(2,1)}) fusion(bf16[2,1,4,8,8,1536]{5,4,3,2,1,0:T(8,128)(2,1)} %own_ref.3), kind=kLoop, calls=%fused_computation | loop fusion | bytes 3145728 | tf_op jit(solution)/shard_map/reshape;squeeze | solution.py:365
  3.2 0.8 dynamic-slice_bitcast_fusion
  4.0 2.9 %collective-permute-start.7 = (bf16[1,64,1536]{2,1,0:T(8,128)(2,1)}, bf16[1,64,1536]{2,1,0:T(8,128)(2,1)S(1)}, u32[]{:S(2)}, u32[]{:S(2)}) collective-permute-start(bf16[1,64,1536]{2,1,0:T(8,128)(2,1)} %get-tuple-element.72), channel_id=1, source_target_pairs={{0,1},{1,0},{2,3},{3,2},{4,5},{5,4},{6,7},{7,6},{8,9},{9,8},{10,11... | collective-permute-start | bytes 589832 | tf_op jit(solution)/shard_map/ppermute | solution.py:361
  6.9 1.5 %collective-permute-start.8 = (bf16[1,64,1536]{2,1,0:T(8,128)(2,1)}, bf16[1,64,1536]{2,1,0:T(8,128)(2,1)S(1)}, u32[]{:S(2)}, u32[]{:S(2)}) collective-permute-start(bf16[1,64,1536]{2,1,0:T(8,128)(2,1)} %get-tuple-element.71), channel_id=1, source_target_pairs={{0,2},{1,3},{2,0},{3,1},{4,6},{5,7},{6,4},{7,5},{8,10},{9,11},{10,... | collective-permute-start | bytes 589832 | tf_op jit(solution)/shard_map/ppermute | solution.py:361
  9.1 2.0 %collective-permute-start.5 = (bf16[2,16,1536]{2,1,0:T(8,128)(2,1)}, bf16[2,16,1536]{2,1,0:T(8,128)(2,1)S(1)}, u32[]{:S(2)}, u32[]{:S(2)}) collective-permute-start(bf16[2,16,1536]{2,1,0:T(8,128)(2,1)} %get-tuple-element.77), channel_id=1, source_target_pairs={{0,1},{1,0},{2,3},{3,2},{4,5},{5,4},{6,7},{7,6},{8,9},{9,8},{10,11... | collective-permute-start | bytes 294920 | tf_op jit(solution)/shard_map/ppermute | solution.py:369
  11.1 2.8 %collective-permute-start.6 = (bf16[2,16,1536]{2,1,0:T(8,128)(2,1)}, bf16[2,16,1536]{2,1,0:T(8,128)(2,1)S(1)}, u32[]{:S(2)}, u32[]{:S(2)}) collective-permute-start(bf16[2,16,1536]{2,1,0:T(8,128)(2,1)} %get-tuple-element.76), channel_id=1, source_target_pairs={{0,31},{1,2},{2,1},{3,4},{4,3},{5,6},{6,5},{7,8},{8,7},{9,10},{10,... | collective-permute-start | bytes 294920 | tf_op jit(solution)/shard_map/ppermute | solution.py:370
  15.3 1.2 %dynamic-slice_bitcast_fusion.3 = (bf16[1,64,1536]{2,1,0:T(8,128)(2,1)S(1)}, bf16[1,64,1536]{2,1,0:T(8,128)(2,1)S(1)}, bf16[1,64,1536]{2,1,0:T(8,128)(2,1)S(1)}) fusion(bf16[4,1,64,1536]{3,2,1,0:T(8,128)(2,1)} %get-tuple-element.69, s32[]{:T(128)S(6)} %select_n.54, s32[]{:T(128)S(6)} %select_n.53, s32[]{:T(128)S(6)} %select_n.52), kind=kLoop, calls=%fused_computation.13 | loop fusion | bytes 1179660 | tf_op jit(solution)/shard_map/jit(dynamic_index_in_dim)/squeeze | solution.py:340
  16.9 2.5 %collective-permute-start.1 = (bf16[1,64,1536]{2,1,0:T(8,128)(2,1)S(1)}, bf16[1,64,1536]{2,1,0:T(8,128)(2,1)S(1)}, u32[]{:S(2)}, u32[]{:S(2)}) collective-permute-start(bf16[1,64,1536]{2,1,0:T(8,128)(2,1)S(1)} %get-tuple-element.74), channel_id=1, source_target_pairs={{0,2},{1,3},{2,0},{3,1},{4,6},{5,7},{6,4},{7,5},{8,10},{9,11},{10,... | collective-permute-start | bytes 589832 | tf_op jit(solution)/shard_map/ppermute | solution.py:361
  20.4 1.5 %collective-permute-start.2 = (bf16[1,64,1536]{2,1,0:T(8,128)(2,1)S(1)}, bf16[1,64,1536]{2,1,0:T(8,128)(2,1)S(1)}, u32[]{:S(2)}, u32[]{:S(2)}) collective-permute-start(bf16[1,64,1536]{2,1,0:T(8,128)(2,1)S(1)} %get-tuple-element.73), channel_id=1, source_target_pairs={{0,3},{1,2},{2,1},{3,0},{4,7},{5,6},{6,5},{7,4},{8,11},{9,10},{10,... | collective-permute-start | bytes 589832 | tf_op jit(solution)/shard_map/ppermute | solution.py:361
  21.8 0.9 %copy-done.11 = bf16[1,64,1536]{2,1,0:T(8,128)(2,1)S(1)} copy-done((bf16[1,64,1536]{2,1,0:T(8,128)(2,1)S(1)}, bf16[1,64,1536]{2,1,0:T(8,128)(2,1)}, u32[]{:S(2)}) %copy-start.11) | copy-done | bytes 196632
  22.8 1.2 %combine.3 = (bf16[64,1536]{1,0:T(8,128)(2,1)S(1)}, bf16[2,32,1536]{2,1,0:T(8,128)(2,1)S(1)}, f32[64,1536]{1,0:T(8,128)S(1)}, f32[64,128]{1,0:T(8,128)S(1)}, bf16[2,64,1536]{2,1,0:T(8,128)(2,1)S(1)}) custom-call(s32[3]{0:T(128)S(1)} %pad_add_fusion.place_ref, bf16[2,1,4,8,8,1536]{5,4,3,2,1,0:T(8,128)(2,1)S(1)} %copy-done, ...), custom_call_target="tpu_custom_call" | custom-call | tf_op jit(solution)/shard_map/combine/pallas_call | solution.py:244
  25.5 1.0 %collective-permute-start.10 = (bf16[32,1536]{1,0:T(8,128)(2,1)}, bf16[32,1536]{1,0:T(8,128)(2,1)}, u32[]{:S(2)}, u32[]{:S(2)}) collective-permute-start(bf16[32,1536]{1,0:T(8,128)(2,1)} %get-tuple-element.82), channel_id=1, source_target_pairs={{0,1},{1,0},{2,3},{3,2},{4,5},{5,4},{6,7},{7,6},{8,9},{9,8},{10,11... | collective-permute-start | bytes 294920 | tf_op jit(solution)/shard_map/ppermute | solution.py:383
  26.6 2.5 %collective-permute-start.11 = (bf16[32,1536]{1,0:T(8,128)(2,1)}, bf16[32,1536]{1,0:T(8,128)(2,1)}, u32[]{:S(2)}, u32[]{:S(2)}) collective-permute-start(bf16[32,1536]{1,0:T(8,128)(2,1)} %get-tuple-element.81), channel_id=1, source_target_pairs={{0,31},{1,2},{2,1},{3,4},{4,3},{5,6},{6,5},{7,8},{8,7},{9,10},{10,... | collective-permute-start | bytes 294920 | tf_op jit(solution)/shard_map/ppermute | solution.py:384
  29.1 2.1 %collective-permute-done.2.rest_2_ = bf16[1,64,1536]{2,1,0:T(8,128)(2,1)S(1)} collective-permute-done((bf16[1,64,1536]{2,1,0:T(8,128)(2,1)S(1)}, bf16[1,64,1536]{2,1,0:T(8,128)(2,1)S(1)}, u32[]{:S(2)}, u32[]{:S(2)}) %collective-permute-start.2) | collective-permute-done | bytes 196640 | tf_op jit(solution)/shard_map/ppermute | solution.py:361
  31.2 1.2 %combine.2 = (bf16[64,1536]{1,0:T(8,128)(2,1)S(1)}, bf16[2,32,1536]{2,1,0:T(8,128)(2,1)S(1)}, f32[64,1536]{1,0:T(8,128)S(1)}, f32[64,128]{1,0:T(8,128)S(1)}, bf16[2,64,1536]{2,1,0:T(8,128)(2,1)S(1)}) custom-call(s32[3]{0:T(128)S(1)} %pad_add_fusion.place_ref, bf16[2,1,4,8,8,1536]{5,4,3,2,1,0:T(8,128)(2,1)S(1)} %copy-done, ...), custom_call_target="tpu_custom_call" | custom-call | tf_op jit(solution)/shard_map/combine/pallas_call | solution.py:244
  32.4 0.7 copy-done.8
  33.9 1.6 %collective-permute-start.3 = (bf16[32,1536]{1,0:T(8,128)(2,1)S(1)}, bf16[32,1536]{1,0:T(8,128)(2,1)S(1)}, u32[]{:S(2)}, u32[]{:S(2)}) collective-permute-start(bf16[32,1536]{1,0:T(8,128)(2,1)S(1)} %get-tuple-element.84), channel_id=1, source_target_pairs={{0,1},{1,0},{2,3},{3,2},{4,5},{5,4},{6,7},{7,6},{8,9},{9,8},{10,11... | collective-permute-start | bytes 294920 | tf_op jit(solution)/shard_map/ppermute | solution.py:383
  35.5 2.2 %collective-permute-start.4 = (bf16[32,1536]{1,0:T(8,128)(2,1)S(1)}, bf16[32,1536]{1,0:T(8,128)(2,1)S(1)}, u32[]{:S(2)}, u32[]{:S(2)}) collective-permute-start(bf16[32,1536]{1,0:T(8,128)(2,1)S(1)} %get-tuple-element.83), channel_id=1, source_target_pairs={{0,31},{1,2},{2,1},{3,4},{4,3},{5,6},{6,5},{7,8},{8,7},{9,10},{10,... | collective-permute-start | bytes 294920 | tf_op jit(solution)/shard_map/ppermute | solution.py:384
  37.8 1.0 %copy-done.5 = bf16[2,64,1536]{2,1,0:T(8,128)(2,1)S(1)} copy-done((bf16[2,64,1536]{2,1,0:T(8,128)(2,1)S(1)}, bf16[2,64,1536]{2,1,0:T(8,128)(2,1)}, u32[]{:S(2)}) %copy-start.5) | copy-done | bytes 393240
  38.8 10.9 %conv.2 = (bf16[2,64,1536]{2,1,0:T(8,128)(2,1)}, f32[2,64,2]{2,1,0:T(8,128)S(1)}, f32[4,32,384]{2,1,0:T(8,128)S(1)}, bf16[64,1536]{1,0:T(8,128)(2,1)S(1)}, bf16[...) custom-call(s32[3]{0:T(128)S(1)} %pad_add_fusion.place_ref, ...), custom_call_target="tpu_custom_call" | custom-call | tf_op jit(solution)/shard_map/conv/pallas_call | solution.py:306
  49.8 10.2 %conv.3 = (bf16[2,64,1536]{2,1,0:T(8,128)(2,1)}, f32[2,64,2]{2,1,0:T(8,128)S(1)}, f32[4,32,384]{2,1,0:T(8,128)S(1)}, bf16[64,1536]{1,0:T(8,128)(2,1)S(1)}, bf16[...) custom-call(s32[3]{0:T(128)S(1)} %pad_add_fusion.place_ref, ...), custom_call_target="tpu_custom_call", output_to_operand_aliasing={{0}: (16, {}), {1}: (17, {})} | custom-call | tf_op jit(solution)/shard_map/conv/pallas_call | solution.py:306
  60.2 3.4 %collective-permute-start.20 = (f32[32,384]{1,0:T(8,128)S(1)}, f32[32,384]{1,0:T(8,128)S(1)}, u32[]{:S(2)}, u32[]{:S(2)}) collective-permute-start(f32[32,384]{1,0:T(8,128)S(1)} %get-tuple-element.79), channel_id=1, source_target_pairs={{0,3},{1,2},{2,1},{3,0},{4,7},{5,6},{6,5},{7,4},{8,11},{9,10},{10,... | collective-permute-start | bytes 147464 | tf_op jit(solution)/shard_map/ppermute | solution.py:361
  64.3 1.6 %collective-permute-done.20 = f32[32,384]{1,0:T(8,128)S(1)} collective-permute-done((f32[32,384]{1,0:T(8,128)S(1)}, f32[32,384]{1,0:T(8,128)S(1)}, u32[]{:S(2)}, u32[]{:S(2)}) %collective-permute-start.20) | collective-permute-done | bytes 49184 | tf_op jit(solution)/shard_map/ppermute | solution.py:361
  66.1 1.3 %collective-permute-start.12 = (bf16[64,1536]{1,0:T(8,128)(2,1)S(1)}, bf16[64,1536]{1,0:T(8,128)(2,1)S(1)}, u32[]{:S(2)}, u32[]{:S(2)}) collective-permute-start(bf16[64,1536]{1,0:T(8,128)(2,1)S(1)} %get-tuple-element.44), channel_id=1, source_target_pairs={{0,1},{1,0},{2,3},{3,2},{4,5},{5,4},{6,7},{7,6},{8,9},{9,8},{10,11... | collective-permute-start | bytes 589832 | tf_op jit(solution)/shard_map/ppermute | solution.py:361
  67.4 1.9 %collective-permute-start.13 = (bf16[64,1536]{1,0:T(8,128)(2,1)S(1)}, bf16[64,1536]{1,0:T(8,128)(2,1)S(1)}, u32[]{:S(2)}, u32[]{:S(2)}) collective-permute-start(bf16[64,1536]{1,0:T(8,128)(2,1)S(1)} %get-tuple-element.45), channel_id=1, source_target_pairs={{0,2},{1,3},{2,0},{3,1},{4,6},{5,7},{6,4},{7,5},{8,10},{9,11},{10,... | collective-permute-start | bytes 589832 | tf_op jit(solution)/shard_map/ppermute | solution.py:361
  69.6 1.3 %collective-permute-start.15 = (bf16[64,1536]{1,0:T(8,128)(2,1)S(1)}, bf16[64,1536]{1,0:T(8,128)(2,1)S(1)}, u32[]{:S(2)}, u32[]{:S(2)}) collective-permute-start(bf16[64,1536]{1,0:T(8,128)(2,1)S(1)} %get-tuple-element.48), channel_id=1, source_target_pairs={{0,1},{1,0},{2,3},{3,2},{4,5},{5,4},{6,7},{7,6},{8,9},{9,8},{10,11... | collective-permute-start | bytes 589832 | tf_op jit(solution)/shard_map/ppermute | solution.py:361
  70.9 1.5 %collective-permute-start.22 = (f32[32,384]{1,0:T(8,128)S(1)}, f32[32,384]{1,0:T(8,128)S(1)}, u32[]{:S(2)}, u32[]{:S(2)}) collective-permute-start(f32[32,384]{1,0:T(8,128)S(1)} %add.106), channel_id=1, source_target_pairs={{0,8},{4,12},{8,0},{12,4},{16,24},{20,28},{24,16},{28,20},{1,9},{5... | collective-permute-start | bytes 147464 | tf_op jit(solution)/shard_map/ppermute | solution.py:405
  72.4 1.3 %broadcast_in_dim.32 = bf16[2,4,64,1536]{3,2,1,0:T(8,128)(2,1)} broadcast(bf16[]{:T(256)} %constant.77.clone.1), dimensions={} | broadcast | bytes 1572866 | tf_op jit(solution)/shard_map/broadcast_in_dim | solution.py:392
  75.1 1.9 %collective-permute-start.16 = (bf16[64,1536]{1,0:T(8,128)(2,1)S(1)}, bf16[64,1536]{1,0:T(8,128)(2,1)S(1)}, u32[]{:S(2)}, u32[]{:S(2)}) collective-permute-start(bf16[64,1536]{1,0:T(8,128)(2,1)S(1)} %get-tuple-element.49), channel_id=1, source_target_pairs={{0,2},{1,3},{2,0},{3,1},{4,6},{5,7},{6,4},{7,5},{8,10},{9,11},{10,... | collective-permute-start | bytes 589832 | tf_op jit(solution)/shard_map/ppermute | solution.py:361
  78.0 0.8 collective-permute-done.13
  78.9 2.8 %collective-permute-start.23 = (f32[32,384]{1,0:T(8,128)S(1)}, f32[32,384]{1,0:T(8,128)S(1)}, u32[]{:S(2)}, u32[]{:S(2)}) collective-permute-start(f32[32,384]{1,0:T(8,128)S(1)} %add.107), channel_id=1, source_target_pairs={{0,16},{4,20},{8,24},{12,28},{16,0},{20,4},{24,8},{28,12},{1,17},{... | collective-permute-start | bytes 147464 | tf_op jit(solution)/shard_map/ppermute | solution.py:405
  84.5 2.7 %collective-permute-done.16 = bf16[64,1536]{1,0:T(8,128)(2,1)S(1)} collective-permute-done((bf16[64,1536]{1,0:T(8,128)(2,1)S(1)}, bf16[64,1536]{1,0:T(8,128)(2,1)S(1)}, u32[]{:S(2)}, u32[]{:S(2)}) %collective-permute-start.16) | collective-permute-done | bytes 196640 | tf_op jit(solution)/shard_map/ppermute | solution.py:361
  (104 shorter events, 14.5 us)
Async XLA Ops:
  3.1 12.0 %copy-start.20 = (f32[2,64,2]{1,2,0:T(2,128)S(1)}, f32[2,64,2]{1,2,0:T(2,128)}, u32[]{:S(2)}) copy-start(f32[2,64,2]{1,2,0:T(2,128)} %param.13) | copy-start | bytes 3076
  3.1 12.1 %copy-start.18 = (f32[1536]{0:T(1024)S(1)}, f32[1536]{0:T(1024)}, u32[]{:S(2)}) copy-start(f32[1536]{0:T(1024)} %param.15) | copy-start | bytes 18436
  3.1 18.7 %copy-start = (bf16[2,1,4,8,8,1536]{5,4,3,2,1,0:T(8,128)(2,1)S(1)}, bf16[2,1,4,8,8,1536]{5,4,3,2,1,0:T(8,128)(2,1)}, u32[]{:S(2)}) copy-start(bf16[2,1,4,8,8,1536]{5,4,3,2,1,0:T(8,128)(2,1)} %own_ref.3) | copy-start | bytes 4718596
  3.1 18.7 %copy-start.2 = (bf16[2,64,1536]{2,1,0:T(8,128)(2,1)S(1)}, bf16[2,64,1536]{2,1,0:T(8,128)(2,1)}, u32[]{:S(2)}) copy-start(bf16[2,64,1536]{2,1,0:T(8,128)(2,1)} %rest_3_.3) | copy-start | bytes 1179652
  4.0 12.6 %collective-permute-start.7 = (bf16[1,64,1536]{2,1,0:T(8,128)(2,1)}, bf16[1,64,1536]{2,1,0:T(8,128)(2,1)S(1)}, u32[]{:S(2)}, u32[]{:S(2)}) collective-permute-start(bf16[1,64,1536]{2,1,0:T(8,128)(2,1)} %get-tuple-element.72), channel_id=1, source_target_pairs={{0,1},{1,0},{2,3},{3,2},{4,5},{5,4},{6,7},{7,6},{8,9},{9,8},{10,11... | collective-permute-start | bytes 589832 | tf_op jit(solution)/shard_map/ppermute | solution.py:361
  6.9 10.0 %collective-permute-start.8 = (bf16[1,64,1536]{2,1,0:T(8,128)(2,1)}, bf16[1,64,1536]{2,1,0:T(8,128)(2,1)S(1)}, u32[]{:S(2)}, u32[]{:S(2)}) collective-permute-start(bf16[1,64,1536]{2,1,0:T(8,128)(2,1)} %get-tuple-element.71), channel_id=1, source_target_pairs={{0,2},{1,3},{2,0},{3,1},{4,6},{5,7},{6,4},{7,5},{8,10},{9,11},{10,... | collective-permute-start | bytes 589832 | tf_op jit(solution)/shard_map/ppermute | solution.py:361
  8.4 11.3 %collective-permute-start.9 = (bf16[1,64,1536]{2,1,0:T(8,128)(2,1)}, bf16[1,64,1536]{2,1,0:T(8,128)(2,1)S(1)}, u32[]{:S(2)}, u32[]{:S(2)}) collective-permute-start(bf16[1,64,1536]{2,1,0:T(8,128)(2,1)} %get-tuple-element.70), channel_id=1, source_target_pairs={{0,3},{1,2},{2,1},{3,0},{4,7},{5,6},{6,5},{7,4},{8,11},{9,10},{10,... | collective-permute-start | bytes 589832 | tf_op jit(solution)/shard_map/ppermute | solution.py:361
  9.1 26.3 %collective-permute-start.5 = (bf16[2,16,1536]{2,1,0:T(8,128)(2,1)}, bf16[2,16,1536]{2,1,0:T(8,128)(2,1)S(1)}, u32[]{:S(2)}, u32[]{:S(2)}) collective-permute-start(bf16[2,16,1536]{2,1,0:T(8,128)(2,1)} %get-tuple-element.77), channel_id=1, source_target_pairs={{0,1},{1,0},{2,3},{3,2},{4,5},{5,4},{6,7},{7,6},{8,9},{9,8},{10,11... | collective-permute-start | bytes 294920 | tf_op jit(solution)/shard_map/ppermute | solution.py:369
  11.1 26.7 %collective-permute-start.6 = (bf16[2,16,1536]{2,1,0:T(8,128)(2,1)}, bf16[2,16,1536]{2,1,0:T(8,128)(2,1)S(1)}, u32[]{:S(2)}, u32[]{:S(2)}) collective-permute-start(bf16[2,16,1536]{2,1,0:T(8,128)(2,1)} %get-tuple-element.76), channel_id=1, source_target_pairs={{0,31},{1,2},{2,1},{3,4},{4,3},{5,6},{6,5},{7,8},{8,7},{9,10},{10,... | collective-permute-start | bytes 294920 | tf_op jit(solution)/shard_map/ppermute | solution.py:370
  16.6 8.9 %collective-permute-start = (bf16[1,64,1536]{2,1,0:T(8,128)(2,1)S(1)}, bf16[1,64,1536]{2,1,0:T(8,128)(2,1)S(1)}, u32[]{:S(2)}, u32[]{:S(2)}) collective-permute-start(bf16[1,64,1536]{2,1,0:T(8,128)(2,1)S(1)} %get-tuple-element.75), channel_id=1, source_target_pairs={{0,1},{1,0},{2,3},{3,2},{4,5},{5,4},{6,7},{7,6},{8,9},{9,8},{10,11... | collective-permute-start | bytes 589832 | tf_op jit(solution)/shard_map/ppermute | solution.py:361
  16.9 9.7 %collective-permute-start.1 = (bf16[1,64,1536]{2,1,0:T(8,128)(2,1)S(1)}, bf16[1,64,1536]{2,1,0:T(8,128)(2,1)S(1)}, u32[]{:S(2)}, u32[]{:S(2)}) collective-permute-start(bf16[1,64,1536]{2,1,0:T(8,128)(2,1)S(1)} %get-tuple-element.74), channel_id=1, source_target_pairs={{0,2},{1,3},{2,0},{3,1},{4,6},{5,7},{6,4},{7,5},{8,10},{9,11},{10,... | collective-permute-start | bytes 589832 | tf_op jit(solution)/shard_map/ppermute | solution.py:361
  20.4 10.8 %collective-permute-start.2 = (bf16[1,64,1536]{2,1,0:T(8,128)(2,1)S(1)}, bf16[1,64,1536]{2,1,0:T(8,128)(2,1)S(1)}, u32[]{:S(2)}, u32[]{:S(2)}) collective-permute-start(bf16[1,64,1536]{2,1,0:T(8,128)(2,1)S(1)} %get-tuple-element.73), channel_id=1, source_target_pairs={{0,3},{1,2},{2,1},{3,0},{4,7},{5,6},{6,5},{7,4},{8,11},{9,10},{10,... | collective-permute-start | bytes 589832 | tf_op jit(solution)/shard_map/ppermute | solution.py:361
  25.5 12.2 %collective-permute-start.10 = (bf16[32,1536]{1,0:T(8,128)(2,1)}, bf16[32,1536]{1,0:T(8,128)(2,1)}, u32[]{:S(2)}, u32[]{:S(2)}) collective-permute-start(bf16[32,1536]{1,0:T(8,128)(2,1)} %get-tuple-element.82), channel_id=1, source_target_pairs={{0,1},{1,0},{2,3},{3,2},{4,5},{5,4},{6,7},{7,6},{8,9},{9,8},{10,11... | collective-permute-start | bytes 294920 | tf_op jit(solution)/shard_map/ppermute | solution.py:383
  26.6 11.2 %copy-start.3 = (f32[31,1536]{1,0:T(8,128)S(1)}, f32[31,1536]{1,0:T(8,128)}, u32[]{:S(2)}) copy-start(f32[31,1536]{1,0:T(8,128)} %kernel_ref.3) | copy-start | bytes 571396
  26.6 11.2 %copy-start.13 = (bf16[64,1536]{1,0:T(8,128)(2,1)S(1)}, bf16[64,1536]{1,0:T(8,128)(2,1)}, u32[]{:S(2)}) copy-start(bf16[64,1536]{1,0:T(8,128)(2,1)} %copy-done.12) | copy-start | bytes 589828
  26.6 11.3 %copy-start.16 = (s32[2,8]{1,0:T(2,128)S(1)}, s32[2,8]{1,0:T(2,128)}, u32[]{:S(2)}) copy-start(s32[2,8]{1,0:T(2,128)} %lengths_ref.3) | copy-start | bytes 196
  26.6 11.2 %collective-permute-start.11 = (bf16[32,1536]{1,0:T(8,128)(2,1)}, bf16[32,1536]{1,0:T(8,128)(2,1)}, u32[]{:S(2)}, u32[]{:S(2)}) collective-permute-start(bf16[32,1536]{1,0:T(8,128)(2,1)} %get-tuple-element.81), channel_id=1, source_target_pairs={{0,31},{1,2},{2,1},{3,4},{4,3},{5,6},{6,5},{7,8},{8,7},{9,10},{10,... | collective-permute-start | bytes 294920 | tf_op jit(solution)/shard_map/ppermute | solution.py:384
  33.8 15.9 %copy-start.9 = (bf16[2,64,1536]{2,1,0:T(8,128)(2,1)S(1)}, bf16[2,64,1536]{2,1,0:T(8,128)(2,1)}, u32[]{:S(2)}) copy-start(bf16[2,64,1536]{2,1,0:T(8,128)(2,1)} %copy-done.8) | copy-start | bytes 1179652
  33.9 15.9 %collective-permute-start.3 = (bf16[32,1536]{1,0:T(8,128)(2,1)S(1)}, bf16[32,1536]{1,0:T(8,128)(2,1)S(1)}, u32[]{:S(2)}, u32[]{:S(2)}) collective-permute-start(bf16[32,1536]{1,0:T(8,128)(2,1)S(1)} %get-tuple-element.84), channel_id=1, source_target_pairs={{0,1},{1,0},{2,3},{3,2},{4,5},{5,4},{6,7},{7,6},{8,9},{9,8},{10,11... | collective-permute-start | bytes 294920 | tf_op jit(solution)/shard_map/ppermute | solution.py:383
  35.5 14.3 %collective-permute-start.4 = (bf16[32,1536]{1,0:T(8,128)(2,1)S(1)}, bf16[32,1536]{1,0:T(8,128)(2,1)S(1)}, u32[]{:S(2)}, u32[]{:S(2)}) collective-permute-start(bf16[32,1536]{1,0:T(8,128)(2,1)S(1)} %get-tuple-element.83), channel_id=1, source_target_pairs={{0,31},{1,2},{2,1},{3,4},{4,3},{5,6},{6,5},{7,8},{8,7},{9,10},{10,... | collective-permute-start | bytes 294920 | tf_op jit(solution)/shard_map/ppermute | solution.py:384
  60.0 4.2 %collective-permute-start.18 = (f32[32,384]{1,0:T(8,128)S(1)}, f32[32,384]{1,0:T(8,128)S(1)}, u32[]{:S(2)}, u32[]{:S(2)}) collective-permute-start(f32[32,384]{1,0:T(8,128)S(1)} %get-tuple-element.78), channel_id=1, source_target_pairs={{0,1},{1,0},{2,3},{3,2},{4,5},{5,4},{6,7},{7,6},{8,9},{9,8},{10,11... | collective-permute-start | bytes 147464 | tf_op jit(solution)/shard_map/ppermute | solution.py:361
  60.1 4.2 %collective-permute-start.19 = (f32[32,384]{1,0:T(8,128)S(1)}, f32[32,384]{1,0:T(8,128)S(1)}, u32[]{:S(2)}, u32[]{:S(2)}) collective-permute-start(f32[32,384]{1,0:T(8,128)S(1)} %get-tuple-element.80), channel_id=1, source_target_pairs={{0,2},{1,3},{2,0},{3,1},{4,6},{5,7},{6,4},{7,5},{8,10},{9,11},{10,... | collective-permute-start | bytes 147464 | tf_op jit(solution)/shard_map/ppermute | solution.py:361
  60.2 5.7 %collective-permute-start.20 = (f32[32,384]{1,0:T(8,128)S(1)}, f32[32,384]{1,0:T(8,128)S(1)}, u32[]{:S(2)}, u32[]{:S(2)}) collective-permute-start(f32[32,384]{1,0:T(8,128)S(1)} %get-tuple-element.79), channel_id=1, source_target_pairs={{0,3},{1,2},{2,1},{3,0},{4,7},{5,6},{6,5},{7,4},{8,11},{9,10},{10,... | collective-permute-start | bytes 147464 | tf_op jit(solution)/shard_map/ppermute | solution.py:361
  65.9 5.0 %collective-permute-start.21 = (f32[32,384]{1,0:T(8,128)S(1)}, f32[32,384]{1,0:T(8,128)S(1)}, u32[]{:S(2)}, u32[]{:S(2)}) collective-permute-start(f32[32,384]{1,0:T(8,128)S(1)} %fusion.10), channel_id=1, source_target_pairs={{0,4},{4,0},{8,12},{12,8},{16,20},{20,16},{24,28},{28,24},{1,5},{5... | collective-permute-start | bytes 147464 | tf_op jit(solution)/shard_map/ppermute | solution.py:405
  66.1 10.9 %collective-permute-start.12 = (bf16[64,1536]{1,0:T(8,128)(2,1)S(1)}, bf16[64,1536]{1,0:T(8,128)(2,1)S(1)}, u32[]{:S(2)}, u32[]{:S(2)}) collective-permute-start(bf16[64,1536]{1,0:T(8,128)(2,1)S(1)} %get-tuple-element.44), channel_id=1, source_target_pairs={{0,1},{1,0},{2,3},{3,2},{4,5},{5,4},{6,7},{7,6},{8,9},{9,8},{10,11... | collective-permute-start | bytes 589832 | tf_op jit(solution)/shard_map/ppermute | solution.py:361
  67.4 11.4 %collective-permute-start.13 = (bf16[64,1536]{1,0:T(8,128)(2,1)S(1)}, bf16[64,1536]{1,0:T(8,128)(2,1)S(1)}, u32[]{:S(2)}, u32[]{:S(2)}) collective-permute-start(bf16[64,1536]{1,0:T(8,128)(2,1)S(1)} %get-tuple-element.45), channel_id=1, source_target_pairs={{0,2},{1,3},{2,0},{3,1},{4,6},{5,7},{6,4},{7,5},{8,10},{9,11},{10,... | collective-permute-start | bytes 589832 | tf_op jit(solution)/shard_map/ppermute | solution.py:361
  69.3 13.1 %collective-permute-start.14 = (bf16[64,1536]{1,0:T(8,128)(2,1)S(1)}, bf16[64,1536]{1,0:T(8,128)(2,1)S(1)}, u32[]{:S(2)}, u32[]{:S(2)}) collective-permute-start(bf16[64,1536]{1,0:T(8,128)(2,1)S(1)} %get-tuple-element.46), channel_id=1, source_target_pairs={{0,3},{1,2},{2,1},{3,0},{4,7},{5,6},{6,5},{7,4},{8,11},{9,10},{10,... | collective-permute-start | bytes 589832 | tf_op jit(solution)/shard_map/ppermute | solution.py:361
  69.6 14.2 %collective-permute-start.15 = (bf16[64,1536]{1,0:T(8,128)(2,1)S(1)}, bf16[64,1536]{1,0:T(8,128)(2,1)S(1)}, u32[]{:S(2)}, u32[]{:S(2)}) collective-permute-start(bf16[64,1536]{1,0:T(8,128)(2,1)S(1)} %get-tuple-element.48), channel_id=1, source_target_pairs={{0,1},{1,0},{2,3},{3,2},{4,5},{5,4},{6,7},{7,6},{8,9},{9,8},{10,11... | collective-permute-start | bytes 589832 | tf_op jit(solution)/shard_map/ppermute | solution.py:361
  70.9 4.2 %collective-permute-start.22 = (f32[32,384]{1,0:T(8,128)S(1)}, f32[32,384]{1,0:T(8,128)S(1)}, u32[]{:S(2)}, u32[]{:S(2)}) collective-permute-start(f32[32,384]{1,0:T(8,128)S(1)} %add.106), channel_id=1, source_target_pairs={{0,8},{4,12},{8,0},{12,4},{16,24},{20,28},{24,16},{28,20},{1,9},{5... | collective-permute-start | bytes 147464 | tf_op jit(solution)/shard_map/ppermute | solution.py:405
  75.1 12.1 %collective-permute-start.16 = (bf16[64,1536]{1,0:T(8,128)(2,1)S(1)}, bf16[64,1536]{1,0:T(8,128)(2,1)S(1)}, u32[]{:S(2)}, u32[]{:S(2)}) collective-permute-start(bf16[64,1536]{1,0:T(8,128)(2,1)S(1)} %get-tuple-element.49), channel_id=1, source_target_pairs={{0,2},{1,3},{2,0},{3,1},{4,6},{5,7},{6,4},{7,5},{8,10},{9,11},{10,... | collective-permute-start | bytes 589832 | tf_op jit(solution)/shard_map/ppermute | solution.py:361
  77.0 11.5 %collective-permute-start.17 = (bf16[64,1536]{1,0:T(8,128)(2,1)S(1)}, bf16[64,1536]{1,0:T(8,128)(2,1)S(1)}, u32[]{:S(2)}, u32[]{:S(2)}) collective-permute-start(bf16[64,1536]{1,0:T(8,128)(2,1)S(1)} %get-tuple-element.50), channel_id=1, source_target_pairs={{0,3},{1,2},{2,1},{3,0},{4,7},{5,6},{6,5},{7,4},{8,11},{9,10},{10,... | collective-permute-start | bytes 589832 | tf_op jit(solution)/shard_map/ppermute | solution.py:361
  78.9 9.0 %collective-permute-start.23 = (f32[32,384]{1,0:T(8,128)S(1)}, f32[32,384]{1,0:T(8,128)S(1)}, u32[]{:S(2)}, u32[]{:S(2)}) collective-permute-start(f32[32,384]{1,0:T(8,128)S(1)} %add.107), channel_id=1, source_target_pairs={{0,16},{4,20},{8,24},{12,28},{16,0},{20,4},{24,8},{28,12},{1,17},{... | collective-permute-start | bytes 147464 | tf_op jit(solution)/shard_map/ppermute | solution.py:405
  (14 other events, 61.3 us)

commit v2 on v1

v2 whole, which is shorter than its diff:
```python
import functools
import math

import jax
import jax.numpy as jnp
from jax import lax
from jax.experimental import pallas as pl
from jax.experimental.pallas import tpu as pltpu
from jax.sharding import PartitionSpec as P

EXPERTS = 32
KW = 31
HALF = 15
CAP = 8
SIDE = 32
GSIDE = 16
F32 = jnp.float32
BF16 = jnp.bfloat16
VMEM_LIMIT = 12 * 1024 * 1024
SMALL_LIMIT = 4 * 1024 * 1024


def slot_table(route_rows, order_row):
    row_count = route_rows.shape[0]
    sort_keys = (order_row[:, None] * 2 + jnp.arange(2, dtype=jnp.int32)[None, :]).reshape(-1)
    owners = route_rows.reshape(-1)
    before = (owners[:, None] == owners[None, :]) & (sort_keys[None, :] < sort_keys[:, None])
    return jnp.sum(before.astype(jnp.int32), axis=1).reshape(row_count, 2)


def combine_kernel(
    group_count,
    place_ref,
    *rest,
):
    table_refs = rest[:group_count]
    frames_ref, grad_out_ref, flat_ref, probs_ref, gain_ref = rest[group_count : group_count + 5]
    conv_in_ref, near_ref, far_ref, nhat_ref, rstd_ref, picked_ref = rest[-6:]
    rows = frames_ref.shape[1]
    width = frames_ref.shape[2]
    flat = flat_ref[0]
    probs = probs_ref[0]
    table = jnp.concatenate([r[...] for r in table_refs], axis=0)
    lane = lax.broadcasted_iota(jnp.int32, (rows, table.shape[0]), 1)
    mixed = frames_ref[0].astype(F32)
    for k in range(2):
        hot = jnp.where(lane == flat[:, k : k + 1], 1.0, 0.0).astype(BF16)
        row = jnp.dot(hot, table, preferred_element_type=F32)
        picked_ref[k] = row.astype(BF16)
        mixed = mixed + probs[:, k : k + 1] * row
    mean = jnp.mean(mixed, axis=1, keepdims=True)
    centred = mixed - mean
    rstd = lax.rsqrt(jnp.mean(centred * centred, axis=1, keepdims=True) + 1e-05)
    nhat = centred * rstd
    nhat_ref[...] = nhat
    rstd_ref[...] = jnp.broadcast_to(rstd, rstd_ref.shape)
    conv_in = (nhat * gain_ref[...]).astype(BF16)
    conv_in_ref[...] = conv_in
    odd = place_ref[1]

    def send(ref, first):
        ref[:SIDE] = conv_in[:SIDE] if first else conv_in[rows - SIDE :]
        ref[SIDE:] = grad_out_ref[0, :GSIDE] if first else grad_out_ref[0, rows - GSIDE :]

    @pl.when(odd == 0)
    def _():
        send(near_ref, False)
        send(far_ref, True)

    @pl.when(odd == 1)
    def _():
        send(near_ref, True)
        send(far_ref, False)


def swish_slope(values):
    sigmoid_v = jax.nn.sigmoid(values)
    return sigmoid_v * (1.0 + values * (1.0 - sigmoid_v))


def conv_kernel(
    group_count,
    first,
    micro,
    frame_total,
    scale,
    place_ref,
    lengths_ref,
    conv_in_ref,
    near_ref,
    far_ref,
    grad_out_ref,
    nhat_ref,
    rstd_ref,
    picked_ref,
    flat_row_ref,
    probs_ref,
    gain_ref,
    kernel_ref,
    *rest,
):
    if first:
        grad_x_ref, grad_probs_ref, terms_ref = rest[:3]
        rest = rest[3:]
        last_terms = None
    else:
        last_terms, _, _, grad_x_ref, grad_probs_ref, terms_ref = rest[:6]
        rest = rest[6:]
    out_refs = rest[:group_count]
    window, gout, shifts, gwin, kacc = rest[group_count:]
    rows, width = conv_in_ref.shape
    mid = rows + 2 * GSIDE
    full = rows + 2 * SIDE
    odd = place_ref[1]

    window[SIDE : SIDE + rows, :] = conv_in_ref[...]
    gout[GSIDE : GSIDE + rows, :] = grad_out_ref[0]

    def receive(before, after):
        window[:SIDE, :] = before[:SIDE]
        window[SIDE + rows :, :] = after[:SIDE]
        gout[:GSIDE, :] = before[SIDE:]
        gout[GSIDE + rows :, :] = after[SIDE:]

    @pl.when(odd == 0)
    def _():
        receive(far_ref, near_ref)

    @pl.when(odd == 1)
    def _():
        receive(near_ref, far_ref)

    gwin[: SIDE - GSIDE, :] = jnp.zeros((SIDE - GSIDE, width), BF16)
    gwin[SIDE - GSIDE + mid :, :] = jnp.zeros((SIDE - GSIDE, width), BF16)

    first_frame = place_ref[0]
    t_local = lax.broadcasted_iota(jnp.int32, (mid, full), 0)
    r_local = lax.broadcasted_iota(jnp.int32, (mid, full), 1)
    t_pos = first_frame - GSIDE + t_local
    r_pos = first_frame - SIDE + r_local

    def count(u, carry):
        end, t_seg, r_seg = carry
        end = end + lengths_ref[micro, u]
        return (
            end,
            t_seg + jnp.where(t_pos >= end, 1, 0),
            r_seg + jnp.where(r_pos >= end, 1, 0),
        )

    zero = jnp.zeros((mid, full), jnp.int32)
    _, t_seg, r_seg = lax.fori_loop(0, lengths_ref.shape[1], count, (0, zero, zero))
    same = (t_seg == r_seg) & (t_pos >= 0) & (t_pos < frame_total) & (r_pos >= 0) & (r_pos < frame_total)
    gap = jnp.where(same, r_local - t_local - (SIDE - GSIDE - HALF), -1)
    for i in range(KW):
        shifts[i * mid : (i + 1) * mid, :] = jnp.where(gap == i, 1.0, 0.0).astype(BF16)

    taps = kernel_ref[...]
    xw = window[...]
    acc = jnp.zeros((mid, width), F32)
    for i in range(KW):
        v = jnp.dot(shifts[i * mid : (i + 1) * mid, :], xw, preferred_element_type=F32)
        acc = acc + taps[i : i + 1, :] * v
    g = (gout[...].astype(F32) * swish_slope(acc)).astype(BF16)
    gwin[SIDE - GSIDE : SIDE - GSIDE + mid, :] = g
    gw = gwin[...]
    x = conv_in_ref[...].astype(F32)
    acc = jnp.zeros((rows, width), F32)
    for j in range(KW):
        base = j * mid + GSIDE
        v = jnp.dot(shifts[base : base + rows, :], gw, preferred_element_type=F32)
        i = KW - 1 - j
        acc = acc + taps[i : i + 1, :] * v
        kacc[i : i + 1, :] = jnp.sum(x * v, axis=0, keepdims=True)
    grad_in = acc.astype(BF16).astype(F32)
    nhat = nhat_ref[...]
    kacc[KW : KW + 1, :] = jnp.sum(grad_in * nhat, axis=0, keepdims=True)
    dn = grad_in * gain_ref[...]
    m1 = jnp.sum(dn, axis=1, keepdims=True) * (1.0 / width)
    m2 = jnp.sum(dn * nhat, axis=1, keepdims=True) * (1.0 / width)
    rstd = rstd_ref[:, :1]
    dmixed = grad_out_ref[0].astype(F32) + rstd * (dn - m1 - nhat * m2)
    grad_x_ref[0] = dmixed.astype(BF16)
    probs = probs_ref[0]
    values = jnp.concatenate(
        [(probs[:, 0:1] * dmixed).astype(BF16), (probs[:, 1:2] * dmixed).astype(BF16)], axis=0
    )
    slots = out_refs[0].shape[0]
    spots = lax.broadcasted_iota(jnp.int32, (slots * group_count, 2 * rows), 0)
    hot = jnp.where(spots == flat_row_ref[0], 1.0, 0.0).astype(BF16)
    placed = jnp.dot(hot, values, preferred_element_type=F32).astype(BF16)
    for e in range(group_count):
        out_refs[e][...] = placed[e * slots : (e + 1) * slots]
    p0 = jnp.sum(dmixed * picked_ref[0].astype(F32), axis=1, keepdims=True)
    p1 = jnp.sum(dmixed * picked_ref[1].astype(F32), axis=1, keepdims=True)
    two = lax.broadcasted_iota(jnp.int32, (rows, 2), 1)
    grad_probs_ref[0] = jnp.where(two == 0, p0, p1)
    part = width // group_count
    for e in range(group_count):
        share = kacc[:, e * part : (e + 1) * part] * scale
        if last_terms is not None:
            share = share + last_terms[e]
        terms_ref[e] = share


def whole(shape):
    return pl.BlockSpec(shape, lambda *_: (0,) * len(shape))


def of_micro(micro, shape):
    return pl.BlockSpec((1,) + shape[1:], lambda *_: (micro,) + (0,) * (len(shape) - 1))


def combine(micro, place, tables, frames, grad_out, flat, probs, gain):
    group_count = len(tables)
    rows, width = frames.shape[1:]
    return pl.pallas_call(
        functools.partial(combine_kernel, group_count),
        grid_spec=pltpu.PrefetchScalarGridSpec(
            num_scalar_prefetch=1,
            grid=(1,),
            in_specs=[whole(t.shape) for t in tables]
            + [
                of_micro(micro, frames.shape),
                of_micro(micro, grad_out.shape),
                of_micro(micro, flat.shape),
                of_micro(micro, probs.shape),
                whole(gain.shape),
            ],
            out_specs=[
                whole((rows, width)),
                whole((SIDE + GSIDE, width)),
                whole((SIDE + GSIDE, width)),
                whole((rows, width)),
                whole((rows, 128)),
                whole((2, rows, width)),
            ],
        ),
        out_shape=[
            jax.ShapeDtypeStruct((rows, width), BF16),
            jax.ShapeDtypeStruct((SIDE + GSIDE, width), BF16),
            jax.ShapeDtypeStruct((SIDE + GSIDE, width), BF16),
            jax.ShapeDtypeStruct((rows, width), F32),
            jax.ShapeDtypeStruct((rows, 128), F32),
            jax.ShapeDtypeStruct((2, rows, width), BF16),
        ],
        compiler_params=pltpu.CompilerParams(vmem_limit_bytes=VMEM_LIMIT),
        cost_estimate=pl.CostEstimate(flops=1500 * 10**6, bytes_accessed=0, transcendentals=0),
        name="combine",
    )(place, *tables, frames, grad_out, flat, probs, gain)


def conv(micro, place, lengths, group_count, frame_total, conv_in, near, far, grad_out, nhat, rstd, picked, flat_row, probs, gain, kernel, earlier):
    rows, width = conv_in.shape
    micro_count = grad_out.shape[0]
    first = earlier is None
    slots = EXPERTS * CAP // group_count
    mid = rows + 2 * GSIDE
    full = rows + 2 * SIDE
    terms_shape = (group_count, KW + 1, width // group_count)
    in_specs = [
        whole(conv_in.shape),
        whole(near.shape),
        whole(far.shape),
        of_micro(micro, grad_out.shape),
        whole(nhat.shape),
        whole(rstd.shape),
        whole(picked.shape),
        of_micro(micro, flat_row.shape),
        of_micro(micro, probs.shape),
        whole(gain.shape),
        whole(kernel.shape),
    ]
    operands = [place, lengths, conv_in, near, far, grad_out, nhat, rstd, picked, flat_row, probs, gain, kernel]
    aliases = {}
    if not first:
        in_specs += [whole(terms_shape), pl.BlockSpec(memory_space=pl.ANY), pl.BlockSpec(memory_space=pl.ANY)]
        aliases = {len(operands) + 1: 0, len(operands) + 2: 1}
        operands += [earlier[2], earlier[0], earlier[1]]
    return pl.pallas_call(
        functools.partial(
            conv_kernel, group_count, first, micro, frame_total, 1.0 / math.sqrt(micro_count * frame_total)
        ),
        grid_spec=pltpu.PrefetchScalarGridSpec(
            num_scalar_prefetch=2,
            grid=(1,),
            in_specs=in_specs,
            out_specs=[
                of_micro(micro, grad_out.shape),
                of_micro(micro, probs.shape),
                whole(terms_shape),
            ]
            + [whole((slots, width))] * group_count,
            scratch_shapes=[
                pltpu.VMEM((full, width), BF16),
                pltpu.VMEM((mid, width), BF16),
                pltpu.VMEM((KW * mid, full), BF16),
                pltpu.VMEM((full, width), BF16),
                pltpu.VMEM((KW + 1, width), F32),
            ],
        ),
        out_shape=[
            jax.ShapeDtypeStruct((micro_count, rows, width), BF16),
            jax.ShapeDtypeStruct(probs.shape, F32),
            jax.ShapeDtypeStruct(terms_shape, F32),
        ]
        + [jax.ShapeDtypeStruct((slots, width), BF16)] * group_count,
        input_output_aliases=aliases,
        compiler_params=pltpu.CompilerParams(vmem_limit_bytes=VMEM_LIMIT),
        cost_estimate=pl.CostEstimate(flops=8 * 10**9, bytes_accessed=0, transcendentals=0),
        name="conv",
    )(*operands)


def finish_kernel(group_count, micro, part_count, place_ref, *refs):
    blocks = refs[:group_count]
    parts = refs[group_count : group_count + part_count]
    rest = refs[group_count + part_count :]
    if part_count:
        _, out_ref, taps_ref, gain_ref, sems = rest
    else:
        out_ref, sems = rest
    me = place_ref[2]
    copies = [
        pltpu.make_async_copy(block, out_ref.at[micro, jnp.bitwise_xor(me, step)], sems.at[step])
        for step, block in enumerate(blocks)
    ]
    for copy in copies:
        copy.start()
    if part_count:
        total = parts[0][...]
        for part in parts[1:]:
            total = total + part[...]
        taps_ref[...] = total[:KW]
        gain_ref[...] = total[KW]
    for copy in copies:
        copy.wait()


def finish(micro, micro_count, place, blocks, parts=(), earlier=None):
    group_count = len(blocks)
    slots, width = blocks[0].shape
    anywhere = pl.BlockSpec(memory_space=pl.ANY)
    out_shape = [jax.ShapeDtypeStruct((micro_count, group_count, slots, width), BF16)]
    out_specs = [anywhere]
    in_specs = [anywhere] * group_count + [whole(p.shape) for p in parts]
    operands = [place, *blocks, *parts]
    aliases = {}
    if earlier is not None:
        aliases = {len(operands): 0}
        operands.append(earlier)
        in_specs.append(anywhere)
        share = parts[0].shape[1]
        out_shape += [jax.ShapeDtypeStruct((KW, share), F32), jax.ShapeDtypeStruct((share,), F32)]
        out_specs += [whole((KW, share)), whole((share,))]
    return pl.pallas_call(
        functools.partial(finish_kernel, group_count, micro, len(parts)),
        grid_spec=pltpu.PrefetchScalarGridSpec(
            num_scalar_prefetch=1,
            grid=(1,),
            in_specs=in_specs,
            out_specs=out_specs,
            scratch_shapes=[pltpu.SemaphoreType.DMA((group_count,))],
        ),
        out_shape=out_shape,
        input_output_aliases=aliases,
        compiler_params=pltpu.CompilerParams(vmem_limit_bytes=4 * 1024 * 1024),
        cost_estimate=pl.CostEstimate(flops=1000 * 10**6, bytes_accessed=0, transcendentals=0),
        name="finish",
    )(*operands)


def take(cells, index):
    return lax.dynamic_index_in_dim(cells, index, axis=0, keepdims=False)


def local(frames, expert_out, routes, order, probs, lengths, gain, kernel, grad_out):
    micro_count, rows, width = frames.shape
    groups = lax.axis_size("expert")
    tm = lax.axis_size("tm")
    both = ("tm", "expert")
    devices = groups * tm
    frame_total = rows * devices
    me = lax.axis_index("expert")
    here = lax.axis_index(both)
    odd = lax.rem(here, 2)
    place = jnp.stack([here * rows, odd, me]).astype(jnp.int32)
    per = EXPERTS // groups
    block = per * CAP
    near_pairs = [(i, i ^ 1) for i in range(devices)]
    far_pairs = [(i, (i - 1) % devices if i % 2 == 0 else (i + 1) % devices) for i in range(devices)]

    def swap(cells, step):
        return lax.ppermute(cells, "expert", [(i, i ^ step) for i in range(groups)])

    tables = []
    cells = expert_out
    sizes = (1, 1, 1) + expert_out.shape[3:]
    for micro in range(micro_count):
        blocks = [
            lax.dynamic_slice(cells, (micro, 0, me ^ step, 0, 0, 0), sizes).reshape(block, width)
            for step in range(groups)
        ]
        cells, *blocks = lax.optimization_barrier([cells, *blocks])
        tables.append([blocks[0]] + [swap(blocks[step], step) for step in range(1, groups)])

    slots = jax.vmap(slot_table)(routes, order[:, 0])
    flat = ((routes // per) ^ me) * block + (routes % per) * CAP + slots
    flat_row = jnp.swapaxes(flat, 1, 2).reshape(micro_count, 1, 2 * rows)
    gain_row = gain[None, :]

    earlier = None
    returned = []
    for micro in range(micro_count):
        conv_in, near, far, nhat, rstd, picked = combine(
            micro, place, tables[micro], frames, grad_out, flat, probs, gain_row
        )
        near = lax.ppermute(near, both, near_pairs)
        far = lax.ppermute(far, both, far_pairs)
        grad_x, grad_probs, terms, *outs = conv(
            micro, place, lengths, groups, frame_total, conv_in, near, far, grad_out,
            nhat, rstd, picked, flat_row, probs, gain_row, kernel, earlier,
        )
        earlier = (grad_x, grad_probs, terms)
        if returned:
            returned[-1], outs = lax.optimization_barrier((returned[-1], outs))
        returned.append([outs[0]] + [swap(outs[step], step) for step in range(1, groups)])

    def over(cells, steps):
        return [lax.ppermute(cells, "tm", [(i, i ^ step) for i in range(tm)]) for step in steps]

    total = take(terms, me)
    for step in range(1, groups):
        total = total + swap(take(terms, me ^ step), step)
    step = 1
    while step < tm // 2:
        total = total + over(total, [step])[0]
        step *= 2
    parts = [total] + over(total, [step])
    grad_expert = None
    for micro in range(micro_count - 1):
        (grad_expert,) = finish(micro, micro_count, place, returned[micro])
    grad_expert, grad_kernel, grad_gain = finish(
        micro_count - 1, micro_count, place, returned[-1], parts, grad_expert
    )
    grad_expert = grad_expert.reshape(micro_count, 1, groups, per, CAP, width)
    return grad_x, grad_expert, grad_probs, grad_kernel, grad_gain


def solution(mesh):
    placed = (
        P(None, ("tm", "expert"), None),
        P(None, "tm", None, "expert", None, None),
        P(None, ("tm", "expert"), None),
        P(None, ("tm", "expert"), None),
        P(None, ("tm", "expert"), None),
        P(),
        P(),
        P(),
        P(None, ("tm", "expert"), None),
    )
    return jax.shard_map(
        local,
        mesh=mesh,
        in_specs=placed,
        out_specs=(
            P(None, ("tm", "expert"), None),
            P(None, "tm", None, "expert", None, None),
            P(None, ("tm", "expert"), None),
            P(None, "expert"),
            P("expert"),
        ),
        check_vma=False,
    )
```

time: 89.4 us -> 69.2 us (0.77)
  local copies, waits for them, and re-layouts: 19.1 us -> 5.98 us
  starting transfers between devices: 35.8 us -> 30.2 us
  Pallas kernels: 23.5 us -> 20.2 us
  waiting for transfers between devices: 8.58 us -> 11.2 us
    ppermute x9 -> x7, starting transfers between devices: 16.6 us -> 8.99 us  [the longest x3 4.48 us: over(): lax.ppermute(cells, 'tm', [(i, i ^ step) for i in range(tm)])]
    pallas_call x2, Pallas kernels: 21.1 us -> 14.3 us  [conv(): pl.pallas_call(functools.partial(conv_kernel, group_count, first, micro,...]
    dynamic_update_slice x8 -> x0, local copies, waits for them, and re-layouts: 5.52 us -> none  [local(): lax.dynamic_update_slice(grad_expert, returned[micro][step][None, None],...]
    unnamed x47 -> x23, local copies, waits for them, and re-layouts: 5.61 us -> 1.64 us
    ppermute x9 -> x7, waiting for transfers between devices: 0.09 us -> 3.91 us  [the longest x3 3.9 us: over(): lax.ppermute(cells, 'tm', [(i, i ^ step) for i in range(tm)])]
    pallas_call x0 -> x2, Pallas kernels: none -> 3.52 us  [finish(): pl.pallas_call(functools.partial(finish_kernel, group_count, micro, len(p...]
    reshape x0 -> x2, local copies, waits for them, and re-layouts: none -> 3.39 us  [local(): lax.dynamic_slice(cells, (micro, 0, me ^ step, 0, 0, 0), sizes)]
    another operation x1 -> x0, local copies, waits for them, and re-layouts: 2.44 us -> none  [local(): source = expert_out[micro, 0].reshape(groups, 1, block, width)]
  transfers between devices with their start and end apart: 24 -> 22, of which waited for: 10 -> 8; matrix products, arithmetic and copies ran while one was open for 13% -> 6% of each run, Pallas kernels for 15% -> 26%
where the time goes in v2:
time: 69.2 us; the launch traced here: 69.1 us
  starting transfers between devices  30.2 us (44%)
  Pallas kernels  20.2 us (29%)
  waiting for transfers between devices  11.2 us (16%)
  local copies, waits for them, and re-layouts  5.98 us (9%)
  between operations  1.08 us (2%)
    ppermute x15, starting transfers between devices, swap(): return lax.ppermute(cells, 'expert', [(i, i ^ step) for i in range(groups)])  21.2 us
    pallas_call x2, Pallas kernels, conv(): pl.pallas_call(functools.partial(conv_kernel, group_count, first, micro,...  14.3 us
    ppermute x15, waiting for transfers between devices, swap(): return lax.ppermute(cells, 'expert', [(i, i ^ step) for i in range(groups)])  7.29 us
    ppermute x3, starting transfers between devices, over(): lax.ppermute(cells, 'tm', [(i, i ^ step) for i in range(tm)])  4.48 us
    ppermute x3, waiting for transfers between devices, over(): lax.ppermute(cells, 'tm', [(i, i ^ step) for i in range(tm)])  3.9 us
    pallas_call x2, Pallas kernels, finish(): pl.pallas_call(functools.partial(finish_kernel, group_count, micro, len(p...  3.52 us
    reshape x2, local copies, waits for them, and re-layouts, local(): lax.dynamic_slice(cells, (micro, 0, me ^ step, 0, 0, 0), sizes)  3.39 us
    ppermute x2, starting transfers between devices, local(): near = lax.ppermute(near, both, near_pairs)  3 us
  transfers between devices with their start and end apart: 22, of which 8 were waited for; matrix products, arithmetic and copies ran while one was open for 6% of the time, Pallas kernels for 26%

profile of v2, /device:TPU:0, one launch (start us, length us, event | category | flops | bytes accessed | tf_op | source)
XLA Modules:
  0.0 69.1 jit_solution(4824111866801111113)
XLA Ops:
  0.7 1.3 %dynamic-slice_bitcast_fusion.4 = (bf16[64,1536]{1,0:T(8,128)(2,1)S(1)}, bf16[64,1536]{1,0:T(8,128)(2,1)S(1)}, bf16[64,1536]{1,0:T(8,128)(2,1)S(1)}, bf16[64,1536]{1,0:T(8,128)(2,1)S(1)}) fusion(bf16[2,1,4,8,8,1536]{5,4,3,2,1,0:T(8,128)(2,1)} %param.10, s32[]{:T(128)S(6)} %select_n.36, s32[]{:T(128)S(6)} %select_n.35, s32[]{:T(128)S(6)} %select_n.34, ...), kind=kLoop, calls=%fused_computation.4 | loop fusion | bytes 1572880 | tf_op jit(solution)/shard_map/reshape | solution.py:401
  2.1 3.0 %collective-permute-start.5 = (bf16[64,1536]{1,0:T(8,128)(2,1)S(1)}, bf16[64,1536]{1,0:T(8,128)(2,1)S(1)}, u32[]{:S(2)}, u32[]{:S(2)}) collective-permute-start(bf16[64,1536]{1,0:T(8,128)(2,1)S(1)} %get-tuple-element.63), channel_id=1, source_target_pairs={{0,1},{1,0},{2,3},{3,2},{4,5},{5,4},{6,7},{7,6},{8,9},{9,8},{10,11... | collective-permute-start | bytes 589832 | tf_op jit(solution)/shard_map/ppermute | solution.py:394
  5.1 1.5 %collective-permute-start.6 = (bf16[64,1536]{1,0:T(8,128)(2,1)S(1)}, bf16[64,1536]{1,0:T(8,128)(2,1)S(1)}, u32[]{:S(2)}, u32[]{:S(2)}) collective-permute-start(bf16[64,1536]{1,0:T(8,128)(2,1)S(1)} %get-tuple-element.64), channel_id=1, source_target_pairs={{0,2},{1,3},{2,0},{3,1},{4,6},{5,7},{6,4},{7,5},{8,10},{9,11},{10,... | collective-permute-start | bytes 589832 | tf_op jit(solution)/shard_map/ppermute | solution.py:394
  6.6 2.0 %dynamic-slice_bitcast_fusion = (bf16[64,1536]{1,0:T(8,128)(2,1)}, bf16[64,1536]{1,0:T(8,128)(2,1)}, bf16[64,1536]{1,0:T(8,128)(2,1)}, bf16[64,1536]{1,0:T(8,128)(2,1)S(1)}) fusion(bf16[2,1,4,8,8,1536]{5,4,3,2,1,0:T(8,128)(2,1)} %param.10, s32[]{:T(128)S(6)} %select_n.36, s32[]{:T(128)S(6)} %select_n.35, s32[]{:T(128)S(6)} %select_n.34, s32[]{:T(128)S(6)} %select_n.33), kind=kLoop, calls=%fused_computation | loop fusion | bytes 1572880 | tf_op jit(solution)/shard_map/reshape | solution.py:401
  8.7 1.9 %collective-permute-start = (bf16[64,1536]{1,0:T(8,128)(2,1)}, bf16[64,1536]{1,0:T(8,128)(2,1)S(1)}, u32[]{:S(2)}, u32[]{:S(2)}) collective-permute-start(bf16[64,1536]{1,0:T(8,128)(2,1)} %get-tuple-element.53), channel_id=1, source_target_pairs={{0,1},{1,0},{2,3},{3,2},{4,5},{5,4},{6,7},{7,6},{8,9},{9,8},{10,11... | collective-permute-start | bytes 589832 | tf_op jit(solution)/shard_map/ppermute | solution.py:394
  10.6 1.5 %collective-permute-start.1 = (bf16[64,1536]{1,0:T(8,128)(2,1)}, bf16[64,1536]{1,0:T(8,128)(2,1)S(1)}, u32[]{:S(2)}, u32[]{:S(2)}) collective-permute-start(bf16[64,1536]{1,0:T(8,128)(2,1)} %get-tuple-element.54), channel_id=1, source_target_pairs={{0,2},{1,3},{2,0},{3,1},{4,6},{5,7},{6,4},{7,5},{8,10},{9,11},{10,... | collective-permute-start | bytes 589832 | tf_op jit(solution)/shard_map/ppermute | solution.py:394
  14.0 2.0 %collective-permute-done.6.rest_2_ = bf16[64,1536]{1,0:T(8,128)(2,1)S(1)} collective-permute-done((bf16[64,1536]{1,0:T(8,128)(2,1)S(1)}, bf16[64,1536]{1,0:T(8,128)(2,1)S(1)}, u32[]{:S(2)}, u32[]{:S(2)}) %collective-permute-start.6) | collective-permute-done | bytes 196640 | tf_op jit(solution)/shard_map/ppermute | solution.py:394
  16.6 1.2 %combine.3 = (bf16[64,1536]{1,0:T(8,128)(2,1)S(1)}, bf16[48,1536]{1,0:T(8,128)(2,1)S(1)}, bf16[48,1536]{1,0:T(8,128)(2,1)S(1)}, f32[64,1536]{1,0:T(8,128)S(1)}, ...) custom-call(s32[3]{0:T(128)S(1)} %pad_add_fusion.place_ref, bf16[64,1536]{1,0:T(8,128)(2,1)S(1)} %get-tuple-element.62.rest_0_, ...), custom_call_target="tpu_custom_call" | custom-call | flops 1500000000 | tf_op jit(solution)/shard_map/combine/pallas_call | solution.py:217
  17.8 0.7 %copy-done.4 = bf16[2,64,1536]{2,1,0:T(8,128)(2,1)} copy-done((bf16[2,64,1536]{2,1,0:T(8,128)(2,1)}, bf16[2,64,1536]{2,1,0:T(8,128)(2,1)S(1)}, u32[]{:S(2)}) %copy-start.4) | copy-done | bytes 393240
  18.5 1.5 %collective-permute-start.8 = (bf16[48,1536]{1,0:T(8,128)(2,1)S(1)}, bf16[48,1536]{1,0:T(8,128)(2,1)S(1)}, u32[]{:S(2)}, u32[]{:S(2)}) collective-permute-start(bf16[48,1536]{1,0:T(8,128)(2,1)S(1)} %get-tuple-element.67), channel_id=1, source_target_pairs={{0,1},{1,0},{2,3},{3,2},{4,5},{5,4},{6,7},{7,6},{8,9},{9,8},{10,11... | collective-permute-start | bytes 442376 | tf_op jit(solution)/shard_map/ppermute | solution.py:418
  20.0 0.7 collective-permute-start.9
  20.9 2.4 %collective-permute-done.1.rest_2_ = bf16[64,1536]{1,0:T(8,128)(2,1)S(1)} collective-permute-done((bf16[64,1536]{1,0:T(8,128)(2,1)}, bf16[64,1536]{1,0:T(8,128)(2,1)S(1)}, u32[]{:S(2)}, u32[]{:S(2)}) %collective-permute-start.1) | collective-permute-done | bytes 196640 | tf_op jit(solution)/shard_map/ppermute | solution.py:394
  23.2 1.8 %collective-permute-done.2.rest_3_ = bf16[64,1536]{1,0:T(8,128)(2,1)S(1)} collective-permute-done((bf16[64,1536]{1,0:T(8,128)(2,1)}, bf16[64,1536]{1,0:T(8,128)(2,1)S(1)}, u32[]{:S(2)}, u32[]{:S(2)}) %collective-permute-start.2) | collective-permute-done | bytes 196640 | tf_op jit(solution)/shard_map/ppermute | solution.py:394
  25.0 1.2 %combine.2 = (bf16[64,1536]{1,0:T(8,128)(2,1)S(1)}, bf16[48,1536]{1,0:T(8,128)(2,1)S(1)}, bf16[48,1536]{1,0:T(8,128)(2,1)S(1)}, f32[64,1536]{1,0:T(8,128)S(1)}, ...) custom-call(s32[3]{0:T(128)S(1)} %pad_add_fusion.place_ref, bf16[64,1536]{1,0:T(8,128)(2,1)S(1)} %get-tuple-element.52.rest_0_, ...), custom_call_target="tpu_custom_call" | custom-call | flops 1500000000 | tf_op jit(solution)/shard_map/combine/pallas_call | solution.py:217
  26.3 1.5 %collective-permute-start.3 = (bf16[48,1536]{1,0:T(8,128)(2,1)S(1)}, bf16[48,1536]{1,0:T(8,128)(2,1)S(1)}, u32[]{:S(2)}, u32[]{:S(2)}) collective-permute-start(bf16[48,1536]{1,0:T(8,128)(2,1)S(1)} %get-tuple-element.57), channel_id=1, source_target_pairs={{0,1},{1,0},{2,3},{3,2},{4,5},{5,4},{6,7},{7,6},{8,9},{9,8},{10,11... | collective-permute-start | bytes 442376 | tf_op jit(solution)/shard_map/ppermute | solution.py:418
  27.8 0.8 %collective-permute-start.4 = (bf16[48,1536]{1,0:T(8,128)(2,1)S(1)}, bf16[48,1536]{1,0:T(8,128)(2,1)S(1)}, u32[]{:S(2)}, u32[]{:S(2)}) collective-permute-start(bf16[48,1536]{1,0:T(8,128)(2,1)S(1)} %get-tuple-element.58), channel_id=1, source_target_pairs={{0,31},{1,2},{2,1},{3,4},{4,3},{5,6},{6,5},{7,8},{8,7},{9,10},{10,... | collective-permute-start | bytes 442376 | tf_op jit(solution)/shard_map/ppermute | solution.py:419
  28.7 7.0 %conv.2 = (bf16[2,64,1536]{2,1,0:T(8,128)(2,1)}, f32[2,64,2]{2,1,0:T(8,128)S(1)}, f32[4,32,384]{2,1,0:T(8,128)S(1)}, bf16[64,1536]{1,0:T(8,128)(2,1)S(1)}, bf16[...) custom-call(s32[3]{0:T(128)S(1)} %pad_add_fusion.place_ref, ...), custom_call_target="tpu_custom_call" | custom-call | flops 8000000000 | tf_op jit(solution)/shard_map/conv/pallas_call | solution.py:280
  35.7 4.2 %collective-permute-start.10 = (bf16[64,1536]{1,0:T(8,128)(2,1)S(1)}, bf16[64,1536]{1,0:T(8,128)(2,1)S(1)}, u32[]{:S(2)}, u32[]{:S(2)}) collective-permute-start(bf16[64,1536]{1,0:T(8,128)(2,1)S(1)} %get-tuple-element.77), channel_id=1, source_target_pairs={{0,1},{1,0},{2,3},{3,2},{4,5},{5,4},{6,7},{7,6},{8,9},{9,8},{10,11... | collective-permute-start | bytes 589832 | tf_op jit(solution)/shard_map/ppermute | solution.py:394
  39.8 1.5 %collective-permute-start.12 = (bf16[64,1536]{1,0:T(8,128)(2,1)S(1)}, bf16[64,1536]{1,0:T(8,128)(2,1)S(1)}, u32[]{:S(2)}, u32[]{:S(2)}) collective-permute-start(bf16[64,1536]{1,0:T(8,128)(2,1)S(1)} %get-tuple-element.79), channel_id=1, source_target_pairs={{0,3},{1,2},{2,1},{3,0},{4,7},{5,6},{6,5},{7,4},{8,11},{9,10},{10,... | collective-permute-start | bytes 589832 | tf_op jit(solution)/shard_map/ppermute | solution.py:394
  41.3 7.3 %conv.3 = (bf16[2,64,1536]{2,1,0:T(8,128)(2,1)}, f32[2,64,2]{2,1,0:T(8,128)S(1)}, f32[4,32,384]{2,1,0:T(8,128)S(1)}, bf16[64,1536]{1,0:T(8,128)(2,1)S(1)}, bf16[...) custom-call(s32[3]{0:T(128)S(1)} %pad_add_fusion.place_ref, ...), custom_call_target="tpu_custom_call", output_to_operand_aliasing={{0}: (14, {}), {1}: (15, {})} | custom-call | flops 8000000000 | tf_op jit(solution)/shard_map/conv/pallas_call | solution.py:280
  48.6 2.1 %collective-permute-start.16 = (f32[32,384]{1,0:T(8,128)S(1)}, f32[32,384]{1,0:T(8,128)S(1)}, u32[]{:S(2)}, u32[]{:S(2)}) collective-permute-start(f32[32,384]{1,0:T(8,128)S(1)} %get-tuple-element.120), channel_id=1, source_target_pairs={{0,1},{1,0},{2,3},{3,2},{4,5},{5,4},{6,7},{7,6},{8,9},{9,8},{10,11... | collective-permute-start | bytes 147464 | tf_op jit(solution)/shard_map/ppermute | solution.py:394
  50.7 1.5 %collective-permute-start.17 = (f32[32,384]{1,0:T(8,128)S(1)}, f32[32,384]{1,0:T(8,128)S(1)}, u32[]{:S(2)}, u32[]{:S(2)}) collective-permute-start(f32[32,384]{1,0:T(8,128)S(1)} %get-tuple-element.122), channel_id=1, source_target_pairs={{0,2},{1,3},{2,0},{3,1},{4,6},{5,7},{6,4},{7,5},{8,10},{9,11},{10,... | collective-permute-start | bytes 147464 | tf_op jit(solution)/shard_map/ppermute | solution.py:394
  52.2 1.9 %collective-permute-start.13 = (bf16[64,1536]{1,0:T(8,128)(2,1)S(1)}, bf16[64,1536]{1,0:T(8,128)(2,1)S(1)}, u32[]{:S(2)}, u32[]{:S(2)}) collective-permute-start(bf16[64,1536]{1,0:T(8,128)(2,1)S(1)} %get-tuple-element.85), channel_id=1, source_target_pairs={{0,1},{1,0},{2,3},{3,2},{4,5},{5,4},{6,7},{7,6},{8,9},{9,8},{10,11... | collective-permute-start | bytes 589832 | tf_op jit(solution)/shard_map/ppermute | solution.py:394
  54.3 1.5 %collective-permute-start.15 = (bf16[64,1536]{1,0:T(8,128)(2,1)S(1)}, bf16[64,1536]{1,0:T(8,128)(2,1)S(1)}, u32[]{:S(2)}, u32[]{:S(2)}) collective-permute-start(bf16[64,1536]{1,0:T(8,128)(2,1)S(1)} %get-tuple-element.87), channel_id=1, source_target_pairs={{0,3},{1,2},{2,1},{3,0},{4,7},{5,6},{6,5},{7,4},{8,11},{9,10},{10,... | collective-permute-start | bytes 589832 | tf_op jit(solution)/shard_map/ppermute | solution.py:394
  56.4 1.2 %collective-permute-done.19 = f32[32,384]{1,0:T(8,128)S(1)} collective-permute-done((f32[32,384]{1,0:T(8,128)S(1)}, f32[32,384]{1,0:T(8,128)S(1)}, u32[]{:S(2)}, u32[]{:S(2)}) %collective-permute-start.19) | collective-permute-done | bytes 49184 | tf_op jit(solution)/shard_map/ppermute | solution.py:430
  57.6 1.7 %collective-permute-start.20 = (f32[32,384]{1,0:T(8,128)S(1)}, f32[32,384]{1,0:T(8,128)S(1)}, u32[]{:S(2)}, u32[]{:S(2)}) collective-permute-start(f32[32,384]{1,0:T(8,128)S(1)} %add.96), channel_id=1, source_target_pairs={{0,8},{4,12},{8,0},{12,4},{16,24},{20,28},{24,16},{28,20},{1,9},{5... | collective-permute-start | bytes 147464 | tf_op jit(solution)/shard_map/ppermute | solution.py:430
  59.3 0.7 copy.60
  60.0 1.8 %collective-permute-done.20 = f32[32,384]{1,0:T(8,128)S(1)} collective-permute-done((f32[32,384]{1,0:T(8,128)S(1)}, f32[32,384]{1,0:T(8,128)S(1)}, u32[]{:S(2)}, u32[]{:S(2)}) %collective-permute-start.20) | collective-permute-done | bytes 49184 | tf_op jit(solution)/shard_map/ppermute | solution.py:430
  61.8 2.7 %collective-permute-start.21 = (f32[32,384]{1,0:T(8,128)S(1)}, f32[32,384]{1,0:T(8,128)S(1)}, u32[]{:S(2)}, u32[]{:S(2)}) collective-permute-start(f32[32,384]{1,0:T(8,128)S(1)} %add.97.refs_4_), channel_id=1, source_target_pairs={{0,16},{4,20},{8,24},{12,28},{16,0},{20,4},{24,8},{28,12},{1,17},{... | collective-permute-start | bytes 147464 | tf_op jit(solution)/shard_map/ppermute | solution.py:430
  64.5 1.4 %finish.2.refs_6_ = bf16[2,4,64,1536]{3,2,1,0:T(8,128)(2,1)} custom-call(s32[3]{0:T(128)S(1)} %pad_add_fusion.place_ref, bf16[64,1536]{1,0:T(8,128)(2,1)S(1)} %get-tuple-element.89.refs_0_, bf16[64,1536]{1,0:T(8,128)(2,1)S(1)} %collective-permute-done.10.refs_1_, bf16[64,1536]{1,0:T(8,128)(2,1)S(1)} %collective-permute-done.11.refs_2_, ...), custom_call_target="tpu_custom_call" | custom-call | flops 1000000000 | tf_op jit(solution)/shard_map/finish/pallas_call | solution.py:356
  65.9 0.9 %collective-permute-done.21.refs_5_ = f32[32,384]{1,0:T(8,128)S(1)} collective-permute-done((f32[32,384]{1,0:T(8,128)S(1)}, f32[32,384]{1,0:T(8,128)S(1)}, u32[]{:S(2)}, u32[]{:S(2)}) %collective-permute-start.21) | collective-permute-done | bytes 49184 | tf_op jit(solution)/shard_map/ppermute | solution.py:430
  66.8 2.1 %finish.3 = (bf16[2,4,64,1536]{3,2,1,0:T(8,128)(2,1)}, f32[31,384]{1,0:T(8,128)}, f32[384]{0:T(512)}) custom-call(s32[3]{0:T(128)S(1)} %pad_add_fusion.place_ref, bf16[64,1536]{1,0:T(8,128)(2,1)S(1)} %get-tuple-element.84.refs_0_, bf16[64,1536]{1,0:T(8,128)(2,1)S(1)} %collective-permute-done.13.refs_1_, ...), custom_call_target="tpu_custom_call", output_to_operand_aliasing={{0}: (7, {})} | custom-call | flops 1000000000 | tf_op jit(solution)/shard_map/finish/pallas_call | solution.py:356
  (63 shorter events, 3.3 us)
Async XLA Ops:
  0.7 11.5 %copy-start.7 = (s32[2,64,2]{1,2,0:T(2,128)S(1)}, s32[2,64,2]{1,2,0:T(2,128)}, u32[]{:S(2)}) copy-start(s32[2,64,2]{1,2,0:T(2,128)} %param.11) | copy-start | bytes 3076
  0.7 11.6 %copy-start.9 = (s32[2,1,64]{2,1,0:T(1,128)S(1)}, s32[2,1,64]{2,1,0:T(1,128)}, u32[]{:S(2)}) copy-start(s32[2,1,64]{2,1,0:T(1,128)} %param.12) | copy-start | bytes 1540
  0.7 13.2 %copy-start.6 = (f32[1536]{0:T(1024)S(1)}, f32[1536]{0:T(1024)}, u32[]{:S(2)}) copy-start(f32[1536]{0:T(1024)} %param.15) | copy-start | bytes 18436
  0.7 13.2 %copy-start.8 = (f32[2,64,2]{1,2,0:T(2,128)S(1)}, f32[2,64,2]{1,2,0:T(2,128)}, u32[]{:S(2)}) copy-start(f32[2,64,2]{1,2,0:T(2,128)} %param.13) | copy-start | bytes 3076
  0.7 15.9 %copy-start = (bf16[2,64,1536]{2,1,0:T(8,128)(2,1)S(1)}, bf16[2,64,1536]{2,1,0:T(8,128)(2,1)}, u32[]{:S(2)}) copy-start(bf16[2,64,1536]{2,1,0:T(8,128)(2,1)} %rest_4_.3) | copy-start | bytes 1179652
  0.7 15.9 %copy-start.1 = (bf16[2,64,1536]{2,1,0:T(8,128)(2,1)S(1)}, bf16[2,64,1536]{2,1,0:T(8,128)(2,1)}, u32[]{:S(2)}) copy-start(bf16[2,64,1536]{2,1,0:T(8,128)(2,1)} %grad_out_ref.3) | copy-start | bytes 1179652
  2.1 11.3 %collective-permute-start.5 = (bf16[64,1536]{1,0:T(8,128)(2,1)S(1)}, bf16[64,1536]{1,0:T(8,128)(2,1)S(1)}, u32[]{:S(2)}, u32[]{:S(2)}) collective-permute-start(bf16[64,1536]{1,0:T(8,128)(2,1)S(1)} %get-tuple-element.63), channel_id=1, source_target_pairs={{0,1},{1,0},{2,3},{3,2},{4,5},{5,4},{6,7},{7,6},{8,9},{9,8},{10,11... | collective-permute-start | bytes 589832 | tf_op jit(solution)/shard_map/ppermute | solution.py:394
  5.1 11.0 %collective-permute-start.6 = (bf16[64,1536]{1,0:T(8,128)(2,1)S(1)}, bf16[64,1536]{1,0:T(8,128)(2,1)S(1)}, u32[]{:S(2)}, u32[]{:S(2)}) collective-permute-start(bf16[64,1536]{1,0:T(8,128)(2,1)S(1)} %get-tuple-element.64), channel_id=1, source_target_pairs={{0,2},{1,3},{2,0},{3,1},{4,6},{5,7},{6,4},{7,5},{8,10},{9,11},{10,... | collective-permute-start | bytes 589832 | tf_op jit(solution)/shard_map/ppermute | solution.py:394
  6.6 10.0 %collective-permute-start.7 = (bf16[64,1536]{1,0:T(8,128)(2,1)S(1)}, bf16[64,1536]{1,0:T(8,128)(2,1)S(1)}, u32[]{:S(2)}, u32[]{:S(2)}) collective-permute-start(bf16[64,1536]{1,0:T(8,128)(2,1)S(1)} %get-tuple-element.65), channel_id=1, source_target_pairs={{0,3},{1,2},{2,1},{3,0},{4,7},{5,6},{6,5},{7,4},{8,11},{9,10},{10,... | collective-permute-start | bytes 589832 | tf_op jit(solution)/shard_map/ppermute | solution.py:394
  8.7 12.2 %collective-permute-start = (bf16[64,1536]{1,0:T(8,128)(2,1)}, bf16[64,1536]{1,0:T(8,128)(2,1)S(1)}, u32[]{:S(2)}, u32[]{:S(2)}) collective-permute-start(bf16[64,1536]{1,0:T(8,128)(2,1)} %get-tuple-element.53), channel_id=1, source_target_pairs={{0,1},{1,0},{2,3},{3,2},{4,5},{5,4},{6,7},{7,6},{8,9},{9,8},{10,11... | collective-permute-start | bytes 589832 | tf_op jit(solution)/shard_map/ppermute | solution.py:394
  10.6 12.6 %collective-permute-start.1 = (bf16[64,1536]{1,0:T(8,128)(2,1)}, bf16[64,1536]{1,0:T(8,128)(2,1)S(1)}, u32[]{:S(2)}, u32[]{:S(2)}) collective-permute-start(bf16[64,1536]{1,0:T(8,128)(2,1)} %get-tuple-element.54), channel_id=1, source_target_pairs={{0,2},{1,3},{2,0},{3,1},{4,6},{5,7},{6,4},{7,5},{8,10},{9,11},{10,... | collective-permute-start | bytes 589832 | tf_op jit(solution)/shard_map/ppermute | solution.py:394
  13.4 11.7 %collective-permute-start.2 = (bf16[64,1536]{1,0:T(8,128)(2,1)}, bf16[64,1536]{1,0:T(8,128)(2,1)S(1)}, u32[]{:S(2)}, u32[]{:S(2)}) collective-permute-start(bf16[64,1536]{1,0:T(8,128)(2,1)} %get-tuple-element.55), channel_id=1, source_target_pairs={{0,3},{1,2},{2,1},{3,0},{4,7},{5,6},{6,5},{7,4},{8,11},{9,10},{10,... | collective-permute-start | bytes 589832 | tf_op jit(solution)/shard_map/ppermute | solution.py:394
  17.8 0.7 %copy-start.4 = (bf16[2,64,1536]{2,1,0:T(8,128)(2,1)}, bf16[2,64,1536]{2,1,0:T(8,128)(2,1)S(1)}, u32[]{:S(2)}) copy-start(bf16[2,64,1536]{2,1,0:T(8,128)(2,1)S(1)} %get-tuple-element.71.picked_ref) | copy-start | bytes 1179652
  18.5 10.1 %collective-permute-start.8 = (bf16[48,1536]{1,0:T(8,128)(2,1)S(1)}, bf16[48,1536]{1,0:T(8,128)(2,1)S(1)}, u32[]{:S(2)}, u32[]{:S(2)}) collective-permute-start(bf16[48,1536]{1,0:T(8,128)(2,1)S(1)} %get-tuple-element.67), channel_id=1, source_target_pairs={{0,1},{1,0},{2,3},{3,2},{4,5},{5,4},{6,7},{7,6},{8,9},{9,8},{10,11... | collective-permute-start | bytes 442376 | tf_op jit(solution)/shard_map/ppermute | solution.py:418
  20.0 8.6 %collective-permute-start.9 = (bf16[48,1536]{1,0:T(8,128)(2,1)S(1)}, bf16[48,1536]{1,0:T(8,128)(2,1)S(1)}, u32[]{:S(2)}, u32[]{:S(2)}) collective-permute-start(bf16[48,1536]{1,0:T(8,128)(2,1)S(1)} %get-tuple-element.68), channel_id=1, source_target_pairs={{0,31},{1,2},{2,1},{3,4},{4,3},{5,6},{6,5},{7,8},{8,7},{9,10},{10,... | collective-permute-start | bytes 442376 | tf_op jit(solution)/shard_map/ppermute | solution.py:419
  20.9 7.8 %copy-start.2 = (f32[31,1536]{1,0:T(8,128)S(1)}, f32[31,1536]{1,0:T(8,128)}, u32[]{:S(2)}) copy-start(f32[31,1536]{1,0:T(8,128)} %kernel_ref.3) | copy-start | bytes 571396
  20.9 7.8 %copy-start.3 = (s32[2,8]{1,0:T(2,128)S(1)}, s32[2,8]{1,0:T(2,128)}, u32[]{:S(2)}) copy-start(s32[2,8]{1,0:T(2,128)} %lengths_ref.3) | copy-start | bytes 196
  20.9 7.8 %copy-start.5 = (bf16[2,64,1536]{2,1,0:T(8,128)(2,1)S(1)}, bf16[2,64,1536]{2,1,0:T(8,128)(2,1)}, u32[]{:S(2)}) copy-start(bf16[2,64,1536]{2,1,0:T(8,128)(2,1)} %copy-done.4) | copy-start | bytes 1179652
  26.3 15.0 %collective-permute-start.3 = (bf16[48,1536]{1,0:T(8,128)(2,1)S(1)}, bf16[48,1536]{1,0:T(8,128)(2,1)S(1)}, u32[]{:S(2)}, u32[]{:S(2)}) collective-permute-start(bf16[48,1536]{1,0:T(8,128)(2,1)S(1)} %get-tuple-element.57), channel_id=1, source_target_pairs={{0,1},{1,0},{2,3},{3,2},{4,5},{5,4},{6,7},{7,6},{8,9},{9,8},{10,11... | collective-permute-start | bytes 442376 | tf_op jit(solution)/shard_map/ppermute | solution.py:418
  27.8 13.5 %collective-permute-start.4 = (bf16[48,1536]{1,0:T(8,128)(2,1)S(1)}, bf16[48,1536]{1,0:T(8,128)(2,1)S(1)}, u32[]{:S(2)}, u32[]{:S(2)}) collective-permute-start(bf16[48,1536]{1,0:T(8,128)(2,1)S(1)} %get-tuple-element.58), channel_id=1, source_target_pairs={{0,31},{1,2},{2,1},{3,4},{4,3},{5,6},{6,5},{7,8},{8,7},{9,10},{10,... | collective-permute-start | bytes 442376 | tf_op jit(solution)/shard_map/ppermute | solution.py:419
  35.7 15.1 %collective-permute-start.10 = (bf16[64,1536]{1,0:T(8,128)(2,1)S(1)}, bf16[64,1536]{1,0:T(8,128)(2,1)S(1)}, u32[]{:S(2)}, u32[]{:S(2)}) collective-permute-start(bf16[64,1536]{1,0:T(8,128)(2,1)S(1)} %get-tuple-element.77), channel_id=1, source_target_pairs={{0,1},{1,0},{2,3},{3,2},{4,5},{5,4},{6,7},{7,6},{8,9},{9,8},{10,11... | collective-permute-start | bytes 589832 | tf_op jit(solution)/shard_map/ppermute | solution.py:394
  39.8 12.4 %collective-permute-start.11 = (bf16[64,1536]{1,0:T(8,128)(2,1)S(1)}, bf16[64,1536]{1,0:T(8,128)(2,1)S(1)}, u32[]{:S(2)}, u32[]{:S(2)}) collective-permute-start(bf16[64,1536]{1,0:T(8,128)(2,1)S(1)} %get-tuple-element.78), channel_id=1, source_target_pairs={{0,2},{1,3},{2,0},{3,1},{4,6},{5,7},{6,4},{7,5},{8,10},{9,11},{10,... | collective-permute-start | bytes 589832 | tf_op jit(solution)/shard_map/ppermute | solution.py:394
  39.8 12.4 %collective-permute-start.12 = (bf16[64,1536]{1,0:T(8,128)(2,1)S(1)}, bf16[64,1536]{1,0:T(8,128)(2,1)S(1)}, u32[]{:S(2)}, u32[]{:S(2)}) collective-permute-start(bf16[64,1536]{1,0:T(8,128)(2,1)S(1)} %get-tuple-element.79), channel_id=1, source_target_pairs={{0,3},{1,2},{2,1},{3,0},{4,7},{5,6},{6,5},{7,4},{8,11},{9,10},{10,... | collective-permute-start | bytes 589832 | tf_op jit(solution)/shard_map/ppermute | solution.py:394
  48.6 5.7 %collective-permute-start.16 = (f32[32,384]{1,0:T(8,128)S(1)}, f32[32,384]{1,0:T(8,128)S(1)}, u32[]{:S(2)}, u32[]{:S(2)}) collective-permute-start(f32[32,384]{1,0:T(8,128)S(1)} %get-tuple-element.120), channel_id=1, source_target_pairs={{0,1},{1,0},{2,3},{3,2},{4,5},{5,4},{6,7},{7,6},{8,9},{9,8},{10,11... | collective-permute-start | bytes 147464 | tf_op jit(solution)/shard_map/ppermute | solution.py:394
  50.7 5.6 %collective-permute-start.18 = (f32[32,384]{1,0:T(8,128)S(1)}, f32[32,384]{1,0:T(8,128)S(1)}, u32[]{:S(2)}, u32[]{:S(2)}) collective-permute-start(f32[32,384]{1,0:T(8,128)S(1)} %get-tuple-element.121), channel_id=1, source_target_pairs={{0,3},{1,2},{2,1},{3,0},{4,7},{5,6},{6,5},{7,4},{8,11},{9,10},{10,... | collective-permute-start | bytes 147464 | tf_op jit(solution)/shard_map/ppermute | solution.py:394
  50.7 5.6 %collective-permute-start.17 = (f32[32,384]{1,0:T(8,128)S(1)}, f32[32,384]{1,0:T(8,128)S(1)}, u32[]{:S(2)}, u32[]{:S(2)}) collective-permute-start(f32[32,384]{1,0:T(8,128)S(1)} %get-tuple-element.122), channel_id=1, source_target_pairs={{0,2},{1,3},{2,0},{3,1},{4,6},{5,7},{6,4},{7,5},{8,10},{9,11},{10,... | collective-permute-start | bytes 147464 | tf_op jit(solution)/shard_map/ppermute | solution.py:394
  52.2 14.6 %collective-permute-start.13 = (bf16[64,1536]{1,0:T(8,128)(2,1)S(1)}, bf16[64,1536]{1,0:T(8,128)(2,1)S(1)}, u32[]{:S(2)}, u32[]{:S(2)}) collective-permute-start(bf16[64,1536]{1,0:T(8,128)(2,1)S(1)} %get-tuple-element.85), channel_id=1, source_target_pairs={{0,1},{1,0},{2,3},{3,2},{4,5},{5,4},{6,7},{7,6},{8,9},{9,8},{10,11... | collective-permute-start | bytes 589832 | tf_op jit(solution)/shard_map/ppermute | solution.py:394
  54.2 12.6 %collective-permute-start.14 = (bf16[64,1536]{1,0:T(8,128)(2,1)S(1)}, bf16[64,1536]{1,0:T(8,128)(2,1)S(1)}, u32[]{:S(2)}, u32[]{:S(2)}) collective-permute-start(bf16[64,1536]{1,0:T(8,128)(2,1)S(1)} %get-tuple-element.86), channel_id=1, source_target_pairs={{0,2},{1,3},{2,0},{3,1},{4,6},{5,7},{6,4},{7,5},{8,10},{9,11},{10,... | collective-permute-start | bytes 589832 | tf_op jit(solution)/shard_map/ppermute | solution.py:394
  54.3 12.6 %collective-permute-start.15 = (bf16[64,1536]{1,0:T(8,128)(2,1)S(1)}, bf16[64,1536]{1,0:T(8,128)(2,1)S(1)}, u32[]{:S(2)}, u32[]{:S(2)}) collective-permute-start(bf16[64,1536]{1,0:T(8,128)(2,1)S(1)} %get-tuple-element.87), channel_id=1, source_target_pairs={{0,3},{1,2},{2,1},{3,0},{4,7},{5,6},{6,5},{7,4},{8,11},{9,10},{10,... | collective-permute-start | bytes 589832 | tf_op jit(solution)/shard_map/ppermute | solution.py:394
  56.3 1.3 %collective-permute-start.19 = (f32[32,384]{1,0:T(8,128)S(1)}, f32[32,384]{1,0:T(8,128)S(1)}, u32[]{:S(2)}, u32[]{:S(2)}) collective-permute-start(f32[32,384]{1,0:T(8,128)S(1)} %fusion.10), channel_id=1, source_target_pairs={{0,4},{4,0},{8,12},{12,8},{16,20},{20,16},{24,28},{28,24},{1,5},{5... | collective-permute-start | bytes 147464 | tf_op jit(solution)/shard_map/ppermute | solution.py:430
  57.6 4.2 %collective-permute-start.20 = (f32[32,384]{1,0:T(8,128)S(1)}, f32[32,384]{1,0:T(8,128)S(1)}, u32[]{:S(2)}, u32[]{:S(2)}) collective-permute-start(f32[32,384]{1,0:T(8,128)S(1)} %add.96), channel_id=1, source_target_pairs={{0,8},{4,12},{8,0},{12,4},{16,24},{20,28},{24,16},{28,20},{1,9},{5... | collective-permute-start | bytes 147464 | tf_op jit(solution)/shard_map/ppermute | solution.py:430
  61.8 5.1 %collective-permute-start.21 = (f32[32,384]{1,0:T(8,128)S(1)}, f32[32,384]{1,0:T(8,128)S(1)}, u32[]{:S(2)}, u32[]{:S(2)}) collective-permute-start(f32[32,384]{1,0:T(8,128)S(1)} %add.97.refs_4_), channel_id=1, source_target_pairs={{0,16},{4,20},{8,24},{12,28},{16,0},{20,4},{24,8},{28,12},{1,17},{... | collective-permute-start | bytes 147464 | tf_op jit(solution)/shard_map/ppermute | solution.py:430

commit v3 on v2

--- a/solution.py
+++ b/solution.py
@@ -312,14 +312,9 @@
     )(*operands)
 
 
-def finish_kernel(group_count, micro, part_count, place_ref, *refs):
+def finish_kernel(group_count, micro, place_ref, *refs):
     blocks = refs[:group_count]
-    parts = refs[group_count : group_count + part_count]
-    rest = refs[group_count + part_count :]
-    if part_count:
-        _, out_ref, taps_ref, gain_ref, sems = rest
-    else:
-        out_ref, sems = rest
+    out_ref, sems = refs[-2:]
     me = place_ref[2]
     copies = [
         pltpu.make_async_copy(block, out_ref.at[micro, jnp.bitwise_xor(me, step)], sems.at[step])
@@ -327,47 +322,53 @@
     ]
     for copy in copies:
         copy.start()
-    if part_count:
-        total = parts[0][...]
-        for part in parts[1:]:
-            total = total + part[...]
-        taps_ref[...] = total[:KW]
-        gain_ref[...] = total[KW]
     for copy in copies:
         copy.wait()
 
 
-def finish(micro, micro_count, place, blocks, parts=(), earlier=None):
+def finish(micro, micro_count, place, blocks, earlier=None):
     group_count = len(blocks)
     slots, width = blocks[0].shape
     anywhere = pl.BlockSpec(memory_space=pl.ANY)
-    out_shape = [jax.ShapeDtypeStruct((micro_count, group_count, slots, width), BF16)]
-    out_specs = [anywhere]
-    in_specs = [anywhere] * group_count + [whole(p.shape) for p in parts]
-    operands = [place, *blocks, *parts]
+    operands = [place, *blocks]
     aliases = {}
     if earlier is not None:
         aliases = {len(operands): 0}
         operands.append(earlier)
-        in_specs.append(anywhere)
-        share = parts[0].shape[1]
-        out_shape += [jax.ShapeDtypeStruct((KW, share), F32), jax.ShapeDtypeStruct((share,), F32)]
-        out_specs += [whole((KW, share)), whole((share,))]
     return pl.pallas_call(
-        functools.partial(finish_kernel, group_count, micro, len(parts)),
-        grid_spec=pltpu.PrefetchScalarGridSpec(
-            num_scalar_prefetch=1,
-            grid=(1,),
-            in_specs=in_specs,
-            out_specs=out_specs,
-            scratch_shapes=[pltpu.SemaphoreType.DMA((group_count,))],
-        ),
-        out_shape=out_shape,
+        functools.partial(finish_kernel, group_count, micro),
+        in_specs=[pl.BlockSpec(memory_space=pltpu.SMEM)] + [anywhere] * (len(operands) - 1),
+        out_specs=anywhere,
+        out_shape=jax.ShapeDtypeStruct((micro_count, group_count, slots, width), BF16),
+        scratch_shapes=[pltpu.SemaphoreType.DMA((group_count,))],
         input_output_aliases=aliases,
-        compiler_params=pltpu.CompilerParams(vmem_limit_bytes=4 * 1024 * 1024),
-        cost_estimate=pl.CostEstimate(flops=1000 * 10**6, bytes_accessed=0, transcendentals=0),
+        compiler_params=pltpu.CompilerParams(vmem_limit_bytes=SMALL_LIMIT),
+        cost_estimate=pl.CostEstimate(flops=1500 * 10**6, bytes_accessed=0, transcendentals=0),
         name="finish",
     )(*operands)
+
+
+def total_kernel(*refs):
+    parts = refs[:-2]
+    taps_ref, gain_ref = refs[-2:]
+    total = parts[0][...]
+    for part in parts[1:]:
+        total = total + part[...]
+    taps_ref[...] = total[:KW]
+    gain_ref[...] = total[KW]
+
+
+def total_of(parts):
+    share = parts[0].shape[1]
+    inside = pl.BlockSpec(memory_space=pltpu.VMEM)
+    return pl.pallas_call(
+        total_kernel,
+        in_specs=[inside] * len(parts),
+        out_specs=[inside, inside],
+        out_shape=[jax.ShapeDtypeStruct((KW, share), F32), jax.ShapeDtypeStruct((share,), F32)],
+        compiler_params=pltpu.CompilerParams(vmem_limit_bytes=SMALL_LIMIT),
+        name="total",
+    )(*parts)
 
 
 def take(cells, index):
@@ -423,6 +424,7 @@
         )
         earlier = (grad_x, grad_probs, terms)
         if returned:
+            returned[-1][:2], terms = lax.optimization_barrier((returned[-1][:2], terms))
             returned[-1], outs = lax.optimization_barrier((returned[-1], outs))
         returned.append([outs[0]] + [swap(outs[step], step) for step in range(1, groups)])
 
@@ -438,11 +440,9 @@
         step *= 2
     parts = [total] + over(total, [step])
     grad_expert = None
-    for micro in range(micro_count - 1):
-        (grad_expert,) = finish(micro, micro_count, place, returned[micro])
-    grad_expert, grad_kernel, grad_gain = finish(
-        micro_count - 1, micro_count, place, returned[-1], parts, grad_expert
-    )
+    for micro in range(micro_count):
+        grad_expert = finish(micro, micro_count, place, returned[micro], grad_expert)
+    grad_kernel, grad_gain = total_of(parts)
     grad_expert = grad_expert.reshape(micro_count, 1, groups, per, CAP, width)
     return grad_x, grad_expert, grad_probs, grad_kernel, grad_gain
 

time: 69.2 us -> 67.6 us (0.977)
  waiting for transfers between devices: 11.2 us -> 9.74 us
    ppermute x3, waiting for transfers between devices: 3.9 us -> 2.44 us  [over(): lax.ppermute(cells, 'tm', [(i, i ^ step) for i in range(tm)])]
    pallas_call x2 -> x3, Pallas kernels: 3.52 us -> 3.53 us  [the longest x2 2.9 us: finish(): pl.pallas_call(functools.partial(finish_kernel, group_count, micro), in_s...]
  transfers between devices with their start and end apart: 22 -> 22, of which waited for: 8 -> 8; matrix products, arithmetic and copies ran while one was open for 6% -> 6% of each run, Pallas kernels for 26% -> 29%
where the time goes in v3:
time: 67.6 us; the launch traced here: 67.5 us
  starting transfers between devices  30.2 us (45%)
  Pallas kernels  20.2 us (30%)
  waiting for transfers between devices  9.74 us (14%)
  local copies, waits for them, and re-layouts  5.99 us (9%)
  between operations  0.92 us (1%)
    ppermute x15, starting transfers between devices, swap(): return lax.ppermute(cells, 'expert', [(i, i ^ step) for i in range(groups)])  21.2 us
    pallas_call x2, Pallas kernels, conv(): pl.pallas_call(functools.partial(conv_kernel, group_count, first, micro,...  14.3 us
    ppermute x15, waiting for transfers between devices, swap(): return lax.ppermute(cells, 'expert', [(i, i ^ step) for i in range(groups)])  7.3 us
    ppermute x3, starting transfers between devices, over(): lax.ppermute(cells, 'tm', [(i, i ^ step) for i in range(tm)])  4.47 us
    reshape x2, local copies, waits for them, and re-layouts, local(): lax.dynamic_slice(cells, (micro, 0, me ^ step, 0, 0, 0), sizes)  3.39 us
    ppermute x2, starting transfers between devices, local(): near = lax.ppermute(near, both, near_pairs)  3 us
    pallas_call x2, Pallas kernels, finish(): pl.pallas_call(functools.partial(finish_kernel, group_count, micro), in_s...  2.9 us
    ppermute x3, waiting for transfers between devices, over(): lax.ppermute(cells, 'tm', [(i, i ^ step) for i in range(tm)])  2.44 us
  transfers between devices with their start and end apart: 22, of which 8 were waited for; matrix products, arithmetic and copies ran while one was open for 6% of the time, Pallas kernels for 29%

profile of v3, /device:TPU:0, one launch (start us, length us, event | category | flops | bytes accessed | tf_op | source)
XLA Modules:
  0.0 67.5 jit_solution(3451633757847931948)
XLA Ops:
  0.7 1.3 %dynamic-slice_bitcast_fusion.4 = (bf16[64,1536]{1,0:T(8,128)(2,1)S(1)}, bf16[64,1536]{1,0:T(8,128)(2,1)S(1)}, bf16[64,1536]{1,0:T(8,128)(2,1)S(1)}, bf16[64,1536]{1,0:T(8,128)(2,1)S(1)}) fusion(bf16[2,1,4,8,8,1536]{5,4,3,2,1,0:T(8,128)(2,1)} %param.10, s32[]{:T(128)S(6)} %select_n.36, s32[]{:T(128)S(6)} %select_n.35, s32[]{:T(128)S(6)} %select_n.34, ...), kind=kLoop, calls=%fused_computation.4 | loop fusion | bytes 1572880 | tf_op jit(solution)/shard_map/reshape | solution.py:402
  2.1 3.0 %collective-permute-start.5 = (bf16[64,1536]{1,0:T(8,128)(2,1)S(1)}, bf16[64,1536]{1,0:T(8,128)(2,1)S(1)}, u32[]{:S(2)}, u32[]{:S(2)}) collective-permute-start(bf16[64,1536]{1,0:T(8,128)(2,1)S(1)} %get-tuple-element.65), channel_id=1, source_target_pairs={{0,1},{1,0},{2,3},{3,2},{4,5},{5,4},{6,7},{7,6},{8,9},{9,8},{10,11... | collective-permute-start | bytes 589832 | tf_op jit(solution)/shard_map/ppermute | solution.py:395
  5.1 1.5 %collective-permute-start.6 = (bf16[64,1536]{1,0:T(8,128)(2,1)S(1)}, bf16[64,1536]{1,0:T(8,128)(2,1)S(1)}, u32[]{:S(2)}, u32[]{:S(2)}) collective-permute-start(bf16[64,1536]{1,0:T(8,128)(2,1)S(1)} %get-tuple-element.66), channel_id=1, source_target_pairs={{0,2},{1,3},{2,0},{3,1},{4,6},{5,7},{6,4},{7,5},{8,10},{9,11},{10,... | collective-permute-start | bytes 589832 | tf_op jit(solution)/shard_map/ppermute | solution.py:395
  6.6 2.0 %dynamic-slice_bitcast_fusion = (bf16[64,1536]{1,0:T(8,128)(2,1)}, bf16[64,1536]{1,0:T(8,128)(2,1)}, bf16[64,1536]{1,0:T(8,128)(2,1)}, bf16[64,1536]{1,0:T(8,128)(2,1)S(1)}) fusion(bf16[2,1,4,8,8,1536]{5,4,3,2,1,0:T(8,128)(2,1)} %param.10, s32[]{:T(128)S(6)} %select_n.36, s32[]{:T(128)S(6)} %select_n.35, s32[]{:T(128)S(6)} %select_n.34, s32[]{:T(128)S(6)} %select_n.33), kind=kLoop, calls=%fused_computation | loop fusion | bytes 1572880 | tf_op jit(solution)/shard_map/reshape | solution.py:402
  8.7 1.9 %collective-permute-start = (bf16[64,1536]{1,0:T(8,128)(2,1)}, bf16[64,1536]{1,0:T(8,128)(2,1)S(1)}, u32[]{:S(2)}, u32[]{:S(2)}) collective-permute-start(bf16[64,1536]{1,0:T(8,128)(2,1)} %get-tuple-element.55), channel_id=1, source_target_pairs={{0,1},{1,0},{2,3},{3,2},{4,5},{5,4},{6,7},{7,6},{8,9},{9,8},{10,11... | collective-permute-start | bytes 589832 | tf_op jit(solution)/shard_map/ppermute | solution.py:395
  10.6 1.5 %collective-permute-start.1 = (bf16[64,1536]{1,0:T(8,128)(2,1)}, bf16[64,1536]{1,0:T(8,128)(2,1)S(1)}, u32[]{:S(2)}, u32[]{:S(2)}) collective-permute-start(bf16[64,1536]{1,0:T(8,128)(2,1)} %get-tuple-element.56), channel_id=1, source_target_pairs={{0,2},{1,3},{2,0},{3,1},{4,6},{5,7},{6,4},{7,5},{8,10},{9,11},{10,... | collective-permute-start | bytes 589832 | tf_op jit(solution)/shard_map/ppermute | solution.py:395
  14.0 2.0 %collective-permute-done.6.rest_2_ = bf16[64,1536]{1,0:T(8,128)(2,1)S(1)} collective-permute-done((bf16[64,1536]{1,0:T(8,128)(2,1)S(1)}, bf16[64,1536]{1,0:T(8,128)(2,1)S(1)}, u32[]{:S(2)}, u32[]{:S(2)}) %collective-permute-start.6) | collective-permute-done | bytes 196640 | tf_op jit(solution)/shard_map/ppermute | solution.py:395
  16.6 1.2 %combine.3 = (bf16[64,1536]{1,0:T(8,128)(2,1)S(1)}, bf16[48,1536]{1,0:T(8,128)(2,1)S(1)}, bf16[48,1536]{1,0:T(8,128)(2,1)S(1)}, f32[64,1536]{1,0:T(8,128)S(1)}, ...) custom-call(s32[3]{0:T(128)S(1)} %pad_add_fusion.place_ref, bf16[64,1536]{1,0:T(8,128)(2,1)S(1)} %get-tuple-element.64.rest_0_, ...), custom_call_target="tpu_custom_call" | custom-call | flops 1500000000 | tf_op jit(solution)/shard_map/combine/pallas_call | solution.py:217
  17.8 0.7 %copy-done.4 = bf16[2,64,1536]{2,1,0:T(8,128)(2,1)} copy-done((bf16[2,64,1536]{2,1,0:T(8,128)(2,1)}, bf16[2,64,1536]{2,1,0:T(8,128)(2,1)S(1)}, u32[]{:S(2)}) %copy-start.4) | copy-done | bytes 393240
  18.5 1.5 %collective-permute-start.8 = (bf16[48,1536]{1,0:T(8,128)(2,1)S(1)}, bf16[48,1536]{1,0:T(8,128)(2,1)S(1)}, u32[]{:S(2)}, u32[]{:S(2)}) collective-permute-start(bf16[48,1536]{1,0:T(8,128)(2,1)S(1)} %get-tuple-element.69), channel_id=1, source_target_pairs={{0,1},{1,0},{2,3},{3,2},{4,5},{5,4},{6,7},{7,6},{8,9},{9,8},{10,11... | collective-permute-start | bytes 442376 | tf_op jit(solution)/shard_map/ppermute | solution.py:419
  20.0 0.7 collective-permute-start.9
  20.9 2.4 %collective-permute-done.1.rest_2_ = bf16[64,1536]{1,0:T(8,128)(2,1)S(1)} collective-permute-done((bf16[64,1536]{1,0:T(8,128)(2,1)}, bf16[64,1536]{1,0:T(8,128)(2,1)S(1)}, u32[]{:S(2)}, u32[]{:S(2)}) %collective-permute-start.1) | collective-permute-done | bytes 196640 | tf_op jit(solution)/shard_map/ppermute | solution.py:395
  23.2 1.8 %collective-permute-done.2.rest_3_ = bf16[64,1536]{1,0:T(8,128)(2,1)S(1)} collective-permute-done((bf16[64,1536]{1,0:T(8,128)(2,1)}, bf16[64,1536]{1,0:T(8,128)(2,1)S(1)}, u32[]{:S(2)}, u32[]{:S(2)}) %collective-permute-start.2) | collective-permute-done | bytes 196640 | tf_op jit(solution)/shard_map/ppermute | solution.py:395
  25.0 1.2 %combine.2 = (bf16[64,1536]{1,0:T(8,128)(2,1)S(1)}, bf16[48,1536]{1,0:T(8,128)(2,1)S(1)}, bf16[48,1536]{1,0:T(8,128)(2,1)S(1)}, f32[64,1536]{1,0:T(8,128)S(1)}, ...) custom-call(s32[3]{0:T(128)S(1)} %pad_add_fusion.place_ref, bf16[64,1536]{1,0:T(8,128)(2,1)S(1)} %get-tuple-element.54.rest_0_, ...), custom_call_target="tpu_custom_call" | custom-call | flops 1500000000 | tf_op jit(solution)/shard_map/combine/pallas_call | solution.py:217
  26.3 1.5 %collective-permute-start.3 = (bf16[48,1536]{1,0:T(8,128)(2,1)S(1)}, bf16[48,1536]{1,0:T(8,128)(2,1)S(1)}, u32[]{:S(2)}, u32[]{:S(2)}) collective-permute-start(bf16[48,1536]{1,0:T(8,128)(2,1)S(1)} %get-tuple-element.59), channel_id=1, source_target_pairs={{0,1},{1,0},{2,3},{3,2},{4,5},{5,4},{6,7},{7,6},{8,9},{9,8},{10,11... | collective-permute-start | bytes 442376 | tf_op jit(solution)/shard_map/ppermute | solution.py:419
  27.8 0.8 %collective-permute-start.4 = (bf16[48,1536]{1,0:T(8,128)(2,1)S(1)}, bf16[48,1536]{1,0:T(8,128)(2,1)S(1)}, u32[]{:S(2)}, u32[]{:S(2)}) collective-permute-start(bf16[48,1536]{1,0:T(8,128)(2,1)S(1)} %get-tuple-element.60), channel_id=1, source_target_pairs={{0,31},{1,2},{2,1},{3,4},{4,3},{5,6},{6,5},{7,8},{8,7},{9,10},{10,... | collective-permute-start | bytes 442376 | tf_op jit(solution)/shard_map/ppermute | solution.py:420
  28.7 7.0 %conv.2 = (bf16[2,64,1536]{2,1,0:T(8,128)(2,1)}, f32[2,64,2]{2,1,0:T(8,128)S(1)}, f32[4,32,384]{2,1,0:T(8,128)S(1)}, bf16[64,1536]{1,0:T(8,128)(2,1)S(1)}, bf16[...) custom-call(s32[3]{0:T(128)S(1)} %pad_add_fusion.place_ref, ...), custom_call_target="tpu_custom_call" | custom-call | flops 8000000000 | tf_op jit(solution)/shard_map/conv/pallas_call | solution.py:280
  35.7 4.2 %collective-permute-start.10 = (bf16[64,1536]{1,0:T(8,128)(2,1)S(1)}, bf16[64,1536]{1,0:T(8,128)(2,1)S(1)}, u32[]{:S(2)}, u32[]{:S(2)}) collective-permute-start(bf16[64,1536]{1,0:T(8,128)(2,1)S(1)} %get-tuple-element.79), channel_id=1, source_target_pairs={{0,1},{1,0},{2,3},{3,2},{4,5},{5,4},{6,7},{7,6},{8,9},{9,8},{10,11... | collective-permute-start | bytes 589832 | tf_op jit(solution)/shard_map/ppermute | solution.py:395
  39.8 1.5 %collective-permute-start.12 = (bf16[64,1536]{1,0:T(8,128)(2,1)S(1)}, bf16[64,1536]{1,0:T(8,128)(2,1)S(1)}, u32[]{:S(2)}, u32[]{:S(2)}) collective-permute-start(bf16[64,1536]{1,0:T(8,128)(2,1)S(1)} %get-tuple-element.84), channel_id=1, source_target_pairs={{0,3},{1,2},{2,1},{3,0},{4,7},{5,6},{6,5},{7,4},{8,11},{9,10},{10,... | collective-permute-start | bytes 589832 | tf_op jit(solution)/shard_map/ppermute | solution.py:395
  41.3 7.3 %conv.3 = (bf16[2,64,1536]{2,1,0:T(8,128)(2,1)}, f32[2,64,2]{2,1,0:T(8,128)S(1)}, f32[4,32,384]{2,1,0:T(8,128)S(1)}, bf16[64,1536]{1,0:T(8,128)(2,1)S(1)}, bf16[...) custom-call(s32[3]{0:T(128)S(1)} %pad_add_fusion.place_ref, ...), custom_call_target="tpu_custom_call", output_to_operand_aliasing={{0}: (14, {}), {1}: (15, {})} | custom-call | flops 8000000000 | tf_op jit(solution)/shard_map/conv/pallas_call | solution.py:280
  48.6 2.1 %collective-permute-start.16 = (f32[32,384]{1,0:T(8,128)S(1)}, f32[32,384]{1,0:T(8,128)S(1)}, u32[]{:S(2)}, u32[]{:S(2)}) collective-permute-start(f32[32,384]{1,0:T(8,128)S(1)} %get-tuple-element.124), channel_id=1, source_target_pairs={{0,1},{1,0},{2,3},{3,2},{4,5},{5,4},{6,7},{7,6},{8,9},{9,8},{10,11... | collective-permute-start | bytes 147464 | tf_op jit(solution)/shard_map/ppermute | solution.py:395
  50.7 1.5 %collective-permute-start.17 = (f32[32,384]{1,0:T(8,128)S(1)}, f32[32,384]{1,0:T(8,128)S(1)}, u32[]{:S(2)}, u32[]{:S(2)}) collective-permute-start(f32[32,384]{1,0:T(8,128)S(1)} %get-tuple-element.126), channel_id=1, source_target_pairs={{0,2},{1,3},{2,0},{3,1},{4,6},{5,7},{6,4},{7,5},{8,10},{9,11},{10,... | collective-permute-start | bytes 147464 | tf_op jit(solution)/shard_map/ppermute | solution.py:395
  52.2 1.9 %collective-permute-start.13 = (bf16[64,1536]{1,0:T(8,128)(2,1)S(1)}, bf16[64,1536]{1,0:T(8,128)(2,1)S(1)}, u32[]{:S(2)}, u32[]{:S(2)}) collective-permute-start(bf16[64,1536]{1,0:T(8,128)(2,1)S(1)} %get-tuple-element.90), channel_id=1, source_target_pairs={{0,1},{1,0},{2,3},{3,2},{4,5},{5,4},{6,7},{7,6},{8,9},{9,8},{10,11... | collective-permute-start | bytes 589832 | tf_op jit(solution)/shard_map/ppermute | solution.py:395
  54.3 1.5 %collective-permute-start.15 = (bf16[64,1536]{1,0:T(8,128)(2,1)S(1)}, bf16[64,1536]{1,0:T(8,128)(2,1)S(1)}, u32[]{:S(2)}, u32[]{:S(2)}) collective-permute-start(bf16[64,1536]{1,0:T(8,128)(2,1)S(1)} %get-tuple-element.92), channel_id=1, source_target_pairs={{0,3},{1,2},{2,1},{3,0},{4,7},{5,6},{6,5},{7,4},{8,11},{9,10},{10,... | collective-permute-start | bytes 589832 | tf_op jit(solution)/shard_map/ppermute | solution.py:395
  56.4 0.7 copy.60
  57.6 1.7 %collective-permute-start.20 = (f32[32,384]{1,0:T(8,128)S(1)}, f32[32,384]{1,0:T(8,128)S(1)}, u32[]{:S(2)}, u32[]{:S(2)}) collective-permute-start(f32[32,384]{1,0:T(8,128)S(1)} %add.96), channel_id=1, source_target_pairs={{0,8},{4,12},{8,0},{12,4},{16,24},{20,28},{24,16},{28,20},{1,9},{5... | collective-permute-start | bytes 147464 | tf_op jit(solution)/shard_map/ppermute | solution.py:432
  59.3 1.4 %finish.2.refs_4_ = bf16[2,4,64,1536]{3,2,1,0:T(8,128)(2,1)} custom-call(s32[3]{0:T(128)S(1)} %pad_add_fusion.place_ref, bf16[64,1536]{1,0:T(8,128)(2,1)S(1)} %get-tuple-element.93.refs_0_, bf16[64,1536]{1,0:T(8,128)(2,1)S(1)} %collective-permute-done.10.refs_1_, bf16[64,1536]{1,0:T(8,128)(2,1)S(1)} %collective-permute-done.11.refs_2_, ...), custom_call_target="tpu_custom_call" | custom-call | flops 1500000000 | tf_op jit(solution)/shard_map/finish/pallas_call | solution.py:338
  60.8 1.0 %collective-permute-done.20 = f32[32,384]{1,0:T(8,128)S(1)} collective-permute-done((f32[32,384]{1,0:T(8,128)S(1)}, f32[32,384]{1,0:T(8,128)S(1)}, u32[]{:S(2)}, u32[]{:S(2)}) %collective-permute-start.20) | collective-permute-done | bytes 49184 | tf_op jit(solution)/shard_map/ppermute | solution.py:432
  61.8 2.7 %collective-permute-start.21 = (f32[32,384]{1,0:T(8,128)S(1)}, f32[32,384]{1,0:T(8,128)S(1)}, u32[]{:S(2)}, u32[]{:S(2)}) collective-permute-start(f32[32,384]{1,0:T(8,128)S(1)} %add.97.refs_0_), channel_id=1, source_target_pairs={{0,16},{4,20},{8,24},{12,28},{16,0},{20,4},{24,8},{28,12},{1,17},{... | collective-permute-start | bytes 147464 | tf_op jit(solution)/shard_map/ppermute | solution.py:432
  64.5 1.5 %finish.3 = bf16[2,4,64,1536]{3,2,1,0:T(8,128)(2,1)} custom-call(s32[3]{0:T(128)S(1)} %pad_add_fusion.place_ref, bf16[64,1536]{1,0:T(8,128)(2,1)S(1)} %get-tuple-element.89.refs_0_, bf16[64,1536]{1,0:T(8,128)(2,1)S(1)} %collective-permute-done.13.refs_1_, bf16[64,1536]{1,0:T(8,128)(2,1)S(1)} %collective-permute-done.14.refs_2_, ...), custom_call_target="tpu_custom_call", output_to_operand_aliasing={{}: (5, {})} | custom-call | flops 1500000000 | tf_op jit(solution)/shard_map/finish/pallas_call | solution.py:338
  66.0 0.9 %collective-permute-done.21.refs_1_ = f32[32,384]{1,0:T(8,128)S(1)} collective-permute-done((f32[32,384]{1,0:T(8,128)S(1)}, f32[32,384]{1,0:T(8,128)S(1)}, u32[]{:S(2)}, u32[]{:S(2)}) %collective-permute-start.21) | collective-permute-done | bytes 49184 | tf_op jit(solution)/shard_map/ppermute | solution.py:432
  66.8 0.6 total.1
  (64 shorter events, 3.9 us)
Async XLA Ops:
  0.7 11.5 %copy-start.7 = (s32[2,64,2]{1,2,0:T(2,128)S(1)}, s32[2,64,2]{1,2,0:T(2,128)}, u32[]{:S(2)}) copy-start(s32[2,64,2]{1,2,0:T(2,128)} %param.11) | copy-start | bytes 3076
  0.7 11.6 %copy-start.9 = (s32[2,1,64]{2,1,0:T(1,128)S(1)}, s32[2,1,64]{2,1,0:T(1,128)}, u32[]{:S(2)}) copy-start(s32[2,1,64]{2,1,0:T(1,128)} %param.12) | copy-start | bytes 1540
  0.7 13.2 %copy-start.6 = (f32[1536]{0:T(1024)S(1)}, f32[1536]{0:T(1024)}, u32[]{:S(2)}) copy-start(f32[1536]{0:T(1024)} %param.15) | copy-start | bytes 18436
  0.7 13.2 %copy-start.8 = (f32[2,64,2]{1,2,0:T(2,128)S(1)}, f32[2,64,2]{1,2,0:T(2,128)}, u32[]{:S(2)}) copy-start(f32[2,64,2]{1,2,0:T(2,128)} %param.13) | copy-start | bytes 3076
  0.7 15.9 %copy-start = (bf16[2,64,1536]{2,1,0:T(8,128)(2,1)S(1)}, bf16[2,64,1536]{2,1,0:T(8,128)(2,1)}, u32[]{:S(2)}) copy-start(bf16[2,64,1536]{2,1,0:T(8,128)(2,1)} %rest_4_.3) | copy-start | bytes 1179652
  0.7 15.9 %copy-start.1 = (bf16[2,64,1536]{2,1,0:T(8,128)(2,1)S(1)}, bf16[2,64,1536]{2,1,0:T(8,128)(2,1)}, u32[]{:S(2)}) copy-start(bf16[2,64,1536]{2,1,0:T(8,128)(2,1)} %grad_out_ref.3) | copy-start | bytes 1179652
  2.1 11.3 %collective-permute-start.5 = (bf16[64,1536]{1,0:T(8,128)(2,1)S(1)}, bf16[64,1536]{1,0:T(8,128)(2,1)S(1)}, u32[]{:S(2)}, u32[]{:S(2)}) collective-permute-start(bf16[64,1536]{1,0:T(8,128)(2,1)S(1)} %get-tuple-element.65), channel_id=1, source_target_pairs={{0,1},{1,0},{2,3},{3,2},{4,5},{5,4},{6,7},{7,6},{8,9},{9,8},{10,11... | collective-permute-start | bytes 589832 | tf_op jit(solution)/shard_map/ppermute | solution.py:395
  5.1 11.0 %collective-permute-start.6 = (bf16[64,1536]{1,0:T(8,128)(2,1)S(1)}, bf16[64,1536]{1,0:T(8,128)(2,1)S(1)}, u32[]{:S(2)}, u32[]{:S(2)}) collective-permute-start(bf16[64,1536]{1,0:T(8,128)(2,1)S(1)} %get-tuple-element.66), channel_id=1, source_target_pairs={{0,2},{1,3},{2,0},{3,1},{4,6},{5,7},{6,4},{7,5},{8,10},{9,11},{10,... | collective-permute-start | bytes 589832 | tf_op jit(solution)/shard_map/ppermute | solution.py:395
  6.6 10.0 %collective-permute-start.7 = (bf16[64,1536]{1,0:T(8,128)(2,1)S(1)}, bf16[64,1536]{1,0:T(8,128)(2,1)S(1)}, u32[]{:S(2)}, u32[]{:S(2)}) collective-permute-start(bf16[64,1536]{1,0:T(8,128)(2,1)S(1)} %get-tuple-element.67), channel_id=1, source_target_pairs={{0,3},{1,2},{2,1},{3,0},{4,7},{5,6},{6,5},{7,4},{8,11},{9,10},{10,... | collective-permute-start | bytes 589832 | tf_op jit(solution)/shard_map/ppermute | solution.py:395
  8.7 12.2 %collective-permute-start = (bf16[64,1536]{1,0:T(8,128)(2,1)}, bf16[64,1536]{1,0:T(8,128)(2,1)S(1)}, u32[]{:S(2)}, u32[]{:S(2)}) collective-permute-start(bf16[64,1536]{1,0:T(8,128)(2,1)} %get-tuple-element.55), channel_id=1, source_target_pairs={{0,1},{1,0},{2,3},{3,2},{4,5},{5,4},{6,7},{7,6},{8,9},{9,8},{10,11... | collective-permute-start | bytes 589832 | tf_op jit(solution)/shard_map/ppermute | solution.py:395
  10.6 12.6 %collective-permute-start.1 = (bf16[64,1536]{1,0:T(8,128)(2,1)}, bf16[64,1536]{1,0:T(8,128)(2,1)S(1)}, u32[]{:S(2)}, u32[]{:S(2)}) collective-permute-start(bf16[64,1536]{1,0:T(8,128)(2,1)} %get-tuple-element.56), channel_id=1, source_target_pairs={{0,2},{1,3},{2,0},{3,1},{4,6},{5,7},{6,4},{7,5},{8,10},{9,11},{10,... | collective-permute-start | bytes 589832 | tf_op jit(solution)/shard_map/ppermute | solution.py:395
  13.4 11.7 %collective-permute-start.2 = (bf16[64,1536]{1,0:T(8,128)(2,1)}, bf16[64,1536]{1,0:T(8,128)(2,1)S(1)}, u32[]{:S(2)}, u32[]{:S(2)}) collective-permute-start(bf16[64,1536]{1,0:T(8,128)(2,1)} %get-tuple-element.57), channel_id=1, source_target_pairs={{0,3},{1,2},{2,1},{3,0},{4,7},{5,6},{6,5},{7,4},{8,11},{9,10},{10,... | collective-permute-start | bytes 589832 | tf_op jit(solution)/shard_map/ppermute | solution.py:395
  17.8 0.7 %copy-start.4 = (bf16[2,64,1536]{2,1,0:T(8,128)(2,1)}, bf16[2,64,1536]{2,1,0:T(8,128)(2,1)S(1)}, u32[]{:S(2)}) copy-start(bf16[2,64,1536]{2,1,0:T(8,128)(2,1)S(1)} %get-tuple-element.73.picked_ref) | copy-start | bytes 1179652
  18.5 10.1 %collective-permute-start.8 = (bf16[48,1536]{1,0:T(8,128)(2,1)S(1)}, bf16[48,1536]{1,0:T(8,128)(2,1)S(1)}, u32[]{:S(2)}, u32[]{:S(2)}) collective-permute-start(bf16[48,1536]{1,0:T(8,128)(2,1)S(1)} %get-tuple-element.69), channel_id=1, source_target_pairs={{0,1},{1,0},{2,3},{3,2},{4,5},{5,4},{6,7},{7,6},{8,9},{9,8},{10,11... | collective-permute-start | bytes 442376 | tf_op jit(solution)/shard_map/ppermute | solution.py:419
  20.0 8.6 %collective-permute-start.9 = (bf16[48,1536]{1,0:T(8,128)(2,1)S(1)}, bf16[48,1536]{1,0:T(8,128)(2,1)S(1)}, u32[]{:S(2)}, u32[]{:S(2)}) collective-permute-start(bf16[48,1536]{1,0:T(8,128)(2,1)S(1)} %get-tuple-element.70), channel_id=1, source_target_pairs={{0,31},{1,2},{2,1},{3,4},{4,3},{5,6},{6,5},{7,8},{8,7},{9,10},{10,... | collective-permute-start | bytes 442376 | tf_op jit(solution)/shard_map/ppermute | solution.py:420
  20.9 7.8 %copy-start.2 = (f32[31,1536]{1,0:T(8,128)S(1)}, f32[31,1536]{1,0:T(8,128)}, u32[]{:S(2)}) copy-start(f32[31,1536]{1,0:T(8,128)} %kernel_ref.3) | copy-start | bytes 571396
  20.9 7.8 %copy-start.3 = (s32[2,8]{1,0:T(2,128)S(1)}, s32[2,8]{1,0:T(2,128)}, u32[]{:S(2)}) copy-start(s32[2,8]{1,0:T(2,128)} %lengths_ref.3) | copy-start | bytes 196
  20.9 7.8 %copy-start.5 = (bf16[2,64,1536]{2,1,0:T(8,128)(2,1)S(1)}, bf16[2,64,1536]{2,1,0:T(8,128)(2,1)}, u32[]{:S(2)}) copy-start(bf16[2,64,1536]{2,1,0:T(8,128)(2,1)} %copy-done.4) | copy-start | bytes 1179652
  26.3 15.0 %collective-permute-start.3 = (bf16[48,1536]{1,0:T(8,128)(2,1)S(1)}, bf16[48,1536]{1,0:T(8,128)(2,1)S(1)}, u32[]{:S(2)}, u32[]{:S(2)}) collective-permute-start(bf16[48,1536]{1,0:T(8,128)(2,1)S(1)} %get-tuple-element.59), channel_id=1, source_target_pairs={{0,1},{1,0},{2,3},{3,2},{4,5},{5,4},{6,7},{7,6},{8,9},{9,8},{10,11... | collective-permute-start | bytes 442376 | tf_op jit(solution)/shard_map/ppermute | solution.py:419
  27.8 13.5 %collective-permute-start.4 = (bf16[48,1536]{1,0:T(8,128)(2,1)S(1)}, bf16[48,1536]{1,0:T(8,128)(2,1)S(1)}, u32[]{:S(2)}, u32[]{:S(2)}) collective-permute-start(bf16[48,1536]{1,0:T(8,128)(2,1)S(1)} %get-tuple-element.60), channel_id=1, source_target_pairs={{0,31},{1,2},{2,1},{3,4},{4,3},{5,6},{6,5},{7,8},{8,7},{9,10},{10,... | collective-permute-start | bytes 442376 | tf_op jit(solution)/shard_map/ppermute | solution.py:420
  35.7 12.9 %collective-permute-start.10 = (bf16[64,1536]{1,0:T(8,128)(2,1)S(1)}, bf16[64,1536]{1,0:T(8,128)(2,1)S(1)}, u32[]{:S(2)}, u32[]{:S(2)}) collective-permute-start(bf16[64,1536]{1,0:T(8,128)(2,1)S(1)} %get-tuple-element.79), channel_id=1, source_target_pairs={{0,1},{1,0},{2,3},{3,2},{4,5},{5,4},{6,7},{7,6},{8,9},{9,8},{10,11... | collective-permute-start | bytes 589832 | tf_op jit(solution)/shard_map/ppermute | solution.py:395
  39.8 12.4 %collective-permute-start.11 = (bf16[64,1536]{1,0:T(8,128)(2,1)S(1)}, bf16[64,1536]{1,0:T(8,128)(2,1)S(1)}, u32[]{:S(2)}, u32[]{:S(2)}) collective-permute-start(bf16[64,1536]{1,0:T(8,128)(2,1)S(1)} %get-tuple-element.83), channel_id=1, source_target_pairs={{0,2},{1,3},{2,0},{3,1},{4,6},{5,7},{6,4},{7,5},{8,10},{9,11},{10,... | collective-permute-start | bytes 589832 | tf_op jit(solution)/shard_map/ppermute | solution.py:395
  39.8 12.4 %collective-permute-start.12 = (bf16[64,1536]{1,0:T(8,128)(2,1)S(1)}, bf16[64,1536]{1,0:T(8,128)(2,1)S(1)}, u32[]{:S(2)}, u32[]{:S(2)}) collective-permute-start(bf16[64,1536]{1,0:T(8,128)(2,1)S(1)} %get-tuple-element.84), channel_id=1, source_target_pairs={{0,3},{1,2},{2,1},{3,0},{4,7},{5,6},{6,5},{7,4},{8,11},{9,10},{10,... | collective-permute-start | bytes 589832 | tf_op jit(solution)/shard_map/ppermute | solution.py:395
  48.6 5.7 %collective-permute-start.16 = (f32[32,384]{1,0:T(8,128)S(1)}, f32[32,384]{1,0:T(8,128)S(1)}, u32[]{:S(2)}, u32[]{:S(2)}) collective-permute-start(f32[32,384]{1,0:T(8,128)S(1)} %get-tuple-element.124), channel_id=1, source_target_pairs={{0,1},{1,0},{2,3},{3,2},{4,5},{5,4},{6,7},{7,6},{8,9},{9,8},{10,11... | collective-permute-start | bytes 147464 | tf_op jit(solution)/shard_map/ppermute | solution.py:395
  50.7 5.6 %collective-permute-start.18 = (f32[32,384]{1,0:T(8,128)S(1)}, f32[32,384]{1,0:T(8,128)S(1)}, u32[]{:S(2)}, u32[]{:S(2)}) collective-permute-start(f32[32,384]{1,0:T(8,128)S(1)} %get-tuple-element.125), channel_id=1, source_target_pairs={{0,3},{1,2},{2,1},{3,0},{4,7},{5,6},{6,5},{7,4},{8,11},{9,10},{10,... | collective-permute-start | bytes 147464 | tf_op jit(solution)/shard_map/ppermute | solution.py:395
  50.7 5.6 %collective-permute-start.17 = (f32[32,384]{1,0:T(8,128)S(1)}, f32[32,384]{1,0:T(8,128)S(1)}, u32[]{:S(2)}, u32[]{:S(2)}) collective-permute-start(f32[32,384]{1,0:T(8,128)S(1)} %get-tuple-element.126), channel_id=1, source_target_pairs={{0,2},{1,3},{2,0},{3,1},{4,6},{5,7},{6,4},{7,5},{8,10},{9,11},{10,... | collective-permute-start | bytes 147464 | tf_op jit(solution)/shard_map/ppermute | solution.py:395
  52.2 12.2 %collective-permute-start.13 = (bf16[64,1536]{1,0:T(8,128)(2,1)S(1)}, bf16[64,1536]{1,0:T(8,128)(2,1)S(1)}, u32[]{:S(2)}, u32[]{:S(2)}) collective-permute-start(bf16[64,1536]{1,0:T(8,128)(2,1)S(1)} %get-tuple-element.90), channel_id=1, source_target_pairs={{0,1},{1,0},{2,3},{3,2},{4,5},{5,4},{6,7},{7,6},{8,9},{9,8},{10,11... | collective-permute-start | bytes 589832 | tf_op jit(solution)/shard_map/ppermute | solution.py:395
  54.2 10.3 %collective-permute-start.14 = (bf16[64,1536]{1,0:T(8,128)(2,1)S(1)}, bf16[64,1536]{1,0:T(8,128)(2,1)S(1)}, u32[]{:S(2)}, u32[]{:S(2)}) collective-permute-start(bf16[64,1536]{1,0:T(8,128)(2,1)S(1)} %get-tuple-element.91), channel_id=1, source_target_pairs={{0,2},{1,3},{2,0},{3,1},{4,6},{5,7},{6,4},{7,5},{8,10},{9,11},{10,... | collective-permute-start | bytes 589832 | tf_op jit(solution)/shard_map/ppermute | solution.py:395
  54.3 10.2 %collective-permute-start.15 = (bf16[64,1536]{1,0:T(8,128)(2,1)S(1)}, bf16[64,1536]{1,0:T(8,128)(2,1)S(1)}, u32[]{:S(2)}, u32[]{:S(2)}) collective-permute-start(bf16[64,1536]{1,0:T(8,128)(2,1)S(1)} %get-tuple-element.92), channel_id=1, source_target_pairs={{0,3},{1,2},{2,1},{3,0},{4,7},{5,6},{6,5},{7,4},{8,11},{9,10},{10,... | collective-permute-start | bytes 589832 | tf_op jit(solution)/shard_map/ppermute | solution.py:395
  56.3 1.3 %collective-permute-start.19 = (f32[32,384]{1,0:T(8,128)S(1)}, f32[32,384]{1,0:T(8,128)S(1)}, u32[]{:S(2)}, u32[]{:S(2)}) collective-permute-start(f32[32,384]{1,0:T(8,128)S(1)} %fusion.10), channel_id=1, source_target_pairs={{0,4},{4,0},{8,12},{12,8},{16,20},{20,16},{24,28},{28,24},{1,5},{5... | collective-permute-start | bytes 147464 | tf_op jit(solution)/shard_map/ppermute | solution.py:432
  57.6 4.2 %collective-permute-start.20 = (f32[32,384]{1,0:T(8,128)S(1)}, f32[32,384]{1,0:T(8,128)S(1)}, u32[]{:S(2)}, u32[]{:S(2)}) collective-permute-start(f32[32,384]{1,0:T(8,128)S(1)} %add.96), channel_id=1, source_target_pairs={{0,8},{4,12},{8,0},{12,4},{16,24},{20,28},{24,16},{28,20},{1,9},{5... | collective-permute-start | bytes 147464 | tf_op jit(solution)/shard_map/ppermute | solution.py:432
  61.8 5.1 %collective-permute-start.21 = (f32[32,384]{1,0:T(8,128)S(1)}, f32[32,384]{1,0:T(8,128)S(1)}, u32[]{:S(2)}, u32[]{:S(2)}) collective-permute-start(f32[32,384]{1,0:T(8,128)S(1)} %add.97.refs_0_), channel_id=1, source_target_pairs={{0,16},{4,20},{8,24},{12,28},{16,0},{20,4},{24,8},{28,12},{1,17},{... | collective-permute-start | bytes 147464 | tf_op jit(solution)/shard_map/ppermute | solution.py:432

commit v4 on v3

--- a/solution.py
+++ b/solution.py
@@ -35,7 +35,7 @@
 ):
     table_refs = rest[:group_count]
     frames_ref, grad_out_ref, flat_ref, probs_ref, gain_ref = rest[group_count : group_count + 5]
-    conv_in_ref, near_ref, far_ref, nhat_ref, rstd_ref, picked_ref = rest[-6:]
+    near_ref, far_ref, nhat_ref, rstd_ref, picked_ref = rest[-5:]
     rows = frames_ref.shape[1]
     width = frames_ref.shape[2]
     flat = flat_ref[0]
@@ -55,7 +55,6 @@
     nhat_ref[...] = nhat
     rstd_ref[...] = jnp.broadcast_to(rstd, rstd_ref.shape)
     conv_in = (nhat * gain_ref[...]).astype(BF16)
-    conv_in_ref[...] = conv_in
     odd = place_ref[1]
 
     def send(ref, first):
@@ -86,7 +85,6 @@
     scale,
     place_ref,
     lengths_ref,
-    conv_in_ref,
     near_ref,
     far_ref,
     grad_out_ref,
@@ -108,12 +106,13 @@
         rest = rest[6:]
     out_refs = rest[:group_count]
     window, gout, shifts, gwin, kacc = rest[group_count:]
-    rows, width = conv_in_ref.shape
+    rows, width = nhat_ref.shape
+    conv_in = (nhat_ref[...] * gain_ref[...]).astype(BF16)
     mid = rows + 2 * GSIDE
     full = rows + 2 * SIDE
     odd = place_ref[1]
 
-    window[SIDE : SIDE + rows, :] = conv_in_ref[...]
+    window[SIDE : SIDE + rows, :] = conv_in
     gout[GSIDE : GSIDE + rows, :] = grad_out_ref[0]
 
     def receive(before, after):
@@ -164,7 +163,7 @@
     g = (gout[...].astype(F32) * swish_slope(acc)).astype(BF16)
     gwin[SIDE - GSIDE : SIDE - GSIDE + mid, :] = g
     gw = gwin[...]
-    x = conv_in_ref[...].astype(F32)
+    x = conv_in.astype(F32)
     acc = jnp.zeros((rows, width), F32)
     for j in range(KW):
         base = j * mid + GSIDE
@@ -228,7 +227,6 @@
                 whole(gain.shape),
             ],
             out_specs=[
-                whole((rows, width)),
                 whole((SIDE + GSIDE, width)),
                 whole((SIDE + GSIDE, width)),
                 whole((rows, width)),
@@ -237,7 +235,6 @@
             ],
         ),
         out_shape=[
-            jax.ShapeDtypeStruct((rows, width), BF16),
             jax.ShapeDtypeStruct((SIDE + GSIDE, width), BF16),
             jax.ShapeDtypeStruct((SIDE + GSIDE, width), BF16),
             jax.ShapeDtypeStruct((rows, width), F32),
@@ -245,13 +242,13 @@
             jax.ShapeDtypeStruct((2, rows, width), BF16),
         ],
         compiler_params=pltpu.CompilerParams(vmem_limit_bytes=VMEM_LIMIT),
-        cost_estimate=pl.CostEstimate(flops=1500 * 10**6, bytes_accessed=0, transcendentals=0),
+        cost_estimate=pl.CostEstimate(flops=3000 * 10**6, bytes_accessed=0, transcendentals=0),
         name="combine",
     )(place, *tables, frames, grad_out, flat, probs, gain)
 
 
-def conv(micro, place, lengths, group_count, frame_total, conv_in, near, far, grad_out, nhat, rstd, picked, flat_row, probs, gain, kernel, earlier):
-    rows, width = conv_in.shape
+def conv(micro, place, lengths, group_count, frame_total, near, far, grad_out, nhat, rstd, picked, flat_row, probs, gain, kernel, earlier):
+    rows, width = nhat.shape
     micro_count = grad_out.shape[0]
     first = earlier is None
     slots = EXPERTS * CAP // group_count
@@ -259,7 +256,6 @@
     full = rows + 2 * SIDE
     terms_shape = (group_count, KW + 1, width // group_count)
     in_specs = [
-        whole(conv_in.shape),
         whole(near.shape),
         whole(far.shape),
         of_micro(micro, grad_out.shape),
@@ -271,7 +267,7 @@
         whole(gain.shape),
         whole(kernel.shape),
     ]
-    operands = [place, lengths, conv_in, near, far, grad_out, nhat, rstd, picked, flat_row, probs, gain, kernel]
+    operands = [place, lengths, near, far, grad_out, nhat, rstd, picked, flat_row, probs, gain, kernel]
     aliases = {}
     if not first:
         in_specs += [whole(terms_shape), pl.BlockSpec(memory_space=pl.ANY), pl.BlockSpec(memory_space=pl.ANY)]
@@ -413,13 +409,13 @@
     earlier = None
     returned = []
     for micro in range(micro_count):
-        conv_in, near, far, nhat, rstd, picked = combine(
+        near, far, nhat, rstd, picked = combine(
             micro, place, tables[micro], frames, grad_out, flat, probs, gain_row
         )
         near = lax.ppermute(near, both, near_pairs)
         far = lax.ppermute(far, both, far_pairs)
         grad_x, grad_probs, terms, *outs = conv(
-            micro, place, lengths, groups, frame_total, conv_in, near, far, grad_out,
+            micro, place, lengths, groups, frame_total, near, far, grad_out,
             nhat, rstd, picked, flat_row, probs, gain_row, kernel, earlier,
         )
         earlier = (grad_x, grad_probs, terms)

time: 67.6 us -> 67.5 us (level)
  waiting for transfers between devices: 9.74 us -> 11.2 us
  local copies, waits for them, and re-layouts: 5.99 us -> 4.67 us
    reshape x2, local copies, waits for them, and re-layouts: 3.39 us -> 1.44 us  [local(): lax.dynamic_slice(cells, (micro, 0, me ^ step, 0, 0, 0), sizes)]
    ppermute x15, waiting for transfers between devices: 7.3 us -> 8.8 us  [swap(): return lax.ppermute(cells, 'expert', [(i, i ^ step) for i in range(groups)])]
    broadcast_in_dim x1, local copies, waits for them, and re-layouts: 0.01 us -> 0.7 us  [local(): gain_row = gain[None, :]]
    unnamed x23 -> x17, local copies, waits for them, and re-layouts: 1.64 us -> 1.57 us
  transfers between devices with their start and end apart: 22 -> 22, of which waited for: 8 -> 7; matrix products, arithmetic and copies ran while one was open for 6% -> 5% of each run, Pallas kernels for 29% -> 29%
where the time goes in v4:
time: 67.5 us; the launch traced here: 67.2 us
  starting transfers between devices  30 us (44%)
  Pallas kernels  20 us (30%)
  waiting for transfers between devices  11.2 us (17%)
  local copies, waits for them, and re-layouts  4.67 us (7%)
  between operations  0.88 us (1%)
    ppermute x15, starting transfers between devices, swap(): return lax.ppermute(cells, 'expert', [(i, i ^ step) for i in range(groups)])  21.6 us
    pallas_call x2, Pallas kernels, conv(): pl.pallas_call(functools.partial(conv_kernel, group_count, first, micro,...  14.1 us
    ppermute x15, waiting for transfers between devices, swap(): return lax.ppermute(cells, 'expert', [(i, i ^ step) for i in range(groups)])  8.8 us
    ppermute x3, starting transfers between devices, over(): lax.ppermute(cells, 'tm', [(i, i ^ step) for i in range(tm)])  4.48 us
    pallas_call x2, Pallas kernels, finish(): pl.pallas_call(functools.partial(finish_kernel, group_count, micro), in_s...  2.9 us
    ppermute x2, starting transfers between devices, local(): near = lax.ppermute(near, both, near_pairs)  2.61 us
    ppermute x3, waiting for transfers between devices, over(): lax.ppermute(cells, 'tm', [(i, i ^ step) for i in range(tm)])  2.43 us
    pallas_call x2, Pallas kernels, combine(): pl.pallas_call(functools.partial(combine_kernel, group_count), grid_spec=...  2.42 us
  transfers between devices with their start and end apart: 22, of which 7 were waited for; matrix products, arithmetic and copies ran while one was open for 5% of the time, Pallas kernels for 29%

profile of v4, /device:TPU:0, one launch (start us, length us, event | category | flops | bytes accessed | tf_op | source)
XLA Modules:
  0.0 67.2 jit_solution(3706438486431298688)
XLA Ops:
  0.7 1.4 %dynamic-slice_bitcast_fusion.4 = (bf16[64,1536]{1,0:T(8,128)(2,1)S(1)}, bf16[64,1536]{1,0:T(8,128)(2,1)S(1)}, bf16[64,1536]{1,0:T(8,128)(2,1)S(1)}, bf16[64,1536]{1,0:T(8,128)(2,1)S(1)}) fusion(bf16[2,1,4,8,8,1536]{5,4,3,2,1,0:T(8,128)(2,1)} %param.10, s32[]{:T(128)S(6)} %select_n.36, s32[]{:T(128)S(6)} %select_n.35, s32[]{:T(128)S(6)} %select_n.34, ...), kind=kLoop, calls=%fused_computation.4 | loop fusion | bytes 1572880 | tf_op jit(solution)/shard_map/reshape | solution.py:398
  2.1 3.0 %collective-permute-start.5 = (bf16[64,1536]{1,0:T(8,128)(2,1)S(1)}, bf16[64,1536]{1,0:T(8,128)(2,1)S(1)}, u32[]{:S(2)}, u32[]{:S(2)}) collective-permute-start(bf16[64,1536]{1,0:T(8,128)(2,1)S(1)} %get-tuple-element.62), channel_id=1, source_target_pairs={{0,1},{1,0},{2,3},{3,2},{4,5},{5,4},{6,7},{7,6},{8,9},{9,8},{10,11... | collective-permute-start | bytes 589832 | tf_op jit(solution)/shard_map/ppermute | solution.py:391
  5.1 1.5 %collective-permute-start.6 = (bf16[64,1536]{1,0:T(8,128)(2,1)S(1)}, bf16[64,1536]{1,0:T(8,128)(2,1)S(1)}, u32[]{:S(2)}, u32[]{:S(2)}) collective-permute-start(bf16[64,1536]{1,0:T(8,128)(2,1)S(1)} %get-tuple-element.63), channel_id=1, source_target_pairs={{0,2},{1,3},{2,0},{3,1},{4,6},{5,7},{6,4},{7,5},{8,10},{9,11},{10,... | collective-permute-start | bytes 589832 | tf_op jit(solution)/shard_map/ppermute | solution.py:391
  6.7 2.0 %collective-permute-start = (bf16[64,1536]{1,0:T(8,128)(2,1)S(1)}, bf16[64,1536]{1,0:T(8,128)(2,1)S(1)}, u32[]{:S(2)}, u32[]{:S(2)}) collective-permute-start(bf16[64,1536]{1,0:T(8,128)(2,1)S(1)} %get-tuple-element.53), channel_id=1, source_target_pairs={{0,1},{1,0},{2,3},{3,2},{4,5},{5,4},{6,7},{7,6},{8,9},{9,8},{10,11... | collective-permute-start | bytes 589832 | tf_op jit(solution)/shard_map/ppermute | solution.py:391
  8.7 1.5 %collective-permute-start.1 = (bf16[64,1536]{1,0:T(8,128)(2,1)S(1)}, bf16[64,1536]{1,0:T(8,128)(2,1)S(1)}, u32[]{:S(2)}, u32[]{:S(2)}) collective-permute-start(bf16[64,1536]{1,0:T(8,128)(2,1)S(1)} %get-tuple-element.54), channel_id=1, source_target_pairs={{0,2},{1,3},{2,0},{3,1},{4,6},{5,7},{6,4},{7,5},{8,10},{9,11},{10,... | collective-permute-start | bytes 589832 | tf_op jit(solution)/shard_map/ppermute | solution.py:391
  11.5 0.7 %broadcast_in_dim.4.rest_8_.gain_ref = f32[1,1536]{1,0:T(1,128)S(1)} reshape(f32[1536]{0:T(1024)} %param.15) | data formatting | bytes 12288 | tf_op jit(solution)/shard_map/broadcast_in_dim | solution.py:407
  12.2 0.8 %copy.54.rest_7_.probs_ref = f32[2,64,2]{2,1,0:T(8,128)S(1)} copy(f32[2,64,2]{1,2,0:T(2,128)} %param.13) | data formatting | bytes 2048 | tf_op args[4]
  13.8 3.2 %collective-permute-done.6.rest_2_ = bf16[64,1536]{1,0:T(8,128)(2,1)S(1)} collective-permute-done((bf16[64,1536]{1,0:T(8,128)(2,1)S(1)}, bf16[64,1536]{1,0:T(8,128)(2,1)S(1)}, u32[]{:S(2)}, u32[]{:S(2)}) %collective-permute-start.6) | collective-permute-done | bytes 196640 | tf_op jit(solution)/shard_map/ppermute | solution.py:391
  17.1 1.2 %combine.3 = (bf16[48,1536]{1,0:T(8,128)(2,1)S(1)}, bf16[48,1536]{1,0:T(8,128)(2,1)S(1)}, f32[64,1536]{1,0:T(8,128)S(1)}, f32[64,128]{1,0:T(8,128)S(1)}, bf16[2,64,1536]{2,1,0:T(8,128)(2,1)S(1)}) custom-call(s32[3]{0:T(128)S(1)} %pad_add_fusion.place_ref, bf16[64,1536]{1,0:T(8,128)(2,1)S(1)} %get-tuple-element.61.rest_0_, ...), custom_call_target="tpu_custom_call" | custom-call | flops 3000000000 | tf_op jit(solution)/shard_map/combine/pallas_call | solution.py:216
  18.3 1.1 %collective-permute-start.8 = (bf16[48,1536]{1,0:T(8,128)(2,1)S(1)}, bf16[48,1536]{1,0:T(8,128)(2,1)S(1)}, u32[]{:S(2)}, u32[]{:S(2)}) collective-permute-start(bf16[48,1536]{1,0:T(8,128)(2,1)S(1)} %get-tuple-element.65), channel_id=1, source_target_pairs={{0,1},{1,0},{2,3},{3,2},{4,5},{5,4},{6,7},{7,6},{8,9},{9,8},{10,11... | collective-permute-start | bytes 442376 | tf_op jit(solution)/shard_map/ppermute | solution.py:415
  19.4 0.7 collective-permute-start.9
  20.1 3.1 %collective-permute-done.1.rest_2_ = bf16[64,1536]{1,0:T(8,128)(2,1)S(1)} collective-permute-done((bf16[64,1536]{1,0:T(8,128)(2,1)S(1)}, bf16[64,1536]{1,0:T(8,128)(2,1)S(1)}, u32[]{:S(2)}, u32[]{:S(2)}) %collective-permute-start.1) | collective-permute-done | bytes 196640 | tf_op jit(solution)/shard_map/ppermute | solution.py:391
  23.2 1.9 %collective-permute-done.2.rest_3_ = bf16[64,1536]{1,0:T(8,128)(2,1)S(1)} collective-permute-done((bf16[64,1536]{1,0:T(8,128)(2,1)S(1)}, bf16[64,1536]{1,0:T(8,128)(2,1)S(1)}, u32[]{:S(2)}, u32[]{:S(2)}) %collective-permute-start.2) | collective-permute-done | bytes 196640 | tf_op jit(solution)/shard_map/ppermute | solution.py:391
  25.1 1.2 %combine.2 = (bf16[48,1536]{1,0:T(8,128)(2,1)S(1)}, bf16[48,1536]{1,0:T(8,128)(2,1)S(1)}, f32[64,1536]{1,0:T(8,128)S(1)}, f32[64,128]{1,0:T(8,128)S(1)}, bf16[2,64,1536]{2,1,0:T(8,128)(2,1)S(1)}) custom-call(s32[3]{0:T(128)S(1)} %pad_add_fusion.place_ref, bf16[64,1536]{1,0:T(8,128)(2,1)S(1)} %get-tuple-element.52.rest_0_, ...), custom_call_target="tpu_custom_call" | custom-call | flops 3000000000 | tf_op jit(solution)/shard_map/combine/pallas_call | solution.py:216
  26.3 1.5 %collective-permute-start.3 = (bf16[48,1536]{1,0:T(8,128)(2,1)S(1)}, bf16[48,1536]{1,0:T(8,128)(2,1)S(1)}, u32[]{:S(2)}, u32[]{:S(2)}) collective-permute-start(bf16[48,1536]{1,0:T(8,128)(2,1)S(1)} %get-tuple-element.56), channel_id=1, source_target_pairs={{0,1},{1,0},{2,3},{3,2},{4,5},{5,4},{6,7},{7,6},{8,9},{9,8},{10,11... | collective-permute-start | bytes 442376 | tf_op jit(solution)/shard_map/ppermute | solution.py:415
  27.8 0.7 %collective-permute-start.4 = (bf16[48,1536]{1,0:T(8,128)(2,1)S(1)}, bf16[48,1536]{1,0:T(8,128)(2,1)S(1)}, u32[]{:S(2)}, u32[]{:S(2)}) collective-permute-start(bf16[48,1536]{1,0:T(8,128)(2,1)S(1)} %get-tuple-element.57), channel_id=1, source_target_pairs={{0,31},{1,2},{2,1},{3,4},{4,3},{5,6},{6,5},{7,8},{8,7},{9,10},{10,... | collective-permute-start | bytes 442376 | tf_op jit(solution)/shard_map/ppermute | solution.py:416
  28.5 6.9 %conv.2 = (bf16[2,64,1536]{2,1,0:T(8,128)(2,1)}, f32[2,64,2]{2,1,0:T(8,128)S(1)}, f32[4,32,384]{2,1,0:T(8,128)S(1)}, bf16[64,1536]{1,0:T(8,128)(2,1)S(1)}, bf16[...) custom-call(s32[3]{0:T(128)S(1)} %pad_add_fusion.place_ref, ...), custom_call_target="tpu_custom_call" | custom-call | flops 8000000000 | tf_op jit(solution)/shard_map/conv/pallas_call | solution.py:276
  35.4 4.3 %collective-permute-start.10 = (bf16[64,1536]{1,0:T(8,128)(2,1)S(1)}, bf16[64,1536]{1,0:T(8,128)(2,1)S(1)}, u32[]{:S(2)}, u32[]{:S(2)}) collective-permute-start(bf16[64,1536]{1,0:T(8,128)(2,1)S(1)} %get-tuple-element.75), channel_id=1, source_target_pairs={{0,1},{1,0},{2,3},{3,2},{4,5},{5,4},{6,7},{7,6},{8,9},{9,8},{10,11... | collective-permute-start | bytes 589832 | tf_op jit(solution)/shard_map/ppermute | solution.py:391
  39.7 1.5 %collective-permute-start.12 = (bf16[64,1536]{1,0:T(8,128)(2,1)S(1)}, bf16[64,1536]{1,0:T(8,128)(2,1)S(1)}, u32[]{:S(2)}, u32[]{:S(2)}) collective-permute-start(bf16[64,1536]{1,0:T(8,128)(2,1)S(1)} %get-tuple-element.80), channel_id=1, source_target_pairs={{0,3},{1,2},{2,1},{3,0},{4,7},{5,6},{6,5},{7,4},{8,11},{9,10},{10,... | collective-permute-start | bytes 589832 | tf_op jit(solution)/shard_map/ppermute | solution.py:391
  41.2 7.2 %conv.3 = (bf16[2,64,1536]{2,1,0:T(8,128)(2,1)}, f32[2,64,2]{2,1,0:T(8,128)S(1)}, f32[4,32,384]{2,1,0:T(8,128)S(1)}, bf16[64,1536]{1,0:T(8,128)(2,1)S(1)}, bf16[...) custom-call(s32[3]{0:T(128)S(1)} %pad_add_fusion.place_ref, ...), custom_call_target="tpu_custom_call", output_to_operand_aliasing={{0}: (13, {}), {1}: (14, {})} | custom-call | flops 8000000000 | tf_op jit(solution)/shard_map/conv/pallas_call | solution.py:276
  48.4 2.1 %collective-permute-start.16 = (f32[32,384]{1,0:T(8,128)S(1)}, f32[32,384]{1,0:T(8,128)S(1)}, u32[]{:S(2)}, u32[]{:S(2)}) collective-permute-start(f32[32,384]{1,0:T(8,128)S(1)} %get-tuple-element.120), channel_id=1, source_target_pairs={{0,1},{1,0},{2,3},{3,2},{4,5},{5,4},{6,7},{7,6},{8,9},{9,8},{10,11... | collective-permute-start | bytes 147464 | tf_op jit(solution)/shard_map/ppermute | solution.py:391
  50.5 1.5 %collective-permute-start.17 = (f32[32,384]{1,0:T(8,128)S(1)}, f32[32,384]{1,0:T(8,128)S(1)}, u32[]{:S(2)}, u32[]{:S(2)}) collective-permute-start(f32[32,384]{1,0:T(8,128)S(1)} %get-tuple-element.122), channel_id=1, source_target_pairs={{0,2},{1,3},{2,0},{3,1},{4,6},{5,7},{6,4},{7,5},{8,10},{9,11},{10,... | collective-permute-start | bytes 147464 | tf_op jit(solution)/shard_map/ppermute | solution.py:391
  52.0 1.9 %collective-permute-start.13 = (bf16[64,1536]{1,0:T(8,128)(2,1)S(1)}, bf16[64,1536]{1,0:T(8,128)(2,1)S(1)}, u32[]{:S(2)}, u32[]{:S(2)}) collective-permute-start(bf16[64,1536]{1,0:T(8,128)(2,1)S(1)} %get-tuple-element.86), channel_id=1, source_target_pairs={{0,1},{1,0},{2,3},{3,2},{4,5},{5,4},{6,7},{7,6},{8,9},{9,8},{10,11... | collective-permute-start | bytes 589832 | tf_op jit(solution)/shard_map/ppermute | solution.py:391
  54.1 1.5 %collective-permute-start.15 = (bf16[64,1536]{1,0:T(8,128)(2,1)S(1)}, bf16[64,1536]{1,0:T(8,128)(2,1)S(1)}, u32[]{:S(2)}, u32[]{:S(2)}) collective-permute-start(bf16[64,1536]{1,0:T(8,128)(2,1)S(1)} %get-tuple-element.88), channel_id=1, source_target_pairs={{0,3},{1,2},{2,1},{3,0},{4,7},{5,6},{6,5},{7,4},{8,11},{9,10},{10,... | collective-permute-start | bytes 589832 | tf_op jit(solution)/shard_map/ppermute | solution.py:391
  56.2 0.7 copy.60
  57.4 1.7 %collective-permute-start.20 = (f32[32,384]{1,0:T(8,128)S(1)}, f32[32,384]{1,0:T(8,128)S(1)}, u32[]{:S(2)}, u32[]{:S(2)}) collective-permute-start(f32[32,384]{1,0:T(8,128)S(1)} %add.96), channel_id=1, source_target_pairs={{0,8},{4,12},{8,0},{12,4},{16,24},{20,28},{24,16},{28,20},{1,9},{5... | collective-permute-start | bytes 147464 | tf_op jit(solution)/shard_map/ppermute | solution.py:428
  59.1 1.4 %finish.2.refs_4_ = bf16[2,4,64,1536]{3,2,1,0:T(8,128)(2,1)} custom-call(s32[3]{0:T(128)S(1)} %pad_add_fusion.place_ref, bf16[64,1536]{1,0:T(8,128)(2,1)S(1)} %get-tuple-element.89.refs_0_, bf16[64,1536]{1,0:T(8,128)(2,1)S(1)} %collective-permute-done.10.refs_1_, bf16[64,1536]{1,0:T(8,128)(2,1)S(1)} %collective-permute-done.11.refs_2_, ...), custom_call_target="tpu_custom_call" | custom-call | flops 1500000000 | tf_op jit(solution)/shard_map/finish/pallas_call | solution.py:334
  60.5 1.0 %collective-permute-done.20 = f32[32,384]{1,0:T(8,128)S(1)} collective-permute-done((f32[32,384]{1,0:T(8,128)S(1)}, f32[32,384]{1,0:T(8,128)S(1)}, u32[]{:S(2)}, u32[]{:S(2)}) %collective-permute-start.20) | collective-permute-done | bytes 49184 | tf_op jit(solution)/shard_map/ppermute | solution.py:428
  61.6 2.7 %collective-permute-start.21 = (f32[32,384]{1,0:T(8,128)S(1)}, f32[32,384]{1,0:T(8,128)S(1)}, u32[]{:S(2)}, u32[]{:S(2)}) collective-permute-start(f32[32,384]{1,0:T(8,128)S(1)} %add.97.refs_0_), channel_id=1, source_target_pairs={{0,16},{4,20},{8,24},{12,28},{16,0},{20,4},{24,8},{28,12},{1,17},{... | collective-permute-start | bytes 147464 | tf_op jit(solution)/shard_map/ppermute | solution.py:428
  64.3 1.5 %finish.3 = bf16[2,4,64,1536]{3,2,1,0:T(8,128)(2,1)} custom-call(s32[3]{0:T(128)S(1)} %pad_add_fusion.place_ref, bf16[64,1536]{1,0:T(8,128)(2,1)S(1)} %get-tuple-element.85.refs_0_, bf16[64,1536]{1,0:T(8,128)(2,1)S(1)} %collective-permute-done.13.refs_1_, bf16[64,1536]{1,0:T(8,128)(2,1)S(1)} %collective-permute-done.14.refs_2_, ...), custom_call_target="tpu_custom_call", output_to_operand_aliasing={{}: (5, {})} | custom-call | flops 1500000000 | tf_op jit(solution)/shard_map/finish/pallas_call | solution.py:334
  65.8 0.9 %collective-permute-done.21.refs_1_ = f32[32,384]{1,0:T(8,128)S(1)} collective-permute-done((f32[32,384]{1,0:T(8,128)S(1)}, f32[32,384]{1,0:T(8,128)S(1)}, u32[]{:S(2)}, u32[]{:S(2)}) %collective-permute-start.21) | collective-permute-done | bytes 49184 | tf_op jit(solution)/shard_map/ppermute | solution.py:428
  66.6 0.6 total.1
  (58 shorter events, 3.5 us)
Async XLA Ops:
  0.7 6.0 %copy-start.4 = (bf16[2,1,4,8,8,1536]{5,4,3,2,1,0:T(8,128)(2,1)S(1)}, bf16[2,1,4,8,8,1536]{5,4,3,2,1,0:T(8,128)(2,1)}, u32[]{:S(2)}) copy-start(bf16[2,1,4,8,8,1536]{5,4,3,2,1,0:T(8,128)(2,1)} %param.10) | copy-start | bytes 4718596
  0.7 9.6 %copy-start.5 = (s32[2,64,2]{1,2,0:T(2,128)S(1)}, s32[2,64,2]{1,2,0:T(2,128)}, u32[]{:S(2)}) copy-start(s32[2,64,2]{1,2,0:T(2,128)} %param.11) | copy-start | bytes 3076
  0.7 9.7 %copy-start.6 = (s32[2,1,64]{2,1,0:T(1,128)S(1)}, s32[2,1,64]{2,1,0:T(1,128)}, u32[]{:S(2)}) copy-start(s32[2,1,64]{2,1,0:T(1,128)} %param.12) | copy-start | bytes 1540
  2.1 15.0 %copy-start = (bf16[2,64,1536]{2,1,0:T(8,128)(2,1)S(1)}, bf16[2,64,1536]{2,1,0:T(8,128)(2,1)}, u32[]{:S(2)}) copy-start(bf16[2,64,1536]{2,1,0:T(8,128)(2,1)} %rest_4_.3) | copy-start | bytes 1179652
  2.1 15.0 %copy-start.1 = (bf16[2,64,1536]{2,1,0:T(8,128)(2,1)S(1)}, bf16[2,64,1536]{2,1,0:T(8,128)(2,1)}, u32[]{:S(2)}) copy-start(bf16[2,64,1536]{2,1,0:T(8,128)(2,1)} %grad_out_ref.3) | copy-start | bytes 1179652
  2.1 11.1 %collective-permute-start.5 = (bf16[64,1536]{1,0:T(8,128)(2,1)S(1)}, bf16[64,1536]{1,0:T(8,128)(2,1)S(1)}, u32[]{:S(2)}, u32[]{:S(2)}) collective-permute-start(bf16[64,1536]{1,0:T(8,128)(2,1)S(1)} %get-tuple-element.62), channel_id=1, source_target_pairs={{0,1},{1,0},{2,3},{3,2},{4,5},{5,4},{6,7},{7,6},{8,9},{9,8},{10,11... | collective-permute-start | bytes 589832 | tf_op jit(solution)/shard_map/ppermute | solution.py:391
  5.1 12.0 %collective-permute-start.6 = (bf16[64,1536]{1,0:T(8,128)(2,1)S(1)}, bf16[64,1536]{1,0:T(8,128)(2,1)S(1)}, u32[]{:S(2)}, u32[]{:S(2)}) collective-permute-start(bf16[64,1536]{1,0:T(8,128)(2,1)S(1)} %get-tuple-element.63), channel_id=1, source_target_pairs={{0,2},{1,3},{2,0},{3,1},{4,6},{5,7},{6,4},{7,5},{8,10},{9,11},{10,... | collective-permute-start | bytes 589832 | tf_op jit(solution)/shard_map/ppermute | solution.py:391
  6.6 10.4 %collective-permute-start.7 = (bf16[64,1536]{1,0:T(8,128)(2,1)S(1)}, bf16[64,1536]{1,0:T(8,128)(2,1)S(1)}, u32[]{:S(2)}, u32[]{:S(2)}) collective-permute-start(bf16[64,1536]{1,0:T(8,128)(2,1)S(1)} %get-tuple-element.64), channel_id=1, source_target_pairs={{0,3},{1,2},{2,1},{3,0},{4,7},{5,6},{6,5},{7,4},{8,11},{9,10},{10,... | collective-permute-start | bytes 589832 | tf_op jit(solution)/shard_map/ppermute | solution.py:391
  6.7 13.3 %collective-permute-start = (bf16[64,1536]{1,0:T(8,128)(2,1)S(1)}, bf16[64,1536]{1,0:T(8,128)(2,1)S(1)}, u32[]{:S(2)}, u32[]{:S(2)}) collective-permute-start(bf16[64,1536]{1,0:T(8,128)(2,1)S(1)} %get-tuple-element.53), channel_id=1, source_target_pairs={{0,1},{1,0},{2,3},{3,2},{4,5},{5,4},{6,7},{7,6},{8,9},{9,8},{10,11... | collective-permute-start | bytes 589832 | tf_op jit(solution)/shard_map/ppermute | solution.py:391
  8.7 14.5 %collective-permute-start.1 = (bf16[64,1536]{1,0:T(8,128)(2,1)S(1)}, bf16[64,1536]{1,0:T(8,128)(2,1)S(1)}, u32[]{:S(2)}, u32[]{:S(2)}) collective-permute-start(bf16[64,1536]{1,0:T(8,128)(2,1)S(1)} %get-tuple-element.54), channel_id=1, source_target_pairs={{0,2},{1,3},{2,0},{3,1},{4,6},{5,7},{6,4},{7,5},{8,10},{9,11},{10,... | collective-permute-start | bytes 589832 | tf_op jit(solution)/shard_map/ppermute | solution.py:391
  13.2 11.8 %collective-permute-start.2 = (bf16[64,1536]{1,0:T(8,128)(2,1)S(1)}, bf16[64,1536]{1,0:T(8,128)(2,1)S(1)}, u32[]{:S(2)}, u32[]{:S(2)}) collective-permute-start(bf16[64,1536]{1,0:T(8,128)(2,1)S(1)} %get-tuple-element.55), channel_id=1, source_target_pairs={{0,3},{1,2},{2,1},{3,0},{4,7},{5,6},{6,5},{7,4},{8,11},{9,10},{10,... | collective-permute-start | bytes 589832 | tf_op jit(solution)/shard_map/ppermute | solution.py:391
  18.3 10.2 %collective-permute-start.8 = (bf16[48,1536]{1,0:T(8,128)(2,1)S(1)}, bf16[48,1536]{1,0:T(8,128)(2,1)S(1)}, u32[]{:S(2)}, u32[]{:S(2)}) collective-permute-start(bf16[48,1536]{1,0:T(8,128)(2,1)S(1)} %get-tuple-element.65), channel_id=1, source_target_pairs={{0,1},{1,0},{2,3},{3,2},{4,5},{5,4},{6,7},{7,6},{8,9},{9,8},{10,11... | collective-permute-start | bytes 442376 | tf_op jit(solution)/shard_map/ppermute | solution.py:415
  19.4 9.1 %copy-start.2 = (f32[31,1536]{1,0:T(8,128)S(1)}, f32[31,1536]{1,0:T(8,128)}, u32[]{:S(2)}) copy-start(f32[31,1536]{1,0:T(8,128)} %kernel_ref.3) | copy-start | bytes 571396
  19.4 9.1 %copy-start.3 = (s32[2,8]{1,0:T(2,128)S(1)}, s32[2,8]{1,0:T(2,128)}, u32[]{:S(2)}) copy-start(s32[2,8]{1,0:T(2,128)} %lengths_ref.3) | copy-start | bytes 196
  19.4 9.1 %collective-permute-start.9 = (bf16[48,1536]{1,0:T(8,128)(2,1)S(1)}, bf16[48,1536]{1,0:T(8,128)(2,1)S(1)}, u32[]{:S(2)}, u32[]{:S(2)}) collective-permute-start(bf16[48,1536]{1,0:T(8,128)(2,1)S(1)} %get-tuple-element.66), channel_id=1, source_target_pairs={{0,31},{1,2},{2,1},{3,4},{4,3},{5,6},{6,5},{7,8},{8,7},{9,10},{10,... | collective-permute-start | bytes 442376 | tf_op jit(solution)/shard_map/ppermute | solution.py:416
  26.3 14.9 %collective-permute-start.3 = (bf16[48,1536]{1,0:T(8,128)(2,1)S(1)}, bf16[48,1536]{1,0:T(8,128)(2,1)S(1)}, u32[]{:S(2)}, u32[]{:S(2)}) collective-permute-start(bf16[48,1536]{1,0:T(8,128)(2,1)S(1)} %get-tuple-element.56), channel_id=1, source_target_pairs={{0,1},{1,0},{2,3},{3,2},{4,5},{5,4},{6,7},{7,6},{8,9},{9,8},{10,11... | collective-permute-start | bytes 442376 | tf_op jit(solution)/shard_map/ppermute | solution.py:415
  27.8 13.4 %collective-permute-start.4 = (bf16[48,1536]{1,0:T(8,128)(2,1)S(1)}, bf16[48,1536]{1,0:T(8,128)(2,1)S(1)}, u32[]{:S(2)}, u32[]{:S(2)}) collective-permute-start(bf16[48,1536]{1,0:T(8,128)(2,1)S(1)} %get-tuple-element.57), channel_id=1, source_target_pairs={{0,31},{1,2},{2,1},{3,4},{4,3},{5,6},{6,5},{7,8},{8,7},{9,10},{10,... | collective-permute-start | bytes 442376 | tf_op jit(solution)/shard_map/ppermute | solution.py:416
  35.4 13.0 %collective-permute-start.10 = (bf16[64,1536]{1,0:T(8,128)(2,1)S(1)}, bf16[64,1536]{1,0:T(8,128)(2,1)S(1)}, u32[]{:S(2)}, u32[]{:S(2)}) collective-permute-start(bf16[64,1536]{1,0:T(8,128)(2,1)S(1)} %get-tuple-element.75), channel_id=1, source_target_pairs={{0,1},{1,0},{2,3},{3,2},{4,5},{5,4},{6,7},{7,6},{8,9},{9,8},{10,11... | collective-permute-start | bytes 589832 | tf_op jit(solution)/shard_map/ppermute | solution.py:391
  39.7 12.3 %collective-permute-start.11 = (bf16[64,1536]{1,0:T(8,128)(2,1)S(1)}, bf16[64,1536]{1,0:T(8,128)(2,1)S(1)}, u32[]{:S(2)}, u32[]{:S(2)}) collective-permute-start(bf16[64,1536]{1,0:T(8,128)(2,1)S(1)} %get-tuple-element.79), channel_id=1, source_target_pairs={{0,2},{1,3},{2,0},{3,1},{4,6},{5,7},{6,4},{7,5},{8,10},{9,11},{10,... | collective-permute-start | bytes 589832 | tf_op jit(solution)/shard_map/ppermute | solution.py:391
  39.7 12.3 %collective-permute-start.12 = (bf16[64,1536]{1,0:T(8,128)(2,1)S(1)}, bf16[64,1536]{1,0:T(8,128)(2,1)S(1)}, u32[]{:S(2)}, u32[]{:S(2)}) collective-permute-start(bf16[64,1536]{1,0:T(8,128)(2,1)S(1)} %get-tuple-element.80), channel_id=1, source_target_pairs={{0,3},{1,2},{2,1},{3,0},{4,7},{5,6},{6,5},{7,4},{8,11},{9,10},{10,... | collective-permute-start | bytes 589832 | tf_op jit(solution)/shard_map/ppermute | solution.py:391
  48.4 5.7 %collective-permute-start.16 = (f32[32,384]{1,0:T(8,128)S(1)}, f32[32,384]{1,0:T(8,128)S(1)}, u32[]{:S(2)}, u32[]{:S(2)}) collective-permute-start(f32[32,384]{1,0:T(8,128)S(1)} %get-tuple-element.120), channel_id=1, source_target_pairs={{0,1},{1,0},{2,3},{3,2},{4,5},{5,4},{6,7},{7,6},{8,9},{9,8},{10,11... | collective-permute-start | bytes 147464 | tf_op jit(solution)/shard_map/ppermute | solution.py:391
  50.5 5.6 %collective-permute-start.18 = (f32[32,384]{1,0:T(8,128)S(1)}, f32[32,384]{1,0:T(8,128)S(1)}, u32[]{:S(2)}, u32[]{:S(2)}) collective-permute-start(f32[32,384]{1,0:T(8,128)S(1)} %get-tuple-element.121), channel_id=1, source_target_pairs={{0,3},{1,2},{2,1},{3,0},{4,7},{5,6},{6,5},{7,4},{8,11},{9,10},{10,... | collective-permute-start | bytes 147464 | tf_op jit(solution)/shard_map/ppermute | solution.py:391
  50.5 5.6 %collective-permute-start.17 = (f32[32,384]{1,0:T(8,128)S(1)}, f32[32,384]{1,0:T(8,128)S(1)}, u32[]{:S(2)}, u32[]{:S(2)}) collective-permute-start(f32[32,384]{1,0:T(8,128)S(1)} %get-tuple-element.122), channel_id=1, source_target_pairs={{0,2},{1,3},{2,0},{3,1},{4,6},{5,7},{6,4},{7,5},{8,10},{9,11},{10,... | collective-permute-start | bytes 147464 | tf_op jit(solution)/shard_map/ppermute | solution.py:391
  52.0 12.2 %collective-permute-start.13 = (bf16[64,1536]{1,0:T(8,128)(2,1)S(1)}, bf16[64,1536]{1,0:T(8,128)(2,1)S(1)}, u32[]{:S(2)}, u32[]{:S(2)}) collective-permute-start(bf16[64,1536]{1,0:T(8,128)(2,1)S(1)} %get-tuple-element.86), channel_id=1, source_target_pairs={{0,1},{1,0},{2,3},{3,2},{4,5},{5,4},{6,7},{7,6},{8,9},{9,8},{10,11... | collective-permute-start | bytes 589832 | tf_op jit(solution)/shard_map/ppermute | solution.py:391
  54.0 10.3 %collective-permute-start.14 = (bf16[64,1536]{1,0:T(8,128)(2,1)S(1)}, bf16[64,1536]{1,0:T(8,128)(2,1)S(1)}, u32[]{:S(2)}, u32[]{:S(2)}) collective-permute-start(bf16[64,1536]{1,0:T(8,128)(2,1)S(1)} %get-tuple-element.87), channel_id=1, source_target_pairs={{0,2},{1,3},{2,0},{3,1},{4,6},{5,7},{6,4},{7,5},{8,10},{9,11},{10,... | collective-permute-start | bytes 589832 | tf_op jit(solution)/shard_map/ppermute | solution.py:391
  54.1 10.2 %collective-permute-start.15 = (bf16[64,1536]{1,0:T(8,128)(2,1)S(1)}, bf16[64,1536]{1,0:T(8,128)(2,1)S(1)}, u32[]{:S(2)}, u32[]{:S(2)}) collective-permute-start(bf16[64,1536]{1,0:T(8,128)(2,1)S(1)} %get-tuple-element.88), channel_id=1, source_target_pairs={{0,3},{1,2},{2,1},{3,0},{4,7},{5,6},{6,5},{7,4},{8,11},{9,10},{10,... | collective-permute-start | bytes 589832 | tf_op jit(solution)/shard_map/ppermute | solution.py:391
  56.1 1.3 %collective-permute-start.19 = (f32[32,384]{1,0:T(8,128)S(1)}, f32[32,384]{1,0:T(8,128)S(1)}, u32[]{:S(2)}, u32[]{:S(2)}) collective-permute-start(f32[32,384]{1,0:T(8,128)S(1)} %fusion.10), channel_id=1, source_target_pairs={{0,4},{4,0},{8,12},{12,8},{16,20},{20,16},{24,28},{28,24},{1,5},{5... | collective-permute-start | bytes 147464 | tf_op jit(solution)/shard_map/ppermute | solution.py:428
  57.4 4.2 %collective-permute-start.20 = (f32[32,384]{1,0:T(8,128)S(1)}, f32[32,384]{1,0:T(8,128)S(1)}, u32[]{:S(2)}, u32[]{:S(2)}) collective-permute-start(f32[32,384]{1,0:T(8,128)S(1)} %add.96), channel_id=1, source_target_pairs={{0,8},{4,12},{8,0},{12,4},{16,24},{20,28},{24,16},{28,20},{1,9},{5... | collective-permute-start | bytes 147464 | tf_op jit(solution)/shard_map/ppermute | solution.py:428
  61.6 5.1 %collective-permute-start.21 = (f32[32,384]{1,0:T(8,128)S(1)}, f32[32,384]{1,0:T(8,128)S(1)}, u32[]{:S(2)}, u32[]{:S(2)}) collective-permute-start(f32[32,384]{1,0:T(8,128)S(1)} %add.97.refs_0_), channel_id=1, source_target_pairs={{0,16},{4,20},{8,24},{12,28},{16,0},{20,4},{24,8},{28,12},{1,17},{... | collective-permute-start | bytes 147464 | tf_op jit(solution)/shard_map/ppermute | solution.py:428

commit v5 on v4

--- a/solution.py
+++ b/solution.py
@@ -393,13 +393,15 @@
     tables = []
     cells = expert_out
     sizes = (1, 1, 1) + expert_out.shape[3:]
+    def block_of(cells, micro, step):
+        return lax.dynamic_slice(cells, (micro, 0, me ^ step, 0, 0, 0), sizes).reshape(block, width)
+
     for micro in range(micro_count):
-        blocks = [
-            lax.dynamic_slice(cells, (micro, 0, me ^ step, 0, 0, 0), sizes).reshape(block, width)
-            for step in range(groups)
-        ]
+        blocks = [block_of(cells, micro, step) for step in range(1, groups)]
         cells, *blocks = lax.optimization_barrier([cells, *blocks])
-        tables.append([blocks[0]] + [swap(blocks[step], step) for step in range(1, groups)])
+        tables.append([None] + [swap(blocks[step - 1], step) for step in range(1, groups)])
+    for micro in range(micro_count):
+        tables[micro][0] = block_of(cells, micro, 0)
 
     slots = jax.vmap(slot_table)(routes, order[:, 0])
     flat = ((routes // per) ^ me) * block + (routes % per) * CAP + slots

time: 67.5 us -> 67.2 us (level)
  waiting for transfers between devices: 11.2 us -> 10.5 us
    reshape x2 -> x3, local copies, waits for them, and re-layouts: 1.44 us -> 3.37 us  [block_of(): lax.dynamic_slice(cells, (micro, 0, me ^ step, 0, 0, 0), sizes)]
    ppermute x15, waiting for transfers between devices: 8.8 us -> 8.08 us  [swap(): return lax.ppermute(cells, 'expert', [(i, i ^ step) for i in range(groups)])]
    broadcast_in_dim x1, local copies, waits for them, and re-layouts: 0.7 us -> 0.01 us  [local(): gain_row = gain[None, :]]
    unnamed x17 -> x19, local copies, waits for them, and re-layouts: 1.57 us -> 0.9 us
  transfers between devices with their start and end apart: 22 -> 22, of which waited for: 7 -> 8; matrix products, arithmetic and copies ran while one was open for 5% -> 7% of each run, Pallas kernels for 29% -> 29%
where the time goes in v5:
time: 67.2 us; the launch traced here: 67 us
  starting transfers between devices  29.9 us (44%)
  Pallas kernels  20 us (30%)
  waiting for transfers between devices  10.5 us (16%)
  local copies, waits for them, and re-layouts  5.23 us (8%)
  between operations  0.91 us (1%)
    ppermute x15, starting transfers between devices, swap(): return lax.ppermute(cells, 'expert', [(i, i ^ step) for i in range(groups)])  21 us
    pallas_call x2, Pallas kernels, conv(): pl.pallas_call(functools.partial(conv_kernel, group_count, first, micro,...  14.1 us
    ppermute x15, waiting for transfers between devices, swap(): return lax.ppermute(cells, 'expert', [(i, i ^ step) for i in range(groups)])  8.08 us
    ppermute x3, starting transfers between devices, over(): lax.ppermute(cells, 'tm', [(i, i ^ step) for i in range(tm)])  4.5 us
    reshape x3, local copies, waits for them, and re-layouts, block_of(): lax.dynamic_slice(cells, (micro, 0, me ^ step, 0, 0, 0), sizes)  3.37 us
    ppermute x2, starting transfers between devices, local(): near = lax.ppermute(near, both, near_pairs)  3.07 us
    pallas_call x2, Pallas kernels, finish(): pl.pallas_call(functools.partial(finish_kernel, group_count, micro), in_s...  2.9 us
    pallas_call x2, Pallas kernels, combine(): pl.pallas_call(functools.partial(combine_kernel, group_count), grid_spec=...  2.42 us
  transfers between devices with their start and end apart: 22, of which 8 were waited for; matrix products, arithmetic and copies ran while one was open for 7% of the time, Pallas kernels for 29%

profile of v5, /device:TPU:0, one launch (start us, length us, event | category | flops | bytes accessed | tf_op | source)
XLA Modules:
  0.0 67.0 jit_solution(5590965244992601670)
XLA Ops:
  0.7 1.2 %dynamic-slice_bitcast_fusion.5 = (bf16[64,1536]{1,0:T(8,128)(2,1)S(1)}, bf16[64,1536]{1,0:T(8,128)(2,1)S(1)}, bf16[64,1536]{1,0:T(8,128)(2,1)S(1)}) fusion(bf16[2,1,4,8,8,1536]{5,4,3,2,1,0:T(8,128)(2,1)} %param.10, s32[]{:T(128)S(6)} %select_n.35, s32[]{:T(128)S(6)} %select_n.34, s32[]{:T(128)S(6)} %select_n.33), kind=kLoop, calls=%fused_computation.5 | loop fusion | bytes 1179660 | tf_op jit(solution)/shard_map/reshape | solution.py:397
  1.9 3.0 %collective-permute-start.5 = (bf16[64,1536]{1,0:T(8,128)(2,1)S(1)}, bf16[64,1536]{1,0:T(8,128)(2,1)S(1)}, u32[]{:S(2)}, u32[]{:S(2)}) collective-permute-start(bf16[64,1536]{1,0:T(8,128)(2,1)S(1)} %get-tuple-element.60), channel_id=1, source_target_pairs={{0,1},{1,0},{2,3},{3,2},{4,5},{5,4},{6,7},{7,6},{8,9},{9,8},{10,11... | collective-permute-start | bytes 589832 | tf_op jit(solution)/shard_map/ppermute | solution.py:391
  4.9 1.5 %collective-permute-start.6 = (bf16[64,1536]{1,0:T(8,128)(2,1)S(1)}, bf16[64,1536]{1,0:T(8,128)(2,1)S(1)}, u32[]{:S(2)}, u32[]{:S(2)}) collective-permute-start(bf16[64,1536]{1,0:T(8,128)(2,1)S(1)} %get-tuple-element.61), channel_id=1, source_target_pairs={{0,2},{1,3},{2,0},{3,1},{4,6},{5,7},{6,4},{7,5},{8,10},{9,11},{10,... | collective-permute-start | bytes 589832 | tf_op jit(solution)/shard_map/ppermute | solution.py:391
  6.4 1.2 %dynamic-slice_bitcast_fusion.2 = (bf16[64,1536]{1,0:T(8,128)(2,1)S(1)}, bf16[64,1536]{1,0:T(8,128)(2,1)S(1)}, bf16[64,1536]{1,0:T(8,128)(2,1)S(1)}) fusion(bf16[2,1,4,8,8,1536]{5,4,3,2,1,0:T(8,128)(2,1)} %param.10, s32[]{:T(128)S(6)} %select_n.35, s32[]{:T(128)S(6)} %select_n.34, s32[]{:T(128)S(6)} %select_n.33), kind=kLoop, calls=%fused_computation.2 | loop fusion | bytes 1179660 | tf_op jit(solution)/shard_map/reshape | solution.py:397
  7.6 2.0 %collective-permute-start = (bf16[64,1536]{1,0:T(8,128)(2,1)S(1)}, bf16[64,1536]{1,0:T(8,128)(2,1)S(1)}, u32[]{:S(2)}, u32[]{:S(2)}) collective-permute-start(bf16[64,1536]{1,0:T(8,128)(2,1)S(1)} %get-tuple-element.52), channel_id=1, source_target_pairs={{0,1},{1,0},{2,3},{3,2},{4,5},{5,4},{6,7},{7,6},{8,9},{9,8},{10,11... | collective-permute-start | bytes 589832 | tf_op jit(solution)/shard_map/ppermute | solution.py:391
  9.6 1.5 %collective-permute-start.1 = (bf16[64,1536]{1,0:T(8,128)(2,1)S(1)}, bf16[64,1536]{1,0:T(8,128)(2,1)S(1)}, u32[]{:S(2)}, u32[]{:S(2)}) collective-permute-start(bf16[64,1536]{1,0:T(8,128)(2,1)S(1)} %get-tuple-element.53), channel_id=1, source_target_pairs={{0,2},{1,3},{2,0},{3,1},{4,6},{5,7},{6,4},{7,5},{8,10},{9,11},{10,... | collective-permute-start | bytes 589832 | tf_op jit(solution)/shard_map/ppermute | solution.py:391
  12.8 1.1 %dynamic-slice_bitcast_fusion = (bf16[64,1536]{1,0:T(8,128)(2,1)S(1)}, bf16[64,1536]{1,0:T(8,128)(2,1)S(1)}) fusion(bf16[2,1,4,8,8,1536]{5,4,3,2,1,0:T(8,128)(2,1)} %param.10, s32[]{:T(128)S(6)} %select_n.36), kind=kLoop, calls=%fused_computation | loop fusion | bytes 786436 | tf_op jit(solution)/shard_map/reshape | solution.py:397
  13.9 2.2 %collective-permute-done.6.rest_2_ = bf16[64,1536]{1,0:T(8,128)(2,1)S(1)} collective-permute-done((bf16[64,1536]{1,0:T(8,128)(2,1)S(1)}, bf16[64,1536]{1,0:T(8,128)(2,1)S(1)}, u32[]{:S(2)}, u32[]{:S(2)}) %collective-permute-start.6) | collective-permute-done | bytes 196640 | tf_op jit(solution)/shard_map/ppermute | solution.py:391
  16.4 1.2 %combine.3 = (bf16[48,1536]{1,0:T(8,128)(2,1)S(1)}, bf16[48,1536]{1,0:T(8,128)(2,1)S(1)}, f32[64,1536]{1,0:T(8,128)S(1)}, f32[64,128]{1,0:T(8,128)S(1)}, bf16[2,64,1536]{2,1,0:T(8,128)(2,1)S(1)}) custom-call(s32[3]{0:T(128)S(1)} %pad_add_fusion.place_ref, bf16[64,1536]{1,0:T(8,128)(2,1)S(1)} %get-tuple-element.110.rest_0_, ...), custom_call_target="tpu_custom_call" | custom-call | flops 3000000000 | tf_op jit(solution)/shard_map/combine/pallas_call | solution.py:216
  17.6 1.6 %collective-permute-start.8 = (bf16[48,1536]{1,0:T(8,128)(2,1)S(1)}, bf16[48,1536]{1,0:T(8,128)(2,1)S(1)}, u32[]{:S(2)}, u32[]{:S(2)}) collective-permute-start(bf16[48,1536]{1,0:T(8,128)(2,1)S(1)} %get-tuple-element.63), channel_id=1, source_target_pairs={{0,1},{1,0},{2,3},{3,2},{4,5},{5,4},{6,7},{7,6},{8,9},{9,8},{10,11... | collective-permute-start | bytes 442376 | tf_op jit(solution)/shard_map/ppermute | solution.py:417
  19.2 0.7 collective-permute-start.9
  19.8 3.1 %collective-permute-done.1.rest_2_ = bf16[64,1536]{1,0:T(8,128)(2,1)S(1)} collective-permute-done((bf16[64,1536]{1,0:T(8,128)(2,1)S(1)}, bf16[64,1536]{1,0:T(8,128)(2,1)S(1)}, u32[]{:S(2)}, u32[]{:S(2)}) %collective-permute-start.1) | collective-permute-done | bytes 196640 | tf_op jit(solution)/shard_map/ppermute | solution.py:391
  23.0 1.9 %collective-permute-done.2.rest_3_ = bf16[64,1536]{1,0:T(8,128)(2,1)S(1)} collective-permute-done((bf16[64,1536]{1,0:T(8,128)(2,1)S(1)}, bf16[64,1536]{1,0:T(8,128)(2,1)S(1)}, u32[]{:S(2)}, u32[]{:S(2)}) %collective-permute-start.2) | collective-permute-done | bytes 196640 | tf_op jit(solution)/shard_map/ppermute | solution.py:391
  24.9 1.2 %combine.2 = (bf16[48,1536]{1,0:T(8,128)(2,1)S(1)}, bf16[48,1536]{1,0:T(8,128)(2,1)S(1)}, f32[64,1536]{1,0:T(8,128)S(1)}, f32[64,128]{1,0:T(8,128)S(1)}, bf16[2,64,1536]{2,1,0:T(8,128)(2,1)S(1)}) custom-call(s32[3]{0:T(128)S(1)} %pad_add_fusion.place_ref, bf16[64,1536]{1,0:T(8,128)(2,1)S(1)} %get-tuple-element.111.rest_0_, ...), custom_call_target="tpu_custom_call" | custom-call | flops 3000000000 | tf_op jit(solution)/shard_map/combine/pallas_call | solution.py:216
  26.1 1.5 %collective-permute-start.3 = (bf16[48,1536]{1,0:T(8,128)(2,1)S(1)}, bf16[48,1536]{1,0:T(8,128)(2,1)S(1)}, u32[]{:S(2)}, u32[]{:S(2)}) collective-permute-start(bf16[48,1536]{1,0:T(8,128)(2,1)S(1)} %get-tuple-element.55), channel_id=1, source_target_pairs={{0,1},{1,0},{2,3},{3,2},{4,5},{5,4},{6,7},{7,6},{8,9},{9,8},{10,11... | collective-permute-start | bytes 442376 | tf_op jit(solution)/shard_map/ppermute | solution.py:417
  27.6 0.7 %collective-permute-start.4 = (bf16[48,1536]{1,0:T(8,128)(2,1)S(1)}, bf16[48,1536]{1,0:T(8,128)(2,1)S(1)}, u32[]{:S(2)}, u32[]{:S(2)}) collective-permute-start(bf16[48,1536]{1,0:T(8,128)(2,1)S(1)} %get-tuple-element.56), channel_id=1, source_target_pairs={{0,31},{1,2},{2,1},{3,4},{4,3},{5,6},{6,5},{7,8},{8,7},{9,10},{10,... | collective-permute-start | bytes 442376 | tf_op jit(solution)/shard_map/ppermute | solution.py:418
  28.3 6.9 %conv.2 = (bf16[2,64,1536]{2,1,0:T(8,128)(2,1)}, f32[2,64,2]{2,1,0:T(8,128)S(1)}, f32[4,32,384]{2,1,0:T(8,128)S(1)}, bf16[64,1536]{1,0:T(8,128)(2,1)S(1)}, bf16[...) custom-call(s32[3]{0:T(128)S(1)} %pad_add_fusion.place_ref, ...), custom_call_target="tpu_custom_call" | custom-call | flops 8000000000 | tf_op jit(solution)/shard_map/conv/pallas_call | solution.py:276
  35.2 4.3 %collective-permute-start.10 = (bf16[64,1536]{1,0:T(8,128)(2,1)S(1)}, bf16[64,1536]{1,0:T(8,128)(2,1)S(1)}, u32[]{:S(2)}, u32[]{:S(2)}) collective-permute-start(bf16[64,1536]{1,0:T(8,128)(2,1)S(1)} %get-tuple-element.73), channel_id=1, source_target_pairs={{0,1},{1,0},{2,3},{3,2},{4,5},{5,4},{6,7},{7,6},{8,9},{9,8},{10,11... | collective-permute-start | bytes 589832 | tf_op jit(solution)/shard_map/ppermute | solution.py:391
  39.5 1.5 %collective-permute-start.12 = (bf16[64,1536]{1,0:T(8,128)(2,1)S(1)}, bf16[64,1536]{1,0:T(8,128)(2,1)S(1)}, u32[]{:S(2)}, u32[]{:S(2)}) collective-permute-start(bf16[64,1536]{1,0:T(8,128)(2,1)S(1)} %get-tuple-element.78), channel_id=1, source_target_pairs={{0,3},{1,2},{2,1},{3,0},{4,7},{5,6},{6,5},{7,4},{8,11},{9,10},{10,... | collective-permute-start | bytes 589832 | tf_op jit(solution)/shard_map/ppermute | solution.py:391
  41.0 7.2 %conv.3 = (bf16[2,64,1536]{2,1,0:T(8,128)(2,1)}, f32[2,64,2]{2,1,0:T(8,128)S(1)}, f32[4,32,384]{2,1,0:T(8,128)S(1)}, bf16[64,1536]{1,0:T(8,128)(2,1)S(1)}, bf16[...) custom-call(s32[3]{0:T(128)S(1)} %pad_add_fusion.place_ref, ...), custom_call_target="tpu_custom_call", output_to_operand_aliasing={{0}: (13, {}), {1}: (14, {})} | custom-call | flops 8000000000 | tf_op jit(solution)/shard_map/conv/pallas_call | solution.py:276
  48.2 2.1 %collective-permute-start.16 = (f32[32,384]{1,0:T(8,128)S(1)}, f32[32,384]{1,0:T(8,128)S(1)}, u32[]{:S(2)}, u32[]{:S(2)}) collective-permute-start(f32[32,384]{1,0:T(8,128)S(1)} %get-tuple-element.118), channel_id=1, source_target_pairs={{0,1},{1,0},{2,3},{3,2},{4,5},{5,4},{6,7},{7,6},{8,9},{9,8},{10,11... | collective-permute-start | bytes 147464 | tf_op jit(solution)/shard_map/ppermute | solution.py:391
  50.3 1.5 %collective-permute-start.17 = (f32[32,384]{1,0:T(8,128)S(1)}, f32[32,384]{1,0:T(8,128)S(1)}, u32[]{:S(2)}, u32[]{:S(2)}) collective-permute-start(f32[32,384]{1,0:T(8,128)S(1)} %get-tuple-element.120), channel_id=1, source_target_pairs={{0,2},{1,3},{2,0},{3,1},{4,6},{5,7},{6,4},{7,5},{8,10},{9,11},{10,... | collective-permute-start | bytes 147464 | tf_op jit(solution)/shard_map/ppermute | solution.py:391
  51.8 1.9 %collective-permute-start.13 = (bf16[64,1536]{1,0:T(8,128)(2,1)S(1)}, bf16[64,1536]{1,0:T(8,128)(2,1)S(1)}, u32[]{:S(2)}, u32[]{:S(2)}) collective-permute-start(bf16[64,1536]{1,0:T(8,128)(2,1)S(1)} %get-tuple-element.84), channel_id=1, source_target_pairs={{0,1},{1,0},{2,3},{3,2},{4,5},{5,4},{6,7},{7,6},{8,9},{9,8},{10,11... | collective-permute-start | bytes 589832 | tf_op jit(solution)/shard_map/ppermute | solution.py:391
  53.8 1.5 %collective-permute-start.15 = (bf16[64,1536]{1,0:T(8,128)(2,1)S(1)}, bf16[64,1536]{1,0:T(8,128)(2,1)S(1)}, u32[]{:S(2)}, u32[]{:S(2)}) collective-permute-start(bf16[64,1536]{1,0:T(8,128)(2,1)S(1)} %get-tuple-element.86), channel_id=1, source_target_pairs={{0,3},{1,2},{2,1},{3,0},{4,7},{5,6},{6,5},{7,4},{8,11},{9,10},{10,... | collective-permute-start | bytes 589832 | tf_op jit(solution)/shard_map/ppermute | solution.py:391
  56.0 0.7 copy.60
  57.2 1.7 %collective-permute-start.20 = (f32[32,384]{1,0:T(8,128)S(1)}, f32[32,384]{1,0:T(8,128)S(1)}, u32[]{:S(2)}, u32[]{:S(2)}) collective-permute-start(f32[32,384]{1,0:T(8,128)S(1)} %add.96), channel_id=1, source_target_pairs={{0,8},{4,12},{8,0},{12,4},{16,24},{20,28},{24,16},{28,20},{1,9},{5... | collective-permute-start | bytes 147464 | tf_op jit(solution)/shard_map/ppermute | solution.py:430
  58.9 1.4 %finish.2.refs_4_ = bf16[2,4,64,1536]{3,2,1,0:T(8,128)(2,1)} custom-call(s32[3]{0:T(128)S(1)} %pad_add_fusion.place_ref, bf16[64,1536]{1,0:T(8,128)(2,1)S(1)} %get-tuple-element.87.refs_0_, bf16[64,1536]{1,0:T(8,128)(2,1)S(1)} %collective-permute-done.10.refs_1_, bf16[64,1536]{1,0:T(8,128)(2,1)S(1)} %collective-permute-done.11.refs_2_, ...), custom_call_target="tpu_custom_call" | custom-call | flops 1500000000 | tf_op jit(solution)/shard_map/finish/pallas_call | solution.py:334
  60.3 1.0 %collective-permute-done.20 = f32[32,384]{1,0:T(8,128)S(1)} collective-permute-done((f32[32,384]{1,0:T(8,128)S(1)}, f32[32,384]{1,0:T(8,128)S(1)}, u32[]{:S(2)}, u32[]{:S(2)}) %collective-permute-start.20) | collective-permute-done | bytes 49184 | tf_op jit(solution)/shard_map/ppermute | solution.py:430
  61.3 2.7 %collective-permute-start.21 = (f32[32,384]{1,0:T(8,128)S(1)}, f32[32,384]{1,0:T(8,128)S(1)}, u32[]{:S(2)}, u32[]{:S(2)}) collective-permute-start(f32[32,384]{1,0:T(8,128)S(1)} %add.97.refs_0_), channel_id=1, source_target_pairs={{0,16},{4,20},{8,24},{12,28},{16,0},{20,4},{24,8},{28,12},{1,17},{... | collective-permute-start | bytes 147464 | tf_op jit(solution)/shard_map/ppermute | solution.py:430
  64.1 1.5 %finish.3 = bf16[2,4,64,1536]{3,2,1,0:T(8,128)(2,1)} custom-call(s32[3]{0:T(128)S(1)} %pad_add_fusion.place_ref, bf16[64,1536]{1,0:T(8,128)(2,1)S(1)} %get-tuple-element.83.refs_0_, bf16[64,1536]{1,0:T(8,128)(2,1)S(1)} %collective-permute-done.13.refs_1_, bf16[64,1536]{1,0:T(8,128)(2,1)S(1)} %collective-permute-done.14.refs_2_, ...), custom_call_target="tpu_custom_call", output_to_operand_aliasing={{}: (5, {})} | custom-call | flops 1500000000 | tf_op jit(solution)/shard_map/finish/pallas_call | solution.py:334
  65.5 0.9 %collective-permute-done.21.refs_1_ = f32[32,384]{1,0:T(8,128)S(1)} collective-permute-done((f32[32,384]{1,0:T(8,128)S(1)}, f32[32,384]{1,0:T(8,128)S(1)}, u32[]{:S(2)}, u32[]{:S(2)}) %collective-permute-start.21) | collective-permute-done | bytes 49184 | tf_op jit(solution)/shard_map/ppermute | solution.py:430
  66.4 0.6 total.1
  (61 shorter events, 3.3 us)
Async XLA Ops:
  0.6 10.5 %copy-start.5 = (s32[2,64,2]{1,2,0:T(2,128)S(1)}, s32[2,64,2]{1,2,0:T(2,128)}, u32[]{:S(2)}) copy-start(s32[2,64,2]{1,2,0:T(2,128)} %param.11) | copy-start | bytes 3076
  0.6 10.6 %copy-start.7 = (s32[2,1,64]{2,1,0:T(1,128)S(1)}, s32[2,1,64]{2,1,0:T(1,128)}, u32[]{:S(2)}) copy-start(s32[2,1,64]{2,1,0:T(1,128)} %param.12) | copy-start | bytes 1540
  0.7 10.6 %copy-start.4 = (f32[1536]{0:T(1024)S(1)}, f32[1536]{0:T(1024)}, u32[]{:S(2)}) copy-start(f32[1536]{0:T(1024)} %param.15) | copy-start | bytes 18436
  0.7 11.1 %copy-start.6 = (f32[2,64,2]{1,2,0:T(2,128)S(1)}, f32[2,64,2]{1,2,0:T(2,128)}, u32[]{:S(2)}) copy-start(f32[2,64,2]{1,2,0:T(2,128)} %param.13) | copy-start | bytes 3076
  1.9 14.5 %copy-start = (bf16[2,64,1536]{2,1,0:T(8,128)(2,1)S(1)}, bf16[2,64,1536]{2,1,0:T(8,128)(2,1)}, u32[]{:S(2)}) copy-start(bf16[2,64,1536]{2,1,0:T(8,128)(2,1)} %rest_4_.3) | copy-start | bytes 1179652
  1.9 14.5 %copy-start.1 = (bf16[2,64,1536]{2,1,0:T(8,128)(2,1)S(1)}, bf16[2,64,1536]{2,1,0:T(8,128)(2,1)}, u32[]{:S(2)}) copy-start(bf16[2,64,1536]{2,1,0:T(8,128)(2,1)} %grad_out_ref.3) | copy-start | bytes 1179652
  1.9 11.9 %collective-permute-start.5 = (bf16[64,1536]{1,0:T(8,128)(2,1)S(1)}, bf16[64,1536]{1,0:T(8,128)(2,1)S(1)}, u32[]{:S(2)}, u32[]{:S(2)}) collective-permute-start(bf16[64,1536]{1,0:T(8,128)(2,1)S(1)} %get-tuple-element.60), channel_id=1, source_target_pairs={{0,1},{1,0},{2,3},{3,2},{4,5},{5,4},{6,7},{7,6},{8,9},{9,8},{10,11... | collective-permute-start | bytes 589832 | tf_op jit(solution)/shard_map/ppermute | solution.py:391
  4.9 11.2 %collective-permute-start.6 = (bf16[64,1536]{1,0:T(8,128)(2,1)S(1)}, bf16[64,1536]{1,0:T(8,128)(2,1)S(1)}, u32[]{:S(2)}, u32[]{:S(2)}) collective-permute-start(bf16[64,1536]{1,0:T(8,128)(2,1)S(1)} %get-tuple-element.61), channel_id=1, source_target_pairs={{0,2},{1,3},{2,0},{3,1},{4,6},{5,7},{6,4},{7,5},{8,10},{9,11},{10,... | collective-permute-start | bytes 589832 | tf_op jit(solution)/shard_map/ppermute | solution.py:391
  6.4 10.0 %collective-permute-start.7 = (bf16[64,1536]{1,0:T(8,128)(2,1)S(1)}, bf16[64,1536]{1,0:T(8,128)(2,1)S(1)}, u32[]{:S(2)}, u32[]{:S(2)}) collective-permute-start(bf16[64,1536]{1,0:T(8,128)(2,1)S(1)} %get-tuple-element.62), channel_id=1, source_target_pairs={{0,3},{1,2},{2,1},{3,0},{4,7},{5,6},{6,5},{7,4},{8,11},{9,10},{10,... | collective-permute-start | bytes 589832 | tf_op jit(solution)/shard_map/ppermute | solution.py:391
  7.6 12.3 %collective-permute-start = (bf16[64,1536]{1,0:T(8,128)(2,1)S(1)}, bf16[64,1536]{1,0:T(8,128)(2,1)S(1)}, u32[]{:S(2)}, u32[]{:S(2)}) collective-permute-start(bf16[64,1536]{1,0:T(8,128)(2,1)S(1)} %get-tuple-element.52), channel_id=1, source_target_pairs={{0,1},{1,0},{2,3},{3,2},{4,5},{5,4},{6,7},{7,6},{8,9},{9,8},{10,11... | collective-permute-start | bytes 589832 | tf_op jit(solution)/shard_map/ppermute | solution.py:391
  9.6 13.4 %collective-permute-start.1 = (bf16[64,1536]{1,0:T(8,128)(2,1)S(1)}, bf16[64,1536]{1,0:T(8,128)(2,1)S(1)}, u32[]{:S(2)}, u32[]{:S(2)}) collective-permute-start(bf16[64,1536]{1,0:T(8,128)(2,1)S(1)} %get-tuple-element.53), channel_id=1, source_target_pairs={{0,2},{1,3},{2,0},{3,1},{4,6},{5,7},{6,4},{7,5},{8,10},{9,11},{10,... | collective-permute-start | bytes 589832 | tf_op jit(solution)/shard_map/ppermute | solution.py:391
  13.8 11.0 %collective-permute-start.2 = (bf16[64,1536]{1,0:T(8,128)(2,1)S(1)}, bf16[64,1536]{1,0:T(8,128)(2,1)S(1)}, u32[]{:S(2)}, u32[]{:S(2)}) collective-permute-start(bf16[64,1536]{1,0:T(8,128)(2,1)S(1)} %get-tuple-element.54), channel_id=1, source_target_pairs={{0,3},{1,2},{2,1},{3,0},{4,7},{5,6},{6,5},{7,4},{8,11},{9,10},{10,... | collective-permute-start | bytes 589832 | tf_op jit(solution)/shard_map/ppermute | solution.py:391
  17.6 10.7 %collective-permute-start.8 = (bf16[48,1536]{1,0:T(8,128)(2,1)S(1)}, bf16[48,1536]{1,0:T(8,128)(2,1)S(1)}, u32[]{:S(2)}, u32[]{:S(2)}) collective-permute-start(bf16[48,1536]{1,0:T(8,128)(2,1)S(1)} %get-tuple-element.63), channel_id=1, source_target_pairs={{0,1},{1,0},{2,3},{3,2},{4,5},{5,4},{6,7},{7,6},{8,9},{9,8},{10,11... | collective-permute-start | bytes 442376 | tf_op jit(solution)/shard_map/ppermute | solution.py:417
  19.2 9.1 %collective-permute-start.9 = (bf16[48,1536]{1,0:T(8,128)(2,1)S(1)}, bf16[48,1536]{1,0:T(8,128)(2,1)S(1)}, u32[]{:S(2)}, u32[]{:S(2)}) collective-permute-start(bf16[48,1536]{1,0:T(8,128)(2,1)S(1)} %get-tuple-element.64), channel_id=1, source_target_pairs={{0,31},{1,2},{2,1},{3,4},{4,3},{5,6},{6,5},{7,8},{8,7},{9,10},{10,... | collective-permute-start | bytes 442376 | tf_op jit(solution)/shard_map/ppermute | solution.py:418
  24.9 3.4 %copy-start.2 = (f32[31,1536]{1,0:T(8,128)S(1)}, f32[31,1536]{1,0:T(8,128)}, u32[]{:S(2)}) copy-start(f32[31,1536]{1,0:T(8,128)} %kernel_ref.3) | copy-start | bytes 571396
  24.9 3.4 %copy-start.3 = (s32[2,8]{1,0:T(2,128)S(1)}, s32[2,8]{1,0:T(2,128)}, u32[]{:S(2)}) copy-start(s32[2,8]{1,0:T(2,128)} %lengths_ref.3) | copy-start | bytes 196
  26.1 14.9 %collective-permute-start.3 = (bf16[48,1536]{1,0:T(8,128)(2,1)S(1)}, bf16[48,1536]{1,0:T(8,128)(2,1)S(1)}, u32[]{:S(2)}, u32[]{:S(2)}) collective-permute-start(bf16[48,1536]{1,0:T(8,128)(2,1)S(1)} %get-tuple-element.55), channel_id=1, source_target_pairs={{0,1},{1,0},{2,3},{3,2},{4,5},{5,4},{6,7},{7,6},{8,9},{9,8},{10,11... | collective-permute-start | bytes 442376 | tf_op jit(solution)/shard_map/ppermute | solution.py:417
  27.6 13.4 %collective-permute-start.4 = (bf16[48,1536]{1,0:T(8,128)(2,1)S(1)}, bf16[48,1536]{1,0:T(8,128)(2,1)S(1)}, u32[]{:S(2)}, u32[]{:S(2)}) collective-permute-start(bf16[48,1536]{1,0:T(8,128)(2,1)S(1)} %get-tuple-element.56), channel_id=1, source_target_pairs={{0,31},{1,2},{2,1},{3,4},{4,3},{5,6},{6,5},{7,8},{8,7},{9,10},{10,... | collective-permute-start | bytes 442376 | tf_op jit(solution)/shard_map/ppermute | solution.py:418
  35.2 13.0 %collective-permute-start.10 = (bf16[64,1536]{1,0:T(8,128)(2,1)S(1)}, bf16[64,1536]{1,0:T(8,128)(2,1)S(1)}, u32[]{:S(2)}, u32[]{:S(2)}) collective-permute-start(bf16[64,1536]{1,0:T(8,128)(2,1)S(1)} %get-tuple-element.73), channel_id=1, source_target_pairs={{0,1},{1,0},{2,3},{3,2},{4,5},{5,4},{6,7},{7,6},{8,9},{9,8},{10,11... | collective-permute-start | bytes 589832 | tf_op jit(solution)/shard_map/ppermute | solution.py:391
  39.5 12.3 %collective-permute-start.11 = (bf16[64,1536]{1,0:T(8,128)(2,1)S(1)}, bf16[64,1536]{1,0:T(8,128)(2,1)S(1)}, u32[]{:S(2)}, u32[]{:S(2)}) collective-permute-start(bf16[64,1536]{1,0:T(8,128)(2,1)S(1)} %get-tuple-element.77), channel_id=1, source_target_pairs={{0,2},{1,3},{2,0},{3,1},{4,6},{5,7},{6,4},{7,5},{8,10},{9,11},{10,... | collective-permute-start | bytes 589832 | tf_op jit(solution)/shard_map/ppermute | solution.py:391
  39.5 12.3 %collective-permute-start.12 = (bf16[64,1536]{1,0:T(8,128)(2,1)S(1)}, bf16[64,1536]{1,0:T(8,128)(2,1)S(1)}, u32[]{:S(2)}, u32[]{:S(2)}) collective-permute-start(bf16[64,1536]{1,0:T(8,128)(2,1)S(1)} %get-tuple-element.78), channel_id=1, source_target_pairs={{0,3},{1,2},{2,1},{3,0},{4,7},{5,6},{6,5},{7,4},{8,11},{9,10},{10,... | collective-permute-start | bytes 589832 | tf_op jit(solution)/shard_map/ppermute | solution.py:391
  48.2 5.6 %collective-permute-start.16 = (f32[32,384]{1,0:T(8,128)S(1)}, f32[32,384]{1,0:T(8,128)S(1)}, u32[]{:S(2)}, u32[]{:S(2)}) collective-permute-start(f32[32,384]{1,0:T(8,128)S(1)} %get-tuple-element.118), channel_id=1, source_target_pairs={{0,1},{1,0},{2,3},{3,2},{4,5},{5,4},{6,7},{7,6},{8,9},{9,8},{10,11... | collective-permute-start | bytes 147464 | tf_op jit(solution)/shard_map/ppermute | solution.py:391
  50.3 5.6 %collective-permute-start.18 = (f32[32,384]{1,0:T(8,128)S(1)}, f32[32,384]{1,0:T(8,128)S(1)}, u32[]{:S(2)}, u32[]{:S(2)}) collective-permute-start(f32[32,384]{1,0:T(8,128)S(1)} %get-tuple-element.119), channel_id=1, source_target_pairs={{0,3},{1,2},{2,1},{3,0},{4,7},{5,6},{6,5},{7,4},{8,11},{9,10},{10,... | collective-permute-start | bytes 147464 | tf_op jit(solution)/shard_map/ppermute | solution.py:391
  50.3 5.6 %collective-permute-start.17 = (f32[32,384]{1,0:T(8,128)S(1)}, f32[32,384]{1,0:T(8,128)S(1)}, u32[]{:S(2)}, u32[]{:S(2)}) collective-permute-start(f32[32,384]{1,0:T(8,128)S(1)} %get-tuple-element.120), channel_id=1, source_target_pairs={{0,2},{1,3},{2,0},{3,1},{4,6},{5,7},{6,4},{7,5},{8,10},{9,11},{10,... | collective-permute-start | bytes 147464 | tf_op jit(solution)/shard_map/ppermute | solution.py:391
  51.8 12.2 %collective-permute-start.13 = (bf16[64,1536]{1,0:T(8,128)(2,1)S(1)}, bf16[64,1536]{1,0:T(8,128)(2,1)S(1)}, u32[]{:S(2)}, u32[]{:S(2)}) collective-permute-start(bf16[64,1536]{1,0:T(8,128)(2,1)S(1)} %get-tuple-element.84), channel_id=1, source_target_pairs={{0,1},{1,0},{2,3},{3,2},{4,5},{5,4},{6,7},{7,6},{8,9},{9,8},{10,11... | collective-permute-start | bytes 589832 | tf_op jit(solution)/shard_map/ppermute | solution.py:391
  53.8 10.3 %collective-permute-start.14 = (bf16[64,1536]{1,0:T(8,128)(2,1)S(1)}, bf16[64,1536]{1,0:T(8,128)(2,1)S(1)}, u32[]{:S(2)}, u32[]{:S(2)}) collective-permute-start(bf16[64,1536]{1,0:T(8,128)(2,1)S(1)} %get-tuple-element.85), channel_id=1, source_target_pairs={{0,2},{1,3},{2,0},{3,1},{4,6},{5,7},{6,4},{7,5},{8,10},{9,11},{10,... | collective-permute-start | bytes 589832 | tf_op jit(solution)/shard_map/ppermute | solution.py:391
  53.8 10.2 %collective-permute-start.15 = (bf16[64,1536]{1,0:T(8,128)(2,1)S(1)}, bf16[64,1536]{1,0:T(8,128)(2,1)S(1)}, u32[]{:S(2)}, u32[]{:S(2)}) collective-permute-start(bf16[64,1536]{1,0:T(8,128)(2,1)S(1)} %get-tuple-element.86), channel_id=1, source_target_pairs={{0,3},{1,2},{2,1},{3,0},{4,7},{5,6},{6,5},{7,4},{8,11},{9,10},{10,... | collective-permute-start | bytes 589832 | tf_op jit(solution)/shard_map/ppermute | solution.py:391
  55.9 1.3 %collective-permute-start.19 = (f32[32,384]{1,0:T(8,128)S(1)}, f32[32,384]{1,0:T(8,128)S(1)}, u32[]{:S(2)}, u32[]{:S(2)}) collective-permute-start(f32[32,384]{1,0:T(8,128)S(1)} %fusion.10), channel_id=1, source_target_pairs={{0,4},{4,0},{8,12},{12,8},{16,20},{20,16},{24,28},{28,24},{1,5},{5... | collective-permute-start | bytes 147464 | tf_op jit(solution)/shard_map/ppermute | solution.py:430
  57.2 4.2 %collective-permute-start.20 = (f32[32,384]{1,0:T(8,128)S(1)}, f32[32,384]{1,0:T(8,128)S(1)}, u32[]{:S(2)}, u32[]{:S(2)}) collective-permute-start(f32[32,384]{1,0:T(8,128)S(1)} %add.96), channel_id=1, source_target_pairs={{0,8},{4,12},{8,0},{12,4},{16,24},{20,28},{24,16},{28,20},{1,9},{5... | collective-permute-start | bytes 147464 | tf_op jit(solution)/shard_map/ppermute | solution.py:430
  61.3 5.1 %collective-permute-start.21 = (f32[32,384]{1,0:T(8,128)S(1)}, f32[32,384]{1,0:T(8,128)S(1)}, u32[]{:S(2)}, u32[]{:S(2)}) collective-permute-start(f32[32,384]{1,0:T(8,128)S(1)} %add.97.refs_0_), channel_id=1, source_target_pairs={{0,16},{4,20},{8,24},{12,28},{16,0},{20,4},{24,8},{28,12},{1,17},{... | collective-permute-start | bytes 147464 | tf_op jit(solution)/shard_map/ppermute | solution.py:430
